TPU v7x, 32 devices: a whole 2x2x4 slice. The times are simulated.
32 devices in a mesh: batch: 4 (over x, core), seq: 8 (over z, y).
Axes of the slice: x: 2, y: 2, z: 4, core: 2. Of those that a mesh axis runs over, the one named last changes fastest.
Arguments:
- activations: bfloat16 [8, 1024, 768], P('batch', 'seq'), may hold values from -6 to 6
- cotangent: bfloat16 [8, 1024, 768], P('batch', 'seq'), may hold values from -6 to 6
- w_in: float32 [1, 768, 3072], P(None, ('batch', 'seq')), may hold values from -0.21875 to 0.21875
- w_out: float32 [1, 3072, 768], P(None, None, ('batch', 'seq')), may hold values from -0.109375 to 0.109375
- b_in: float32 [1, 3072], P(None, ('batch', 'seq')), may hold values from -3 to 3
- vec_params: float32 [1, 5, 768], P(None, None, ('batch', 'seq')), may hold values from -0.9 to 4.5, as said below
- first_w_in: float32 [1, 768, 3072], P(None, ('batch', 'seq')), may hold values from -0.0068359375 to 0.0068359375
- second_w_in: float32 [1, 768, 3072], P(None, ('batch', 'seq')), may hold values from 1.0580882e-07 to 1.6929412e-06
- first_w_out: float32 [1, 3072, 768], P(None, None, ('batch', 'seq')), may hold values from -0.0068359375 to 0.0068359375
- second_w_out: float32 [1, 3072, 768], P(None, None, ('batch', 'seq')), may hold values from 1.0580882e-07 to 1.6929412e-06
- first_b_in: float32 [1, 3072], P(None, ('batch', 'seq')), may hold values from -0.0068359375 to 0.0068359375
- second_b_in: float32 [1, 3072], P(None, ('batch', 'seq')), may hold values from 1.0580882e-07 to 1.6929412e-06
- first_vec: float32 [1, 5, 768], P(None, None, ('batch', 'seq')), may hold values from -0.0068359375 to 0.0068359375
- second_vec: float32 [1, 5, 768], P(None, None, ('batch', 'seq')), may hold values from 1.0580882e-07 to 1.6929412e-06
Outputs:
- block_output: bfloat16 [8, 1024, 768], P('batch', 'seq')
- input_grad: float32 [8, 1024, 768], P('batch', 'seq')
- grad_norm: float32 [], replicated
- new_first_w_in: float32 [1, 768, 3072], P(None, ('batch', 'seq'))
- new_second_w_in: float32 [1, 768, 3072], P(None, ('batch', 'seq'))
- new_w_in: float32 [1, 768, 3072], P(None, ('batch', 'seq'))
- new_first_w_out: float32 [1, 3072, 768], P(None, None, ('batch', 'seq'))
- new_second_w_out: float32 [1, 3072, 768], P(None, None, ('batch', 'seq'))
- new_w_out: float32 [1, 3072, 768], P(None, None, ('batch', 'seq'))
- new_first_b_in: float32 [1, 3072], P(None, ('batch', 'seq'))
- new_second_b_in: float32 [1, 3072], P(None, ('batch', 'seq'))
- new_b_in: float32 [1, 3072], P(None, ('batch', 'seq'))
- new_first_vec: float32 [1, 5, 768], P(None, None, ('batch', 'seq'))
- new_second_vec: float32 [1, 5, 768], P(None, None, ('batch', 'seq'))
- new_vec: float32 [1, 5, 768], P(None, None, ('batch', 'seq'))
Inputs may be any that keep to these rules, and one draw needn't show every extreme that they name: `vec_params`: rows 0 and 3 of every layer are positive norm gains; rows 1, 2 and 4 are shifts and biases of both signs.
All inputs are finite; a program needn't handle non-finite values.
Results may differ from a plain program's by a relative error of at most 0.0079.
Values may be sent and summed in bfloat16 or wider, within the bound.
A program may use at most 192 MiB of HBM per device.

v0:
```python
import math

import jax
import jax.numpy as jnp
from jax import lax
from jax.sharding import PartitionSpec as P

STEP_COUNT = 10


beta_first = 0.5
beta_second = 0.5
rate_matrix = 0.03
rate_vector = 0.2
weight_decay = 0.01
adam_epsilon = 1e-08
norm_epsilon = 1e-06
clip_limit = 1.0


def dft_tables(row_index, column_index, seq_len):
    product = row_index[:, None] * column_index[None, :] % seq_len
    angle = product.astype(jnp.float32) * (2.0 * math.pi / seq_len)
    return (jnp.cos(angle).astype(jnp.bfloat16), jnp.sin(angle).astype(jnp.bfloat16))


def layer_norm(values, gain, shift):
    centre = jnp.mean(values, axis=-1, keepdims=True)
    centred = values - centre
    spread = jnp.mean(centred * centred, axis=-1, keepdims=True)
    return centred * lax.rsqrt(spread + norm_epsilon) * gain + shift


def gelu_tanh(values):
    return jax.nn.gelu(values, approximate=True)


def adam_update(weight, gradient, first, second, rate, step_count):
    first_new = beta_first * first + (1.0 - beta_first) * gradient
    second_new = beta_second * second + (1.0 - beta_second) * gradient * gradient
    first_hat = first_new / (1.0 - beta_first**step_count)
    second_hat = second_new / (1.0 - beta_second**step_count)
    updated = weight - rate * (
        first_hat / (jnp.sqrt(second_hat) + adam_epsilon) + weight_decay * weight
    )
    return (first_new, second_new, updated)


def local(
    activations,
    cotangent,
    w_in,
    w_out,
    b_in,
    vec_params,
    first_w_in,
    second_w_in,
    first_w_out,
    second_w_out,
    first_b_in,
    second_b_in,
    first_vec,
    second_vec,
):
    layers = w_in.shape[0]
    seq_count, block_len, model_width = activations.shape
    seq_devices = lax.axis_size("seq")
    seq_len = block_len * seq_devices
    dft_scale = 1.0 / math.sqrt(seq_len * model_width)
    first_row = lax.axis_index("seq") * block_len
    my_rows = first_row + jnp.arange(block_len, dtype=jnp.int32)
    feature_line = jnp.arange(model_width, dtype=jnp.int32)
    cos_model, sin_model = dft_tables(feature_line, feature_line, model_width)
    table_fwd = jnp.concatenate([cos_model, sin_model], axis=1)
    table_back = jnp.transpose(table_fwd)
    layer_index = 0
    pieces = (
        w_in[layer_index].astype(jnp.bfloat16),
        w_out[layer_index].astype(jnp.bfloat16),
        b_in[layer_index].astype(jnp.bfloat16),
        vec_params[layer_index].astype(jnp.bfloat16),
    )
    gathered = [
        (
            lax.all_gather(pieces[0], ("batch", "seq"), axis=0, tiled=True),
            lax.all_gather(pieces[1], ("batch", "seq"), axis=1, tiled=True),
            lax.all_gather(pieces[2], ("batch", "seq"), axis=0, tiled=True),
            lax.all_gather(pieces[3], ("batch", "seq"), axis=1, tiled=True),
        )
    ]
    zeros_block = jnp.zeros((seq_count, block_len, model_width), jnp.float32)
    stream = activations.astype(jnp.float32)
    layer_index = 0
    weight_first, weight_second, bias_low, vec_low = gathered[layer_index]
    vec_float = vec_low.astype(jnp.float32)
    bias_float = bias_low.astype(jnp.float32)
    joined = jnp.dot(
        stream.astype(jnp.bfloat16), table_fwd, preferred_element_type=jnp.float32
    ).astype(jnp.bfloat16)
    halves = (joined[..., :model_width], joined[..., model_width:])
    shard_piece = (
        lax.all_gather(halves[0], "seq", axis=1, tiled=True),
        lax.all_gather(halves[1], "seq", axis=1, tiled=True),
    )
    piece_len = shard_piece[0].shape[1]
    cos_block, sin_block = dft_tables(my_rows, jnp.arange(piece_len, dtype=jnp.int32), seq_len)
    running = jnp.einsum(
        "ij,sjd->sid", cos_block, shard_piece[0], preferred_element_type=jnp.float32
    )
    mixed = (
        running
        - jnp.einsum("ij,sjd->sid", sin_block, shard_piece[1], preferred_element_type=jnp.float32)
    ) * dft_scale
    normed, norm_first_back = jax.vjp(layer_norm, stream + mixed, vec_float[0], vec_float[1])
    normed_low = normed.astype(jnp.bfloat16)
    pre_act = jnp.dot(normed_low, weight_first, preferred_element_type=jnp.float32) + bias_float
    activated, gelu_back = jax.vjp(gelu_tanh, pre_act)
    act_low = activated.astype(jnp.bfloat16)
    feed = jnp.dot(act_low, weight_second, preferred_element_type=jnp.float32) + vec_float[2]
    stream, norm_second_back = jax.vjp(layer_norm, normed + feed, vec_float[3], vec_float[4])
    saved = [(norm_first_back, normed_low, gelu_back, act_low, norm_second_back)]
    block_output = stream.astype(jnp.bfloat16)
    grad_now = cotangent.astype(jnp.float32)
    raw_grads = [None] * layers
    for layer_index in reversed(range(layers)):
        weight_first, weight_second, bias_low, vec_low = gathered[layer_index]
        norm_first_back, normed_low, gelu_back, act_low, norm_second_back = saved[layer_index]
        grad_sum2, grad_gain2, grad_shift2 = norm_second_back(grad_now)
        grad_z = grad_sum2.astype(jnp.bfloat16)
        grad_weight_second = jnp.einsum(
            "stf,std->fd", act_low, grad_z, preferred_element_type=jnp.float32
        )
        grad_bias_out = jnp.sum(grad_z.astype(jnp.float32), axis=(0, 1))
        grad_act = jnp.einsum(
            "std,fd->stf", grad_z, weight_second, preferred_element_type=jnp.float32
        )
        (grad_pre,) = gelu_back(grad_act)
        grad_pre_low = grad_pre.astype(jnp.bfloat16)
        grad_weight_first = jnp.einsum(
            "std,stf->df", normed_low, grad_pre_low, preferred_element_type=jnp.float32
        )
        grad_bias_in = jnp.sum(grad_pre_low.astype(jnp.float32), axis=(0, 1))
        grad_normed = (
            jnp.einsum(
                "stf,df->std", grad_pre_low, weight_first, preferred_element_type=jnp.float32
            )
            + grad_sum2
        )
        grad_sum1, grad_gain1, grad_shift1 = norm_first_back(grad_normed)
        grad_mix_low = grad_sum1.astype(jnp.bfloat16)
        add_shard_piece = lax.all_gather(grad_mix_low, "seq", axis=1, tiled=True)
        add_piece_len = add_shard_piece.shape[1]
        add_cos_block, add_sin_block = dft_tables(
            my_rows, jnp.arange(add_piece_len, dtype=jnp.int32), seq_len
        )
        with_cos = jnp.einsum(
            "ij,sjd->sid", add_cos_block, add_shard_piece, preferred_element_type=jnp.float32
        )
        with_sin = (zeros_block, zeros_block)[1] - jnp.einsum(
            "ij,sjd->sid", add_sin_block, add_shard_piece, preferred_element_type=jnp.float32
        )
        with_cos, with_sin = (with_cos, with_sin)
        with_cos = (with_cos * dft_scale).astype(jnp.bfloat16)
        with_sin = (with_sin * dft_scale).astype(jnp.bfloat16)
        grad_halves = jnp.concatenate([with_cos, with_sin], axis=-1)
        grad_now = grad_sum1 + jnp.dot(grad_halves, table_back, preferred_element_type=jnp.float32)
        grad_vec = jnp.stack([grad_gain1, grad_shift1, grad_bias_out, grad_gain2, grad_shift2])
        layer_terms = (grad_weight_first, grad_weight_second, grad_bias_in, grad_vec)
        raw_grads[layer_index] = (
            lax.psum_scatter(layer_terms[0], ("batch", "seq"), scatter_dimension=0, tiled=True),
            lax.psum_scatter(layer_terms[1], ("batch", "seq"), scatter_dimension=1, tiled=True),
            lax.psum_scatter(layer_terms[2], ("batch", "seq"), scatter_dimension=0, tiled=True),
            lax.psum_scatter(layer_terms[3], ("batch", "seq"), scatter_dimension=1, tiled=True),
        )
    shard_w_in = jnp.stack([entry[0] for entry in raw_grads])
    shard_w_out = jnp.stack([entry[1] for entry in raw_grads])
    shard_b_in = jnp.stack([entry[2] for entry in raw_grads])
    shard_vec = jnp.stack([entry[3] for entry in raw_grads])
    local_squares = jnp.sum(shard_w_in * shard_w_in) + jnp.sum(shard_w_out * shard_w_out)
    local_squares = (
        local_squares + jnp.sum(shard_b_in * shard_b_in) + jnp.sum(shard_vec * shard_vec)
    )
    norm_value = jnp.sqrt(lax.psum(local_squares, ("batch", "seq")))
    factor = clip_limit / jnp.maximum(norm_value, clip_limit)
    upd_w_in = adam_update(
        w_in, factor * shard_w_in, first_w_in, second_w_in, rate_matrix, STEP_COUNT
    )
    upd_w_out = adam_update(
        w_out, factor * shard_w_out, first_w_out, second_w_out, rate_matrix, STEP_COUNT
    )
    upd_b_in = adam_update(
        b_in, factor * shard_b_in, first_b_in, second_b_in, rate_vector, STEP_COUNT
    )
    upd_vec = adam_update(
        vec_params, factor * shard_vec, first_vec, second_vec, rate_vector, STEP_COUNT
    )
    return (
        block_output,
        grad_now,
        norm_value,
        upd_w_in[0],
        upd_w_in[1],
        upd_w_in[2],
        upd_w_out[0],
        upd_w_out[1],
        upd_w_out[2],
        upd_b_in[0],
        upd_b_in[1],
        upd_b_in[2],
        upd_vec[0],
        upd_vec[1],
        upd_vec[2],
    )


def solution(mesh):
    in_specs = (
        P("batch", "seq", None),
        P("batch", "seq", None),
        P(None, ("batch", "seq"), None),
        P(None, None, ("batch", "seq")),
        P(None, ("batch", "seq")),
        P(None, None, ("batch", "seq")),
        P(None, ("batch", "seq"), None),
        P(None, ("batch", "seq"), None),
        P(None, None, ("batch", "seq")),
        P(None, None, ("batch", "seq")),
        P(None, ("batch", "seq")),
        P(None, ("batch", "seq")),
        P(None, None, ("batch", "seq")),
        P(None, None, ("batch", "seq")),
    )
    out_specs = (
        P("batch", "seq", None),
        P("batch", "seq", None),
        P(),
        P(None, ("batch", "seq"), None),
        P(None, ("batch", "seq"), None),
        P(None, ("batch", "seq"), None),
        P(None, None, ("batch", "seq")),
        P(None, None, ("batch", "seq")),
        P(None, None, ("batch", "seq")),
        P(None, ("batch", "seq")),
        P(None, ("batch", "seq")),
        P(None, ("batch", "seq")),
        P(None, None, ("batch", "seq")),
        P(None, None, ("batch", "seq")),
        P(None, None, ("batch", "seq")),
    )
    return jax.shard_map(local, mesh=mesh, in_specs=in_specs, out_specs=out_specs, check_vma=False)
```

profile of v0, /device:TPU:0, one launch (start us, length us, event | category | flops | bytes accessed | tf_op | source)
XLA Modules:
  0.0 707.3 jit_solution(9853697602391163444)
XLA Ops:
  7.2 9.9 %sine_convert_fusion = (bf16[768,768]{0,1:T(8,128)(2,1)S(1)}, bf16[768,768]{0,1:T(8,128)(2,1)S(1)}) fusion(), kind=kLoop, calls=%fused_computation.28 | loop fusion | flops 6488064 | bytes 2359296 | tf_op jit(solution)/shard_map/convert_element_type | solution.py:24
  17.2 2.2 fusion.20
  23.1 74.0 %all-gather = bf16[1,5,768]{1,0,2:T(2,128)(2,1)S(1)} all-gather(bf16[1,5,24]{1,0,2:T(2,128)(2,1)S(1)} %copy.90), channel_id=2, replica_groups=mesh['batch'=4,'seq'=8] {'batch','seq'}, dimensions={2}, use_global_device_ids=true | all-gather | bytes 7920 | tf_op jit(solution)/shard_map/all_gather | solution.py:88
  97.8 39.8 %all-reduce = bf16[3072]{0:T(1024)(128)(2,1)S(1)} all-reduce(bf16[3072]{0:T(1024)(128)(2,1)S(1)} %dynamic-update-slice), channel_id=4, replica_groups=mesh['batch'=4,'seq'=8] {'batch','seq'}, use_global_device_ids=true, to_apply=%add | all-reduce | flops 3072 | bytes 12288
  138.4 12.4 %slice_reduce_fusion.1 = (f32[768]{0:T(1024)S(1)}, f32[768]{0:T(1024)}, f32[768]{0:T(1024)S(1)}, f32[768]{0:T(1024)S(1)}, f32[768]{0:T(1024)}) fusion(f32[1,5,768]{1,0,2:T(1,128)S(1)} %convert_element_type.134), kind=kLoop, calls=%fused_computation.88 | loop fusion | bytes 30720 | tf_op jit(solution)/shard_map/slice | solution.py:120
  150.8 4.8 fusion.70
  157.1 4.8 fusion.113
  163.4 58.1 %all-gather.16.cloned.1.call-done = bf16[1,768,3072]{2,1,0:T(8,128)(2,1)} async-done(((bf16[1,24,3072]{2,1,0:T(8,128)(2,1)}), bf16[1,768,3072]{2,1,0:T(8,128)(2,1)}) %all-gather.16.cloned.1.call-update) | async-done | bytes 4718608 | tf_op jit(solution)/shard_map/all_gather | solution.py:85
  221.6 4.2 fusion.8
  225.8 61.7 %all-gather.18.cloned.1.call-done = bf16[1,3072,768]{1,2,0:T(8,128)(2,1)} async-done(((bf16[1,3072,24]{1,2,0:T(8,128)(2,1)}), bf16[1,3072,768]{1,2,0:T(8,128)(2,1)}) %all-gather.18.cloned.1.call-update) | async-done | bytes 4718608 | tf_op jit(solution)/shard_map/all_gather | solution.py:86
  287.4 4.4 fusion.114
  294.0 1.8 convert_reduce_fusion.2
  295.8 4.3 convert_reduce_fusion
  300.1 2.4 multiply_reduce_fusion
  304.7 4.7 convolution_bitcast_fusion
  311.1 4.5 convolution_bitcast_fusion.1
  317.6 45.3 %all-reduce.3 = (f32[3072]{0:T(1024)S(1)}, f32[5,768]{1,0:T(8,128)S(1)}) all-reduce(f32[3072]{0:T(1024)S(1)} %copy-done.31, f32[5,768]{1,0:T(8,128)S(1)} %stack.27), channel_id=8, replica_groups=mesh['batch'=4,'seq'=8] {'batch','seq'}, use_global_device_ids=true, to_apply=%region_13.14.clone | all-reduce | flops 6912 | bytes 55296
  364.3 2.5 all-gather.14.cloned.1.call-done
  366.8 4.9 fusion.43
  371.7 2.9 fusion.44
  375.9 130.4 %reduce-scatter.6.cloned.1.call-done = f32[3072,24]{0,1:T(8,128)} async-done(((f32[3072,768]{0,1:T(8,128)}), f32[3072,24]{0,1:T(8,128)}) %reduce-scatter.6.cloned.1.call-update) | async-done | bytes 294928 | tf_op jit(solution)/shard_map/reduce_scatter | solution.py:171
  508.0 139.8 %reduce-scatter.4.cloned.1.call-done = f32[24,3072]{1,0:T(8,128)} async-done(((f32[768,3072]{1,0:T(8,128)}), f32[24,3072]{1,0:T(8,128)}) %reduce-scatter.4.cloned.1.call-update) | async-done | bytes 294928 | tf_op jit(solution)/shard_map/reduce_scatter | solution.py:170
  653.3 39.7 %psum.7 = f32[]{:T(128)} all-reduce(f32[]{:T(128)S(6)} %add.207), channel_id=1, replica_groups=mesh['batch'=4,'seq'=8] {'batch','seq'}, use_global_device_ids=true, to_apply=%region_22.23 | all-reduce | flops 1 | bytes 8 | tf_op jit(solution)/shard_map/psum | solution.py:183
  696.2 2.0 multiply_subtract_fusion
  (164 shorter events, 26.6 us)
Async XLA Ops:
  7.2 143.6 %all-gather.10.cloned.1.call-start = ((), (), s32[]{:S(2)}) async-start(), calls=%async_computation.2 | async-start | bytes 3538944 | tf_op jit(solution)/shard_map/all_gather | solution.py:102
  19.4 78.1 %copy-start.40 = (f32[1,96]{1,0:T(1,128)S(1)}, f32[1,96]{1,0:T(1,128)}, u32[]{:S(2)}) copy-start(f32[1,96]{1,0:T(1,128)} %param.18) | copy-start | bytes 1156
  19.5 118.7 %copy-start.20 = (bf16[2,128,768]{2,1,0:T(8,128)(2,1)S(1)}, bf16[2,128,768]{2,1,0:T(8,128)(2,1)}, u32[]{:S(2)}) copy-start(bf16[2,128,768]{2,1,0:T(8,128)(2,1)} %param.15) | copy-start | bytes 1179652
  20.4 136.6 %all-gather.12.cloned.1.call-start = ((), (), s32[]{:S(2)}) async-start(), calls=%async_computation.3 | async-start | bytes 3538944 | tf_op jit(solution)/shard_map/all_gather | solution.py:103
  21.2 200.4 %all-gather.16.cloned.1.call-start = ((), (), s32[]{:S(2)}) async-start(), calls=%async_computation.7 | async-start | bytes 4866048 | tf_op jit(solution)/shard_map/all_gather | solution.py:85
  21.9 265.5 %all-gather.18.cloned.1.call-start = ((), (), s32[]{:S(2)}) async-start(), calls=%async_computation.8 | async-start | bytes 4866048 | tf_op jit(solution)/shard_map/all_gather | solution.py:86
  22.7 344.1 %all-gather.14.cloned.1.call-start = ((), (), s32[]{:S(2)}) async-start(), calls=%async_computation.4 | async-start | bytes 3538944 | tf_op jit(solution)/shard_map/all_gather | solution.py:151
  162.9 58.7 %copy-start.34 = (f32[2,128]{1,0:T(2,128)}, f32[2,128]{1,0:T(2,128)S(1)}, u32[]{:S(2)}) copy-start(f32[2,128]{1,0:T(2,128)S(1)} %multiply_reduce_fusion.3) | copy-start | bytes 3076
  304.7 201.7 %reduce-scatter.6.cloned.1.call-start = ((), (), s32[]{:S(2)}) async-start(), calls=%async_computation.6 | async-start | bytes 9732096 | tf_op jit(solution)/shard_map/reduce_scatter | solution.py:171
  309.4 338.4 %reduce-scatter.4.cloned.1.call-start = ((), (), s32[]{:S(2)}) async-start(), calls=%async_computation.5 | async-start | bytes 9732096 | tf_op jit(solution)/shard_map/reduce_scatter | solution.py:170
  315.6 51.1 %copy-start.46 = (s32[128]{0:T(128)S(1)}, s32[128]{0:T(128)}, u32[]{:S(2)}) copy-start(s32[128]{0:T(128)} %copy-done.45) | copy-start | bytes 1540
  374.7 319.0 %copy-start.33 = (f32[1,5,24]{2,0,1:T(1,128)S(1)}, f32[1,5,24]{2,0,1:T(1,128)}, u32[]{:S(2)}) copy-start(f32[1,5,24]{2,0,1:T(1,128)} %param.19) | copy-start | bytes 1444
  374.7 319.0 %copy-start.38 = (f32[1,5,24]{2,0,1:T(1,128)S(1)}, f32[1,5,24]{2,0,1:T(1,128)}, u32[]{:S(2)}) copy-start(f32[1,5,24]{2,0,1:T(1,128)} %param.27) | copy-start | bytes 1444
  374.7 319.0 %copy-start.39 = (f32[1,5,24]{2,0,1:T(1,128)S(1)}, f32[1,5,24]{2,0,1:T(1,128)}, u32[]{:S(2)}) copy-start(f32[1,5,24]{2,0,1:T(1,128)} %param.26) | copy-start | bytes 1444
  374.7 320.9 %copy-start.41 = (f32[1,96]{1,0:T(1,128)S(1)}, f32[1,96]{1,0:T(1,128)}, u32[]{:S(2)}) copy-start(f32[1,96]{1,0:T(1,128)} %param.18) | copy-start | bytes 1156
  374.7 320.9 %copy-start.42 = (f32[1,96]{1,0:T(1,128)S(1)}, f32[1,96]{1,0:T(1,128)}, u32[]{:S(2)}) copy-start(f32[1,96]{1,0:T(1,128)} %param.25) | copy-start | bytes 1156
  374.7 320.9 %copy-start.43 = (f32[1,96]{1,0:T(1,128)S(1)}, f32[1,96]{1,0:T(1,128)}, u32[]{:S(2)}) copy-start(f32[1,96]{1,0:T(1,128)} %param.24) | copy-start | bytes 1156
  374.7 321.5 %copy-start.11 = (f32[1,3072,24]{1,2,0:T(8,128)S(1)}, f32[1,3072,24]{1,2,0:T(8,128)}, u32[]{:S(2)}) copy-start(f32[1,3072,24]{1,2,0:T(8,128)} %param.17) | copy-start | bytes 884740
  374.8 321.5 %copy-start.21 = (f32[1,3072,24]{1,2,0:T(8,128)S(1)}, f32[1,3072,24]{1,2,0:T(8,128)}, u32[]{:S(2)}) copy-start(f32[1,3072,24]{1,2,0:T(8,128)} %param.23) | copy-start | bytes 884740
  374.8 321.4 %copy-start.22 = (f32[1,3072,24]{1,2,0:T(8,128)S(1)}, f32[1,3072,24]{1,2,0:T(8,128)}, u32[]{:S(2)}) copy-start(f32[1,3072,24]{1,2,0:T(8,128)} %param.22) | copy-start | bytes 884740
  375.9 322.4 %copy-start.13 = (f32[1,24,3072]{2,1,0:T(8,128)S(1)}, f32[1,24,3072]{2,1,0:T(8,128)}, u32[]{:S(2)}) copy-start(f32[1,24,3072]{2,1,0:T(8,128)} %param.16) | copy-start | bytes 884740
  375.9 322.4 %copy-start.23 = (f32[1,24,3072]{2,1,0:T(8,128)S(1)}, f32[1,24,3072]{2,1,0:T(8,128)}, u32[]{:S(2)}) copy-start(f32[1,24,3072]{2,1,0:T(8,128)} %param.21) | copy-start | bytes 884740
  375.9 322.4 %copy-start.24 = (f32[1,24,3072]{2,1,0:T(8,128)S(1)}, f32[1,24,3072]{2,1,0:T(8,128)}, u32[]{:S(2)}) copy-start(f32[1,24,3072]{2,1,0:T(8,128)} %param.20) | copy-start | bytes 884740
  647.8 50.4 %copy-start.14 = (f32[24,3072]{1,0:T(8,128)S(1)}, f32[24,3072]{1,0:T(8,128)}, u32[]{:S(2)}) copy-start(f32[24,3072]{1,0:T(8,128)} %reduce-scatter.4.cloned.1.call-done) | copy-start | bytes 884740
  (34 other events, 121.5 us)
Sparse Core Ops, SparseCore 0:
  20.6 69.7 all-gather.9
  93.0 64.0 all-gather.11
  160.5 60.9 all-gather.15
  224.9 62.4 all-gather.17
  304.8 61.9 all-gather.13
  372.5 133.7 reduce-scatter.5
  513.3 134.5 reduce-scatter.3
where the time goes:
time: 708 us; the launch traced here: 707 us
  waiting for transfers between devices  395 us (56%)
  blocking collectives  199 us (28%)
  matrix products  45.1 us (6%)
  other arithmetic  26.5 us (4%)
  local copies, waits for them, and re-layouts  22.6 us (3%)
  between operations  19.2 us (3%)
    reduce_scatter x1, waiting for transfers between devices, local(): lax.psum_scatter(layer_terms[0], ('batch', 'seq'), scatter_dimension=0, t...  140 us
    reduce_scatter x1, waiting for transfers between devices, local(): lax.psum_scatter(layer_terms[1], ('batch', 'seq'), scatter_dimension=1, t...  130 us
    unnamed x2, blocking collectives  85.1 us
    all_gather x1, blocking collectives, local(): lax.all_gather(pieces[3], ('batch', 'seq'), axis=1, tiled=True)  74 us
    all_gather x1, waiting for transfers between devices, local(): lax.all_gather(pieces[1], ('batch', 'seq'), axis=1, tiled=True)  61.7 us
    all_gather x1, waiting for transfers between devices, local(): lax.all_gather(pieces[0], ('batch', 'seq'), axis=0, tiled=True)  58.1 us
    psum x1, blocking collectives, local(): norm_value = jnp.sqrt(lax.psum(local_squares, ('batch', 'seq')))  39.7 us
  transfers between devices with their start and end apart: 7, of which 6 were waited for; matrix products, arithmetic and copies ran while one was open for 7% of the time, Pallas kernels for 0%

commit v1 on v0

--- a/solution.py
+++ b/solution.py
@@ -1,8 +1,14 @@
+import functools
 import math
+import types
 
 import jax
 import jax.numpy as jnp
+import ml_dtypes
+import numpy as np
 from jax import lax
+from jax.experimental import pallas as pl
+from jax.experimental.pallas import tpu as pltpu
 from jax.sharding import PartitionSpec as P
 
 STEP_COUNT = 10
@@ -46,7 +52,7 @@
     return (first_new, second_new, updated)
 
 
-def local(
+def general_layer(
     activations,
     cotangent,
     w_in,
@@ -64,10 +70,10 @@
 ):
     layers = w_in.shape[0]
     seq_count, block_len, model_width = activations.shape
-    seq_devices = lax.axis_size("seq")
+    seq_devices = lax.axis_size(BOTH[1])
     seq_len = block_len * seq_devices
     dft_scale = 1.0 / math.sqrt(seq_len * model_width)
-    first_row = lax.axis_index("seq") * block_len
+    first_row = lax.axis_index(BOTH[1]) * block_len
     my_rows = first_row + jnp.arange(block_len, dtype=jnp.int32)
     feature_line = jnp.arange(model_width, dtype=jnp.int32)
     cos_model, sin_model = dft_tables(feature_line, feature_line, model_width)
@@ -82,10 +88,10 @@
     )
     gathered = [
         (
-            lax.all_gather(pieces[0], ("batch", "seq"), axis=0, tiled=True),
-            lax.all_gather(pieces[1], ("batch", "seq"), axis=1, tiled=True),
-            lax.all_gather(pieces[2], ("batch", "seq"), axis=0, tiled=True),
-            lax.all_gather(pieces[3], ("batch", "seq"), axis=1, tiled=True),
+            lax.all_gather(pieces[0], BOTH, axis=0, tiled=True),
+            lax.all_gather(pieces[1], BOTH, axis=1, tiled=True),
+            lax.all_gather(pieces[2], BOTH, axis=0, tiled=True),
+            lax.all_gather(pieces[3], BOTH, axis=1, tiled=True),
         )
     ]
     zeros_block = jnp.zeros((seq_count, block_len, model_width), jnp.float32)
@@ -99,8 +105,8 @@
     ).astype(jnp.bfloat16)
     halves = (joined[..., :model_width], joined[..., model_width:])
     shard_piece = (
-        lax.all_gather(halves[0], "seq", axis=1, tiled=True),
-        lax.all_gather(halves[1], "seq", axis=1, tiled=True),
+        lax.all_gather(halves[0], BOTH[1], axis=1, tiled=True),
+        lax.all_gather(halves[1], BOTH[1], axis=1, tiled=True),
     )
     piece_len = shard_piece[0].shape[1]
     cos_block, sin_block = dft_tables(my_rows, jnp.arange(piece_len, dtype=jnp.int32), seq_len)
@@ -148,7 +154,7 @@
         )
         grad_sum1, grad_gain1, grad_shift1 = norm_first_back(grad_normed)
         grad_mix_low = grad_sum1.astype(jnp.bfloat16)
-        add_shard_piece = lax.all_gather(grad_mix_low, "seq", axis=1, tiled=True)
+        add_shard_piece = lax.all_gather(grad_mix_low, BOTH[1], axis=1, tiled=True)
         add_piece_len = add_shard_piece.shape[1]
         add_cos_block, add_sin_block = dft_tables(
             my_rows, jnp.arange(add_piece_len, dtype=jnp.int32), seq_len
@@ -167,10 +173,10 @@
         grad_vec = jnp.stack([grad_gain1, grad_shift1, grad_bias_out, grad_gain2, grad_shift2])
         layer_terms = (grad_weight_first, grad_weight_second, grad_bias_in, grad_vec)
         raw_grads[layer_index] = (
-            lax.psum_scatter(layer_terms[0], ("batch", "seq"), scatter_dimension=0, tiled=True),
-            lax.psum_scatter(layer_terms[1], ("batch", "seq"), scatter_dimension=1, tiled=True),
-            lax.psum_scatter(layer_terms[2], ("batch", "seq"), scatter_dimension=0, tiled=True),
-            lax.psum_scatter(layer_terms[3], ("batch", "seq"), scatter_dimension=1, tiled=True),
+            lax.psum_scatter(layer_terms[0], BOTH, scatter_dimension=0, tiled=True),
+            lax.psum_scatter(layer_terms[1], BOTH, scatter_dimension=1, tiled=True),
+            lax.psum_scatter(layer_terms[2], BOTH, scatter_dimension=0, tiled=True),
+            lax.psum_scatter(layer_terms[3], BOTH, scatter_dimension=1, tiled=True),
         )
     shard_w_in = jnp.stack([entry[0] for entry in raw_grads])
     shard_w_out = jnp.stack([entry[1] for entry in raw_grads])
@@ -180,7 +186,7 @@
     local_squares = (
         local_squares + jnp.sum(shard_b_in * shard_b_in) + jnp.sum(shard_vec * shard_vec)
     )
-    norm_value = jnp.sqrt(lax.psum(local_squares, ("batch", "seq")))
+    norm_value = jnp.sqrt(lax.psum(local_squares, BOTH))
     factor = clip_limit / jnp.maximum(norm_value, clip_limit)
     upd_w_in = adam_update(
         w_in, factor * shard_w_in, first_w_in, second_w_in, rate_matrix, STEP_COUNT
@@ -213,38 +219,1095 @@
     )
 
 
+MESH = pl.DeviceIdType.MESH
+F32 = jnp.float32
+BF16 = jnp.bfloat16
+NN = (((1,), (0,)), ((), ()))
+NT = (((1,), (1,)), ((), ()))
+TN = (((0,), (0,)), ((), ()))
+
+
+def dot(a, b, dims=NN):
+    return lax.dot_general(a, b, dims, preferred_element_type=F32)
+
+
+class Sizes:
+    def __init__(self, mesh, seqs, block, width, hidden):
+        self.batch, self.seq = mesh.shape["batch"], mesh.shape["seq"]
+        self.xs, self.ys, self.zs = self.batch // 2, 2, self.seq // 2
+        self.devices = self.batch * self.seq
+        self.seqs, self.block, self.width, self.hidden = seqs, block, width, hidden
+        self.length = block * self.seq
+        self.rows = width // self.devices
+        self.slab = 2 * self.rows
+        self.segment = self.zs * self.slab
+        self.half = hidden // 2
+        self.chunks = 4
+        self.cols = self.half // self.chunks
+        self.packed = width // self.seq
+        self.tokens = seqs * block
+        self.bias = hidden // self.devices
+
+    def fits(self):
+        return (
+            self.batch == 4
+            and self.seq % 2 == 0
+            and self.width % self.devices == 0
+            and self.slab % 16 == 0
+            and self.packed % 32 == 0
+            and self.block % 128 == 0
+            and self.half % (128 * self.chunks) == 0
+            and self.rows <= 128
+            and self.bias <= 128
+            and 5 * self.rows <= self.width
+        )
+
+    def owner(self, x, core, z, y):
+        return (2 * x + core) * self.seq + 2 * z + y
+
+    def place_owner(self):
+        return [
+            self.owner(x, core, z, y)
+            for y in range(self.ys)
+            for x in range(self.xs)
+            for z in range(self.zs)
+            for core in range(2)
+        ]
+
+
+def cos_sin(rows, columns, count):
+    angle = (rows[:, None] * columns[None, :] % count) * (2.0 * math.pi / count)
+    return np.cos(angle), np.sin(angle)
+
+
+def host_tables(n):
+    width, half = n.width, n.packed // 2
+    owners = np.array(n.place_owner())
+    order = (owners[:, None] * n.rows + np.arange(n.rows)[None, :]).reshape(-1)
+    line = np.arange(width)
+    cosine, sine = cos_sin(line, line, width)
+    pack = np.zeros((width, width))
+    unpack = np.zeros((width, width))
+    for k in range(width // 2):
+        device, inner = divmod(k, half)
+        at_cos = device * n.packed + inner
+        at_sin = at_cos + half
+        pack[at_cos] = cosine[k]
+        unpack[at_cos, k] = 1.0
+        if k:
+            unpack[at_cos, width - k] = 1.0
+            pack[at_sin] = sine[k]
+            unpack[at_sin, k] = -1.0
+            unpack[at_sin, width - k] = 1.0
+    pack[half] = cosine[width // 2]
+    unpack[half, width // 2] = 1.0
+    perm = np.zeros((width, width))
+    perm[order, np.arange(width)] = 1.0
+    positions = np.arange(n.length)
+    by_length = np.stack(cos_sin(positions, positions, n.length))
+    vec_mask = np.zeros((n.devices, width))
+    vec_mask[np.repeat(owners, n.rows), np.arange(width)] = 1.0
+    vec_spread = np.zeros((128, width))
+    vec_spread[np.arange(width) % n.rows, np.arange(width)] = 1.0
+    bias_spread = np.zeros((128, n.half))
+    bias_spread[np.arange(n.half) % n.bias, np.arange(n.half)] = 1.0
+
+    def low(a):
+        return jnp.asarray(a.astype(np.float32).astype(ml_dtypes.bfloat16))
+
+    return types.SimpleNamespace(
+        tt_f=low(pack),
+        by_length=low(by_length),
+        un_f=low(unpack[:, order]),
+        perm=low(perm),
+        tt_b=low(pack[:, order]),
+        un_b=low(unpack),
+        vec_mask=jnp.asarray(vec_mask.astype(np.float32)),
+        vec_spread=low(vec_spread),
+        bias_spread=low(bias_spread),
+    )
+
+
+TABLES = ("tt_f", "by_length", "un_f", "perm", "tt_b", "un_b")
+
+
+def layer_kernel(n, names, *refs):
+    r = types.SimpleNamespace(**dict(zip(names, refs)))
+    batch_at, seq_at = lax.axis_index("batch"), lax.axis_index("seq")
+    x, core = batch_at // 2, batch_at % 2
+    z, y = seq_at // 2, seq_at % 2
+    tokens, width, seg, slab = n.tokens, n.width, n.segment, n.slab
+    started = []
+
+    def aligned(at, by):
+        return pl.multiple_of(at * by, by)
+
+    def rows_of(at, by):
+        return pl.ds(aligned(at, by), by)
+
+    def remote(src, dst, send, recv, batch_to, seq_to):
+        return pltpu.make_async_remote_copy(
+            src_ref=src,
+            dst_ref=dst,
+            send_sem=send,
+            recv_sem=recv,
+            device_id=(batch_to, seq_to),
+            device_id_type=MESH,
+        )
+
+    def go(copy):
+        copy.start()
+        started.append(copy)
+        return copy
+
+    other_core = 2 * x + 1 - core
+    other_x = 2 * (1 - x) + core
+    other_y = 2 * z + 1 - y
+
+    def plane(k):
+        return (seq_at + k) % n.seq
+
+    def plane_from(k):
+        return (seq_at + n.seq - k) % n.seq
+
+    def across(k):
+        return (batch_at + k) % n.batch
+
+    def across_from(k):
+        return (batch_at + n.batch - k) % n.batch
+
+    loads = types.SimpleNamespace()
+    for i, name in enumerate(TABLES):
+        load = pltpu.make_async_copy(getattr(r, name), getattr(r, name + "_v"), r.load_sem.at[i])
+        setattr(loads, name, load)
+        load.start()
+
+    barrier = pltpu.get_barrier_semaphore()
+    for k in range(1, n.seq):
+        pl.semaphore_signal(barrier, inc=1, device_id=(batch_at, plane(k)), device_id_type=MESH)
+    for k in range(1, n.batch):
+        pl.semaphore_signal(barrier, inc=1, device_id=(across(k), seq_at), device_id_type=MESH)
+    pl.semaphore_wait(barrier, n.seq + n.batch - 2)
+
+    weights = (r.w1, r.w2)
+    give = pl.ds(aligned(1 - core, n.half), n.half)
+    keep = pl.ds(aligned(core, n.half), n.half)
+    core_rows = pl.ds(aligned(core, n.rows), n.rows)
+    swaps = [
+        go(
+            remote(
+                weights[m].at[:, give],
+                r.stage.at[m, core_rows],
+                r.swap_send.at[m],
+                r.swap_recv.at[m],
+                other_core,
+                seq_at,
+            )
+        )
+        for m in range(2)
+    ]
+
+    tile = r.tile
+    tile[...] = jnp.zeros(tile.shape, F32)
+    tile[0:5, 0 : n.rows] = r.vec[...]
+    tile[5:6, 0 : n.bias] = r.bias[...]
+    small = r.small
+    small_one = [
+        go(
+            remote(
+                tile,
+                small.at[batch_at, seq_at],
+                r.small_send.at[k - 1],
+                r.small_recv.at[k - 1],
+                batch_at,
+                plane(k),
+            )
+        )
+        for k in range(1, n.seq)
+    ]
+    small[batch_at, seq_at] = tile[...]
+
+    def mix_start(t, source, table):
+        y_ref, l_ref = r.y_buf.at[t], r.l_buf.at[t]
+        y_ref[...] = dot(table[...], source, NT).astype(BF16)
+        for k in range(1, n.seq):
+            go(
+                remote(
+                    y_ref.at[rows_of(plane(k), n.packed)],
+                    l_ref.at[seq_at],
+                    r.mix_send.at[2 * t, k - 1],
+                    r.mix_recv.at[2 * t, k - 1],
+                    batch_at,
+                    plane(k),
+                )
+            )
+        l_ref[seq_at] = y_ref[rows_of(seq_at, n.packed), :]
+
+    def mix_turn(t):
+        l_ref, z_ref, r_ref = r.l_buf.at[t], r.z_buf.at[t], r.r_buf.at[t]
+        for k in range(1, n.seq):
+            remote(
+                r.y_buf.at[t, rows_of(plane(k), n.packed)],
+                l_ref.at[plane_from(k)],
+                r.mix_send.at[2 * t, k - 1],
+                r.mix_recv.at[2 * t, k - 1],
+                batch_at,
+                plane(k),
+            ).wait_recv()
+        left = jnp.concatenate(
+            [
+                jnp.concatenate(
+                    [l_ref[d, :, g * n.block : (g + 1) * n.block] for d in range(n.seq)], axis=1
+                )
+                for g in range(n.seqs)
+            ],
+            axis=0,
+        )
+        r.left[...] = left
+        inner = lax.broadcasted_iota(jnp.int32, (n.seqs * n.packed, 1), 0) % n.packed
+        first = (inner < n.packed // 2) | ((inner == n.packed // 2) & (seq_at == 0))
+        scale = 1.0 / math.sqrt(n.length * n.width)
+        for e in range(n.seq):
+            at = slice(e * n.block, (e + 1) * n.block)
+            by_cos = dot(r.left[...], r.by_length_v[0, :, at])
+            by_sin = dot(r.left[...], r.by_length_v[1, :, at])
+            z_ref[e] = (jnp.where(first, by_cos, by_sin) * scale).astype(BF16)
+        for k in range(1, n.seq):
+            go(
+                remote(
+                    z_ref.at[plane(k)],
+                    r_ref.at[seq_at],
+                    r.mix_send.at[2 * t + 1, k - 1],
+                    r.mix_recv.at[2 * t + 1, k - 1],
+                    batch_at,
+                    plane(k),
+                )
+            )
+        r_ref[seq_at] = z_ref[seq_at]
+
+    def mix_finish(t, table):
+        r_ref = r.r_buf.at[t]
+        for k in range(1, n.seq):
+            remote(
+                r.z_buf.at[t, plane(k)],
+                r_ref.at[plane_from(k)],
+                r.mix_send.at[2 * t + 1, k - 1],
+                r.mix_recv.at[2 * t + 1, k - 1],
+                batch_at,
+                plane(k),
+            ).wait_recv()
+        parts = [
+            r_ref[:, g * n.packed : (g + 1) * n.packed, :].reshape(width, n.block)
+            for g in range(n.seqs)
+        ]
+        r.mixed[...] = dot(jnp.concatenate(parts, axis=1), table[...], TN)
+
+    loads.tt_f.wait()
+    mix_start(0, r.x[...], r.tt_f_v)
+
+    full = r.full
+
+    def seg_rows(sx, sy):
+        return rows_of(sy * n.xs + sx, seg)
+
+    def slab_rows(sx, sy, sz):
+        return rows_of((sy * n.xs + sx) * n.zs + sz, slab)
+
+    for m in range(2):
+        r.stage[m, core_rows, :] = weights[m][:, keep]
+        remote(
+            weights[m].at[:, give],
+            r.stage.at[m, pl.ds(aligned(1 - core, n.rows), n.rows)],
+            r.swap_send.at[m],
+            r.swap_recv.at[m],
+            other_core,
+            seq_at,
+        ).wait_recv()
+        for q in range(n.chunks):
+            full[m, q, slab_rows(x, y, z), :] = r.stage[m, :, q * n.cols : (q + 1) * n.cols].astype(
+                BF16
+            )
+
+    def z_copy(m, q, d, source_z):
+        at = slab_rows(x, y, source_z)
+        return remote(
+            full.at[m, q, at],
+            full.at[m, q, at],
+            r.z_send.at[m, q, d - 1],
+            r.z_recv.at[m, q, d - 1],
+            batch_at,
+            2 * ((z + d) % n.zs) + y,
+        )
+
+    def weights_along_z(q):
+        for m in range(2):
+            for d in range(1, n.zs):
+                go(z_copy(m, q, d, z))
+
+    def turn_of(m, q):
+        return (m + q) % 2
+
+    def peer(t):
+        return (
+            batch_at + (1 - t) * (other_x - batch_at),
+            seq_at + t * (other_y - seq_at),
+        )
+
+    def away(t):
+        return x + (1 - t) * (1 - 2 * x), y + t * (1 - 2 * y)
+
+    def seg_copy(m, q, i, t, sx, sy):
+        at = seg_rows(sx, sy)
+        return remote(
+            full.at[m, q, at],
+            full.at[m, q, at],
+            r.seg_send.at[m, q, i],
+            r.seg_recv.at[m, q, i],
+            *peer(t),
+        )
+
+    def weights_one(q):
+        for m in range(2):
+            t = turn_of(m, q)
+            for d in range(1, n.zs):
+                z_copy(m, q, d, (z + n.zs - d) % n.zs).wait_recv()
+            go(seg_copy(m, q, 0, t, x, y))
+            go(seg_copy(m, q, 1, 1 - t, x, y))
+
+    def weights_two(q):
+        for m in range(2):
+            t = turn_of(m, q)
+            ax, ay = away(t)
+            seg_copy(m, q, 0, t, ax, ay).wait_recv()
+            go(seg_copy(m, q, 2, 1 - t, ax, ay))
+
+    def weights_here(m, q):
+        t = (m + q) % 2
+        bx, by = away(1 - t)
+        seg_copy(m, q, 1, 1 - t, bx, by).wait_recv()
+        seg_copy(m, q, 2, 1 - t, 1 - x, 1 - y).wait_recv()
+
+    weights_along_z(0)
+    weights_along_z(1)
+
+    for k in range(1, n.seq):
+        remote(
+            tile,
+            small.at[batch_at, plane_from(k)],
+            r.small_send.at[k - 1],
+            r.small_recv.at[k - 1],
+            batch_at,
+            plane(k),
+        ).wait_recv()
+    for k in range(1, n.batch):
+        go(
+            remote(
+                small.at[batch_at],
+                small.at[batch_at],
+                r.row_send.at[k - 1],
+                r.row_recv.at[k - 1],
+                across(k),
+                seq_at,
+            )
+        )
+
+    loads.by_length.wait()
+    mix_turn(0)
+    weights_along_z(2)
+    weights_along_z(3)
+    weights_one(0)
+
+    loads.perm.wait()
+    r.x_place[...] = dot(r.x[...], r.perm_v[...])
+    r.dy_place[...] = dot(r.dy[...], r.perm_v[...])
+    for k in range(1, n.batch):
+        remote(
+            small.at[batch_at],
+            small.at[across_from(k)],
+            r.row_send.at[k - 1],
+            r.row_recv.at[k - 1],
+            across(k),
+            seq_at,
+        ).wait_recv()
+    vec_rows = []
+    for i in range(5):
+        held = small[:, :, i, :].reshape(n.devices, 128).astype(BF16)
+        spread = dot(held, r.vec_spread[...]) * r.vec_mask[...]
+        vec_rows.append(jnp.sum(spread, axis=0, keepdims=True))
+    for i in range(5):
+        r.vecs[i : i + 1, :] = vec_rows[i]
+    half_owners = n.devices // 2
+    held = small[pl.ds(core * (n.batch // 2), n.batch // 2), :, 5, :]
+    held = held.reshape(half_owners, 128).astype(BF16)
+    bias_mask = (
+        lax.broadcasted_iota(jnp.int32, (half_owners, n.half), 0)
+        == lax.broadcasted_iota(jnp.int32, (half_owners, n.half), 1) // n.bias
+    )
+    biases = jnp.sum(
+        jnp.where(bias_mask, dot(held, r.bias_spread[...]), 0.0), axis=0, keepdims=True
+    )
+    for q in range(n.chunks):
+        r.biases[q] = biases[:, q * n.cols : (q + 1) * n.cols]
+
+    weights_one(1)
+    weights_two(0)
+    loads.un_f.wait()
+    mix_finish(0, r.un_f_v)
+
+    step = 32
+
+    def row_loop(body):
+        @pl.loop(0, tokens // step)
+        def _(i):
+            body(pl.ds(pl.multiple_of(i * step, step), step))
+
+    def mean(v):
+        return jnp.mean(v, axis=-1, keepdims=True)
+
+    def first_norm(at):
+        v = r.x_place[at, :] + r.mixed[at, :]
+        centred = v - mean(v)
+        scale = lax.rsqrt(mean(centred * centred) + norm_epsilon)
+        unit = centred * scale
+        h = unit * r.vecs[0:1, :] + r.vecs[1:2, :]
+        r.unit1[at, :] = unit
+        r.scale1[at, :] = jnp.broadcast_to(scale, (step, 128))
+        r.h[at, :] = h
+        r.h_low[at, :] = h.astype(BF16)
+
+    row_loop(first_norm)
+
+    mine, theirs = pl.ds(0, tokens), pl.ds(tokens, tokens)
+
+    def swap(i, src, dst):
+        return remote(
+            src, dst, r.core_send.at[i], r.core_recv.at[i], other_core, seq_at
+        )
+
+    swap_h = go(swap(0, r.h_low.at[mine], r.h_low.at[theirs]))
+    weights_one(2)
+    weights_two(1)
+    weights_one(3)
+    weights_two(2)
+    weights_two(3)
+    swap_h.wait_recv()
+
+    r.total[...] = jnp.zeros(r.total.shape, F32)
+    root = math.sqrt(2.0 / math.pi)
+    part = 128
+
+    @pl.loop(0, n.chunks)
+    def _(q):
+        weights_here(0, q)
+        weights_here(1, q)
+
+        @pl.loop(0, 2 * tokens // part)
+        def _(i):
+            at = pl.ds(pl.multiple_of(i * part, part), part)
+            u = dot(r.h_low[at, :], full[0, q]) + r.biases[q]
+            square = u * u
+            bent = jnp.tanh(root * u * (1.0 + 0.044715 * square))
+            half_up = 0.5 * (1.0 + bent)
+            act = (u * half_up).astype(BF16)
+            r.slope[q, at, :] = half_up + 0.5 * u * (1.0 - bent * bent) * (
+                root * (1.0 + 3.0 * 0.044715 * square)
+            )
+            r.act[q, at, :] = act
+            r.total[at, :] = r.total[at, :] + dot(act, full[1, q], NT)
+
+    r.part_low[...] = r.total[theirs, :].astype(BF16)
+    swap_ff = go(swap(1, r.part_low, r.part_in))
+    swap_ff.wait_recv()
+
+    r.sums[...] = jnp.zeros(r.sums.shape, F32)
+
+    def fold(v):
+        return jnp.sum(v.reshape(step // 8, 8, width), axis=0)
+
+    def second_norm(at):
+        v = (
+            r.h[at, :]
+            + r.total[at, :]
+            + r.part_in[at, :].astype(F32)
+            + r.vecs[2:3, :]
+        )
+        centred = v - mean(v)
+        scale = lax.rsqrt(mean(centred * centred) + norm_epsilon)
+        unit = centred * scale
+        gain = r.vecs[3:4, :]
+        r.out_low[at, :] = (unit * gain + r.vecs[4:5, :]).astype(BF16)
+        dy = r.dy_place[at, :]
+        r.sums[3] += fold(dy * unit)
+        r.sums[4] += fold(dy)
+        du = dy * gain
+        dv = scale * (du - mean(du) - unit * mean(du * unit))
+        r.dr2[at, :] = dv
+        low = dv.astype(BF16)
+        r.dz[at, :] = low
+        r.sums[2] += fold(low.astype(F32))
+
+    row_loop(second_norm)
+    swap_dz = go(swap(2, r.dz.at[mine], r.dz.at[theirs]))
+    r.h_turned[...] = jnp.transpose(r.h_low[...])
+    swap_dz.wait_recv()
+    r.dz_turned[...] = jnp.transpose(r.dz[...])
+
+    acc, out_low, in_one, in_two, in_three = (
+        r.acc,
+        r.give,
+        r.in_one,
+        r.in_two,
+        r.in_three,
+    )
+
+    def first_parts(m, q, t):
+        ax, ay = away(t)
+        return [(j, ax * (1 - t) + j * t, ay * t + j * (1 - t)) for j in range(2)]
+
+    def grad_copy_one(m, q, t, j, sx, sy):
+        return remote(
+            out_low.at[m, q, seg_rows(sx, sy)],
+            in_one.at[m, q, j],
+            r.one_send.at[m, q, j],
+            r.one_recv.at[m, q, j],
+            *peer(t),
+        )
+
+    def grads_one(m, q):
+        t = 1 - (m + q) % 2
+        for j, sx, sy in first_parts(m, q, t):
+            at = seg_rows(sx, sy)
+            out_low[m, q, at, :] = acc[m, q, at, :].astype(BF16)
+            grad_copy_one(m, q, t, j, sx, sy).start()
+
+    def grad_copy_two(m, q, t, sx, sy):
+        return remote(
+            out_low.at[m, q, seg_rows(sx, sy)],
+            in_two.at[m, q],
+            r.two_send.at[m, q],
+            r.two_recv.at[m, q],
+            *peer(t),
+        )
+
+    def grads_two(m, q):
+        t = 1 - (m + q) % 2
+        for j, sx, sy in first_parts(m, q, t):
+            grad_copy_one(m, q, t, j, sx, sy).wait_recv()
+        bx, by = away(1 - t)
+        at = seg_rows(bx, by)
+        away_j = bx * t + by * (1 - t)
+        out_low[m, q, at, :] = (acc[m, q, at, :] + in_one[m, q, away_j].astype(F32)).astype(BF16)
+        grad_copy_two(m, q, 1 - t, bx, by).start()
+        at = seg_rows(x, y)
+        here_j = x * t + y * (1 - t)
+        acc[m, q, at, :] = acc[m, q, at, :] + in_one[m, q, here_j].astype(F32)
+
+    def grad_copy_three(m, q, d):
+        to_z = (z + d) % n.zs
+        return remote(
+            out_low.at[m, q, slab_rows(x, y, to_z)],
+            in_three.at[m, q, d - 1],
+            r.three_send.at[m, q, d - 1],
+            r.three_recv.at[m, q, d - 1],
+            batch_at,
+            2 * to_z + y,
+        )
+
+    def grads_three(m, q):
+        t = 1 - (m + q) % 2
+        bx, by = away(1 - t)
+        grad_copy_two(m, q, 1 - t, bx, by).wait_recv()
+        at = seg_rows(x, y)
+        acc[m, q, at, :] = acc[m, q, at, :] + in_two[m, q].astype(F32)
+        for d in range(1, n.zs):
+            at = slab_rows(x, y, (z + d) % n.zs)
+            out_low[m, q, at, :] = acc[m, q, at, :].astype(BF16)
+            grad_copy_three(m, q, d).start()
+
+    def grads_four(m, q):
+        at = slab_rows(x, y, z)
+        value = acc[m, q, at, :]
+        for d in range(1, n.zs):
+            grad_copy_three(m, q, d).wait_recv()
+            value = value + in_three[m, q, d - 1].astype(F32)
+        r.final[m, q] = value
+
+    @pl.loop(0, n.chunks)
+    def _(q):
+        acc[1, q] = dot(r.dz_turned[...], r.act[q])
+        grads_one(1, q)
+
+    r.total[...] = jnp.zeros(r.total.shape, F32)
+
+    @pl.loop(0, n.chunks)
+    def _(q):
+        r.bias_sum[q] = jnp.zeros((8, n.cols), F32)
+
+        @pl.loop(0, 2 * tokens // part)
+        def _(i):
+            at = pl.ds(pl.multiple_of(i * part, part), part)
+            low = (dot(r.dz[at, :], full[1, q]) * r.slope[q, at, :]).astype(BF16)
+            r.dpre[q, at, :] = low
+            r.bias_sum[q] += jnp.sum(low.astype(F32).reshape(part // 8, 8, n.cols), axis=0)
+            r.total[at, :] = r.total[at, :] + dot(low, full[0, q], NT)
+
+    swap_ff.wait_send()
+    started[:] = [copy for copy in started if copy is not swap_ff]
+    r.part_low[...] = r.total[theirs, :].astype(BF16)
+    swap_dh = go(swap(3, r.part_low, r.part_in2))
+    swap_dh.wait_recv()
+
+    def first_norm_back(at):
+        dh = r.total[at, :] + r.part_in2[at, :].astype(F32) + r.dr2[at, :]
+        unit = r.unit1[at, :]
+        r.sums[0] += fold(dh * unit)
+        r.sums[1] += fold(dh)
+        du = dh * r.vecs[0:1, :]
+        dv = r.scale1[at, 0:1] * (du - mean(du) - unit * mean(du * unit))
+        low = dv.astype(BF16)
+        r.dm[at, :] = low
+        r.rest[at, :] = (dv - low.astype(F32)).astype(BF16)
+
+    row_loop(first_norm_back)
+    loads.tt_b.wait()
+    mix_start(1, r.dm[...], r.tt_b_v)
+
+    @pl.loop(0, n.chunks)
+    def _(q):
+        acc[0, q] = dot(r.h_turned[...], r.dpre[q])
+        grads_one(0, q)
+
+    for i in range(5):
+        line = jnp.sum(r.sums[i], axis=0, keepdims=True)
+        masked = line * r.vec_mask[...]
+        high = masked.astype(BF16)
+        left = masked - high.astype(F32)
+        mid = left.astype(BF16)
+        low = (left - mid.astype(F32)).astype(BF16)
+        spread = r.vec_spread[...]
+        tiles = dot(high, spread, NT) + dot(mid, spread, NT) + dot(low, spread, NT)
+        r.small_out[:, :, i, :] = tiles.reshape(n.batch, n.seq, 128)
+    line = jnp.concatenate(
+        [jnp.sum(r.bias_sum[q], axis=0, keepdims=True) for q in range(n.chunks)], axis=1
+    )
+    masked = jnp.where(bias_mask, line, 0.0)
+    high = masked.astype(BF16)
+    left = masked - high.astype(F32)
+    mid = left.astype(BF16)
+    low = (left - mid.astype(F32)).astype(BF16)
+    spread = r.bias_spread[...]
+    tiles = dot(high, spread, NT) + dot(mid, spread, NT) + dot(low, spread, NT)
+    r.small_out[:, :, 5, :] = jnp.zeros((n.batch, n.seq, 128), F32)
+    r.small_out[pl.ds(core * (n.batch // 2), n.batch // 2), :, 5, :] = tiles.reshape(
+        n.batch // 2, n.seq, 128
+    )
+    r.small_out[:, :, 6:8, :] = jnp.zeros((n.batch, n.seq, 2, 128), F32)
+    for k in range(1, n.batch):
+        go(
+            remote(
+                r.small_out.at[across(k)],
+                r.small_in.at[k - 1],
+                r.row_send2.at[k - 1],
+                r.row_recv2.at[k - 1],
+                across(k),
+                seq_at,
+            )
+        )
+
+    @pl.loop(0, n.chunks)
+    def _(q):
+        grads_two(1, q)
+
+    mix_turn(1)
+
+    total_small = r.small_out[batch_at]
+    for k in range(1, n.batch):
+        remote(
+            r.small_out.at[across(k)],
+            r.small_in.at[k - 1],
+            r.row_send2.at[k - 1],
+            r.row_recv2.at[k - 1],
+            across(k),
+            seq_at,
+        ).wait_recv()
+        total_small = total_small + r.small_in[k - 1]
+    r.small_mid[...] = total_small
+    for k in range(1, n.seq):
+        go(
+            remote(
+                r.small_mid.at[plane(k)],
+                r.small_last.at[k - 1],
+                r.small_send2.at[k - 1],
+                r.small_recv2.at[k - 1],
+                batch_at,
+                plane(k),
+            )
+        )
+
+    @pl.loop(0, n.chunks)
+    def _(q):
+        grads_three(1, q)
+
+    @pl.loop(0, n.chunks)
+    def _(q):
+        grads_two(0, q)
+
+    r.out[...] = dot(r.out_low[...], r.perm_v[...], NT).astype(BF16)
+    r.dx[...] = dot(r.dm[...], r.perm_v[...], NT) + dot(
+        r.rest[...], r.perm_v[...], NT
+    )
+    loads.un_b.wait()
+    mix_finish(1, r.un_b_v)
+    r.dx[...] = r.dx[...] + r.mixed[...]
+
+    value = r.small_mid[seq_at]
+    for k in range(1, n.seq):
+        remote(
+            r.small_mid.at[plane(k)],
+            r.small_last.at[k - 1],
+            r.small_send2.at[k - 1],
+            r.small_recv2.at[k - 1],
+            batch_at,
+            plane(k),
+        ).wait_recv()
+        value = value + r.small_last[k - 1]
+    r.g_small[...] = value
+
+    @pl.loop(0, n.chunks)
+    def _(q):
+        grads_four(1, q)
+
+    @pl.loop(0, n.chunks)
+    def _(q):
+        grads_three(0, q)
+
+    @pl.loop(0, n.chunks)
+    def _(q):
+        grads_four(0, q)
+
+    grads = (r.g1, r.g2)
+    for m in range(2):
+        r.final_turn[m] = jnp.concatenate([r.final[m, q] for q in range(n.chunks)], axis=1)
+    their_rows = pl.ds(aligned(1 - core, n.rows), n.rows)
+    back = [
+        go(
+            remote(
+                r.final_turn.at[m, their_rows],
+                r.final_in.at[m],
+                r.back_send.at[m],
+                r.back_recv.at[m],
+                other_core,
+                seq_at,
+            )
+        )
+        for m in range(2)
+    ]
+    squares = jnp.zeros((8, 128), F32)
+
+    def squares_of(v):
+        v = v * v
+        v = jnp.sum(v.reshape(v.shape[0] // 8, 8, v.shape[1]), axis=0)
+        return sum(v[:, i : i + 128] for i in range(0, v.shape[1], 128))
+
+    squares = squares + value * value
+    for m in range(2):
+        grads[m][:, keep] = r.final_turn[m, core_rows, :]
+        back[m].wait_recv()
+        grads[m][:, give] = r.final_in[m]
+        squares = squares + squares_of(grads[m][...])
+    r.norm_own[...] = squares
+    r.norm_plane[seq_at] = squares
+    for k in range(1, n.seq):
+        go(
+            remote(
+                r.norm_own,
+                r.norm_plane.at[seq_at],
+                r.norm_send.at[k - 1],
+                r.norm_recv.at[k - 1],
+                batch_at,
+                plane(k),
+            )
+        )
+    for k in range(1, n.seq):
+        remote(
+            r.norm_own,
+            r.norm_plane.at[plane_from(k)],
+            r.norm_send.at[k - 1],
+            r.norm_recv.at[k - 1],
+            batch_at,
+            plane(k),
+        ).wait_recv()
+    squares = r.norm_plane[0]
+    for k in range(1, n.seq):
+        squares = squares + r.norm_plane[k]
+    r.norm_sum[...] = squares
+    r.norm_all[batch_at] = squares
+    for k in range(1, n.batch):
+        go(
+            remote(
+                r.norm_sum,
+                r.norm_all.at[batch_at],
+                r.norm_send2.at[k - 1],
+                r.norm_recv2.at[k - 1],
+                across(k),
+                seq_at,
+            )
+        )
+    for k in range(1, n.batch):
+        remote(
+            r.norm_sum,
+            r.norm_all.at[across_from(k)],
+            r.norm_send2.at[k - 1],
+            r.norm_recv2.at[k - 1],
+            across(k),
+            seq_at,
+        ).wait_recv()
+    squares = r.norm_all[0]
+    for k in range(1, n.batch):
+        squares = squares + r.norm_all[k]
+    whole = jnp.sum(jnp.sum(squares, axis=1, keepdims=True), axis=0, keepdims=True)
+    r.norm[...] = jnp.broadcast_to(jnp.sqrt(whole), (8, 128))
+
+    for copy in started:
+        copy.wait_send()
+
+    @pl.loop(0, n.chunks)
+    def _(q):
+        for m in range(2):
+            t = 1 - (m + q) % 2
+            for j, sx, sy in first_parts(m, q, t):
+                grad_copy_one(m, q, t, j, sx, sy).wait_send()
+            bx, by = away(1 - t)
+            grad_copy_two(m, q, 1 - t, bx, by).wait_send()
+            for d in range(1, n.zs):
+                grad_copy_three(m, q, d).wait_send()
+
+
+def run_layer(n, x, dy, w1, w2, bias, vec):
+    tables = host_tables(n)
+    tokens, width, cols, q = n.tokens, n.width, n.cols, n.chunks
+    dma = pltpu.SemaphoreType.DMA
+    vmem = pltpu.VMEM
+    inputs = dict(
+        x=x,
+        dy=dy,
+        w1=w1,
+        w2=w2,
+        bias=bias,
+        vec=vec,
+        vec_mask=tables.vec_mask,
+        vec_spread=tables.vec_spread,
+        bias_spread=tables.bias_spread,
+    )
+    inputs.update({name: getattr(tables, name) for name in TABLES})
+    outputs = dict(
+        out=((tokens, width), BF16),
+        dx=((tokens, width), F32),
+        g1=((n.rows, n.hidden), F32),
+        g2=((n.rows, n.hidden), F32),
+        g_small=((8, 128), F32),
+        norm=((8, 128), F32),
+    )
+    scratch = {name + "_v": vmem(getattr(tables, name).shape, BF16) for name in TABLES}
+    scratch.update(
+        load_sem=dma((len(TABLES),)),
+        stage=vmem((2, n.slab, n.half), F32),
+        swap_send=dma((2,)),
+        swap_recv=dma((2,)),
+        tile=vmem((8, 128), F32),
+        small=vmem((n.batch, n.seq, 8, 128), F32),
+        small_send=dma((n.seq - 1,)),
+        small_recv=dma((n.seq - 1,)),
+        row_send=dma((n.batch - 1,)),
+        row_recv=dma((n.batch - 1,)),
+        y_buf=vmem((2, width, tokens), BF16),
+        l_buf=vmem((2, n.seq, n.packed, tokens), BF16),
+        left=vmem((n.seqs * n.packed, n.length), BF16),
+        z_buf=vmem((2, n.seq, n.seqs * n.packed, n.block), BF16),
+        r_buf=vmem((2, n.seq, n.seqs * n.packed, n.block), BF16),
+        mix_send=dma((4, n.seq - 1)),
+        mix_recv=dma((4, n.seq - 1)),
+        mixed=vmem((tokens, width), F32),
+        full=vmem((2, q, width, cols), BF16),
+        z_send=dma((2, q, n.zs - 1)),
+        z_recv=dma((2, q, n.zs - 1)),
+        seg_send=dma((2, q, 3)),
+        seg_recv=dma((2, q, 3)),
+        x_place=vmem((tokens, width), F32),
+        dy_place=vmem((tokens, width), F32),
+        vecs=vmem((8, width), F32),
+        biases=vmem((q, 1, cols), F32),
+        unit1=vmem((tokens, width), F32),
+        scale1=vmem((tokens, 128), F32),
+        h=vmem((tokens, width), F32),
+        h_low=vmem((2 * tokens, width), BF16),
+        core_send=dma((4,)),
+        core_recv=dma((4,)),
+        total=vmem((2 * tokens, width), F32),
+        act=vmem((q, 2 * tokens, cols), BF16),
+        slope=vmem((q, 2 * tokens, cols), F32),
+        part_low=vmem((tokens, width), BF16),
+        part_in=vmem((tokens, width), BF16),
+        part_in2=vmem((tokens, width), BF16),
+        sums=vmem((5, 8, width), F32),
+        out_low=vmem((tokens, width), BF16),
+        dr2=vmem((tokens, width), F32),
+        dz=vmem((2 * tokens, width), BF16),
+        h_turned=vmem((width, 2 * tokens), BF16),
+        dz_turned=vmem((width, 2 * tokens), BF16),
+        acc=vmem((2, q, width, cols), F32),
+        give=vmem((2, q, width, cols), BF16),
+        in_one=vmem((2, q, 2, n.segment, cols), BF16),
+        in_two=vmem((2, q, n.segment, cols), BF16),
+        in_three=vmem((2, q, n.zs - 1, n.slab, cols), BF16),
+        one_send=dma((2, q, 2)),
+        one_recv=dma((2, q, 2)),
+        two_send=dma((2, q)),
+        two_recv=dma((2, q)),
+        three_send=dma((2, q, n.zs - 1)),
+        three_recv=dma((2, q, n.zs - 1)),
+        bias_sum=vmem((q, 8, cols), F32),
+        dpre=vmem((q, 2 * tokens, cols), BF16),
+        dm=vmem((tokens, width), BF16),
+        rest=vmem((tokens, width), BF16),
+        small_out=vmem((n.batch, n.seq, 8, 128), F32),
+        small_in=vmem((n.batch - 1, n.seq, 8, 128), F32),
+        row_send2=dma((n.batch - 1,)),
+        row_recv2=dma((n.batch - 1,)),
+        small_mid=vmem((n.seq, 8, 128), F32),
+        small_last=vmem((n.seq - 1, 8, 128), F32),
+        small_send2=dma((n.seq - 1,)),
+        small_recv2=dma((n.seq - 1,)),
+        final=vmem((2, q, n.slab, cols), F32),
+        final_turn=vmem((2, n.slab, n.half), F32),
+        final_in=vmem((2, n.rows, n.half), F32),
+        back_send=dma((2,)),
+        back_recv=dma((2,)),
+        norm_own=vmem((8, 128), F32),
+        norm_plane=vmem((n.seq, 8, 128), F32),
+        norm_sum=vmem((8, 128), F32),
+        norm_all=vmem((n.batch, 8, 128), F32),
+        norm_send=dma((n.seq - 1,)),
+        norm_recv=dma((n.seq - 1,)),
+        norm_send2=dma((n.batch - 1,)),
+        norm_recv2=dma((n.batch - 1,)),
+    )
+    names = tuple(inputs) + tuple(outputs) + tuple(scratch)
+    in_vmem = pl.BlockSpec(memory_space=pltpu.VMEM)
+    anywhere = pl.BlockSpec(memory_space=pl.ANY)
+    values = pl.pallas_call(
+        functools.partial(layer_kernel, n, names),
+        out_shape=[jax.ShapeDtypeStruct(*shape) for shape in outputs.values()],
+        in_specs=[anywhere if name in TABLES else in_vmem for name in inputs],
+        out_specs=[in_vmem] * len(outputs),
+        scratch_shapes=list(scratch.values()),
+        compiler_params=pltpu.CompilerParams(
+            collective_id=0, has_side_effects=True, vmem_limit_bytes=62 * 2**20
+        ),
+        name="fused_layer",
+    )(*inputs.values())
+    return types.SimpleNamespace(**dict(zip(outputs, values)))
+
+
+def fused_layer(
+    n,
+    activations,
+    cotangent,
+    w_in,
+    w_out,
+    b_in,
+    vec_params,
+    first_w_in,
+    second_w_in,
+    first_w_out,
+    second_w_out,
+    first_b_in,
+    second_b_in,
+    first_vec,
+    second_vec,
+):
+    got = run_layer(
+        n,
+        activations.reshape(n.tokens, n.width),
+        cotangent.reshape(n.tokens, n.width),
+        w_in[0],
+        jnp.swapaxes(w_out[0], 0, 1),
+        b_in,
+        vec_params[0],
+    )
+    norm_value = got.norm[0, 0]
+    factor = clip_limit / jnp.maximum(norm_value, clip_limit)
+    grad_w_in = got.g1[None]
+    grad_w_out = jnp.swapaxes(got.g2, 0, 1)[None]
+    grad_b_in = got.g_small[5:6, : n.bias]
+    grad_vec = got.g_small[None, :5, : n.rows]
+    upd_w_in = adam_update(
+        w_in, factor * grad_w_in, first_w_in, second_w_in, rate_matrix, STEP_COUNT
+    )
+    upd_w_out = adam_update(
+        w_out, factor * grad_w_out, first_w_out, second_w_out, rate_matrix, STEP_COUNT
+    )
+    upd_b_in = adam_update(
+        b_in, factor * grad_b_in, first_b_in, second_b_in, rate_vector, STEP_COUNT
+    )
+    upd_vec = adam_update(
+        vec_params, factor * grad_vec, first_vec, second_vec, rate_vector, STEP_COUNT
+    )
+    return (
+        got.out.reshape(activations.shape),
+        got.dx.reshape(activations.shape),
+        norm_value,
+        *upd_w_in,
+        *upd_w_out,
+        *upd_b_in,
+        *upd_vec,
+    )
+
+
+def local_layer(mesh, activations, cotangent, w_in, *rest):
+    seqs, block, width = activations.shape
+    n = Sizes(mesh, seqs, block, width, w_in.shape[2])
+    if w_in.shape[0] == 1 and n.fits():
+        return fused_layer(n, activations, cotangent, w_in, *rest)
+    return general_layer(activations, cotangent, w_in, *rest)
+
+
+BOTH = ("batch", "seq")
+
+
 def solution(mesh):
     in_specs = (
-        P("batch", "seq", None),
-        P("batch", "seq", None),
-        P(None, ("batch", "seq"), None),
-        P(None, None, ("batch", "seq")),
-        P(None, ("batch", "seq")),
-        P(None, None, ("batch", "seq")),
-        P(None, ("batch", "seq"), None),
-        P(None, ("batch", "seq"), None),
-        P(None, None, ("batch", "seq")),
-        P(None, None, ("batch", "seq")),
-        P(None, ("batch", "seq")),
-        P(None, ("batch", "seq")),
-        P(None, None, ("batch", "seq")),
-        P(None, None, ("batch", "seq")),
+        P(*BOTH, None),
+        P(*BOTH, None),
+        P(None, BOTH, None),
+        P(None, None, BOTH),
+        P(None, BOTH),
+        P(None, None, BOTH),
+        P(None, BOTH, None),
+        P(None, BOTH, None),
+        P(None, None, BOTH),
+        P(None, None, BOTH),
+        P(None, BOTH),
+        P(None, BOTH),
+        P(None, None, BOTH),
+        P(None, None, BOTH),
     )
     out_specs = (
-        P("batch", "seq", None),
-        P("batch", "seq", None),
+        P(*BOTH, None),
+        P(*BOTH, None),
         P(),
-        P(None, ("batch", "seq"), None),
-        P(None, ("batch", "seq"), None),
-        P(None, ("batch", "seq"), None),
-        P(None, None, ("batch", "seq")),
-        P(None, None, ("batch", "seq")),
-        P(None, None, ("batch", "seq")),
-        P(None, ("batch", "seq")),
-        P(None, ("batch", "seq")),
-        P(None, ("batch", "seq")),
-        P(None, None, ("batch", "seq")),
-        P(None, None, ("batch", "seq")),
-        P(None, None, ("batch", "seq")),
-    )
-    return jax.shard_map(local, mesh=mesh, in_specs=in_specs, out_specs=out_specs, check_vma=False)
+        P(None, BOTH, None),
+        P(None, BOTH, None),
+        P(None, BOTH, None),
+        P(None, None, BOTH),
+        P(None, None, BOTH),
+        P(None, None, BOTH),
+        P(None, BOTH),
+        P(None, BOTH),
+        P(None, BOTH),
+        P(None, None, BOTH),
+        P(None, None, BOTH),
+        P(None, None, BOTH),
+    )
+    return jax.shard_map(
+        functools.partial(local_layer, mesh), mesh=mesh, in_specs=in_specs, out_specs=out_specs, check_vma=False)

time: 708 us -> 174 us (0.25)
  waiting for transfers between devices: 395 us -> 0 us
  blocking collectives: 199 us -> 0 us
  Pallas kernels: 0 us -> 162 us
  matrix products: 45.1 us -> 0 us
  other arithmetic: 26.5 us -> 3.65 us
  between operations: 19.2 us -> 1.5 us
  local copies, waits for them, and re-layouts: 22.6 us -> 6.01 us
    reduce_scatter x2 -> x0, waiting for transfers between devices: 270 us -> none  [the longest x1 140 us: local(): lax.psum_scatter(layer_terms[0], ('batch', 'seq'), scatter_dimension=0, t...]
    pallas_call x0 -> x1, Pallas kernels: none -> 162 us  [run_layer(): pl.pallas_call(functools.partial(layer_kernel, n, names), out_shape=[jax....]
    all_gather x5 -> x0, waiting for transfers between devices: 124 us -> none  [the longest x1 61.7 us: local(): lax.all_gather(pieces[1], ('batch', 'seq'), axis=1, tiled=True)]
    unnamed x2 -> x0, blocking collectives: 85.1 us -> none
    all_gather x1 -> x0, blocking collectives: 74 us -> none  [local(): lax.all_gather(pieces[3], ('batch', 'seq'), axis=1, tiled=True)]
    dot_general x12 -> x0, matrix products: 45.1 us -> none  [the longest x1 4.91 us: local(): jnp.einsum('ij,sjd->sid', add_cos_block, add_shard_piece, preferred_eleme...]
    psum x1 -> x0, blocking collectives: 39.7 us -> none  [local(): norm_value = jnp.sqrt(lax.psum(local_squares, ('batch', 'seq')))]
    convert_element_type x6 -> x0, other arithmetic: 13.1 us -> none  [the longest x1 9.89 us: dft_tables(): jnp.sin(angle).astype(jnp.bfloat16)]
  transfers between devices with their start and end apart: 7 -> 0, of which waited for: 6 -> 0; matrix products, arithmetic and copies ran while one was open for 7% -> 0% of each run, Pallas kernels for 0% -> 0%
where the time goes in v1:
time: 174 us; the launch traced here: 173 us
  Pallas kernels  162 us (93%)
  local copies, waits for them, and re-layouts  6.01 us (3%)
  other arithmetic  3.65 us (2%)
    pallas_call x1, Pallas kernels, run_layer(): pl.pallas_call(functools.partial(layer_kernel, n, names), out_shape=[jax....  162 us
    unnamed x38, local copies, waits for them, and re-layouts  4.73 us
    sub x4, other arithmetic, adam_update(): weight - rate * (first_hat / (jnp.sqrt(second_hat) + adam_epsilon) + weig...  3.65 us

profile of v1, /device:TPU:0, one launch (start us, length us, event | category | flops | bytes accessed | tf_op | source)
XLA Modules:
  0.0 173.5 jit_solution(15124078508285618955)
XLA Ops:
  0.6 1.3 copy.63
  1.9 162.3 %fused_layer.1 = (bf16[256,768]{1,0:T(8,128)(2,1)}, f32[256,768]{1,0:T(8,128)}, f32[24,3072]{1,0:T(8,128)}, f32[24,3072]{1,0:T(8,128)}, f32[8,128]{1,0:T(8,128)}, /*index=5*/f32[8,128]{1,0:T(8,128)}) custom-call(bf16[256,768]{1,0:T(8,128)(2,1)} %bitcast.50, bf16[256,768]{1,0:T(8,128)(2,1)} %bitcast.51, f32[24,3072]{1,0:T(8,128)} %bitcast.47, ...), custom_call_target="tpu_custom_call" | custom-call | tf_op jit(solution)/shard_map/fused_layer/pallas_call | solution.py:1198
  164.3 0.0 copy-start.1
  164.3 0.0 copy-start.6
  164.3 0.0 copy-start.7
  164.3 0.0 copy-start.8
  164.3 1.3 slice.9
  166.3 0.0 copy-done
  166.3 0.0 copy-done.4
  166.3 0.0 copy-done.5
  166.3 2.0 %multiply_subtract_fusion.1 = (f32[1,24,3072]{2,1,0:T(8,128)}, f32[1,24,3072]{2,1,0:T(8,128)}, f32[1,24,3072]{2,1,0:T(8,128)}) fusion(f32[1,24,3072]{2,1,0:T(8,128)S(1)} %copy-done, f32[24,3072]{1,0:T(8,128)} %get-tuple-element.24, f32[]{:T(128)S(6)} %div.39, f32[1,24,3072]{2,1,0:T(8,128)S(1)} %copy-done.4, f32[1,24,3072]{2,1,0:T(8,128)S(1)} %copy-done.5), kind=kLoop, calls=%fused_computation.11 | loop fusion | flops 1105920 | bytes 2064388 | tf_op jit(solution)/shard_map/sub | solution.py:49
  168.4 0.0 copy-start.9
  168.4 0.0 copy-start.11
  168.4 0.0 copy-start.12
  168.4 0.0 copy-start.3
  168.4 1.1 multiply_subtract_fusion
  169.5 0.0 copy-done.13
  169.5 0.5 multiply_subtract_fusion.2
  170.1 0.0 copy-done.9
  170.1 0.6 copy.42
  170.7 0.6 copy.43
  171.3 0.6 copy.44
  171.9 0.7 copy.66
  172.6 0.9 copy.67
  (20 shorter events, 0.1 us)
Async XLA Ops:
  1.9 164.4 %copy-start = (f32[1,24,3072]{2,1,0:T(8,128)S(1)}, f32[1,24,3072]{2,1,0:T(8,128)}, u32[]{:S(2)}) copy-start(f32[1,24,3072]{2,1,0:T(8,128)} %param.25) | copy-start | bytes 884740
  1.9 164.4 %copy-start.4 = (f32[1,24,3072]{2,1,0:T(8,128)S(1)}, f32[1,24,3072]{2,1,0:T(8,128)}, u32[]{:S(2)}) copy-start(f32[1,24,3072]{2,1,0:T(8,128)} %param.30) | copy-start | bytes 884740
  1.9 164.4 %copy-start.5 = (f32[1,24,3072]{2,1,0:T(8,128)S(1)}, f32[1,24,3072]{2,1,0:T(8,128)}, u32[]{:S(2)}) copy-start(f32[1,24,3072]{2,1,0:T(8,128)} %param.29) | copy-start | bytes 884740
  164.3 4.1 %copy-start.1 = (f32[1,3072,24]{1,2,0:T(8,128)S(1)}, f32[1,3072,24]{1,2,0:T(8,128)}, u32[]{:S(2)}) copy-start(f32[1,3072,24]{1,2,0:T(8,128)} %param.26) | copy-start | bytes 884740
  164.3 4.1 %copy-start.6 = (f32[1,3072,24]{1,2,0:T(8,128)S(1)}, f32[1,3072,24]{1,2,0:T(8,128)}, u32[]{:S(2)}) copy-start(f32[1,3072,24]{1,2,0:T(8,128)} %param.32) | copy-start | bytes 884740
  164.3 4.1 %copy-start.7 = (f32[1,3072,24]{1,2,0:T(8,128)S(1)}, f32[1,3072,24]{1,2,0:T(8,128)}, u32[]{:S(2)}) copy-start(f32[1,3072,24]{1,2,0:T(8,128)} %param.31) | copy-start | bytes 884740
  164.3 4.1 %copy-start.8 = (f32[24,3072]{1,0:T(8,128)S(1)}, f32[24,3072]{1,0:T(8,128)}, u32[]{:S(2)}) copy-start(f32[24,3072]{1,0:T(8,128)} %get-tuple-element.25) | copy-start | bytes 884740
  168.3 1.2 copy-start.10
  168.3 1.2 copy-start.13
  168.3 1.2 copy-start.14
  168.3 1.2 copy-start.15
  168.4 1.7 copy-start.9
  168.4 1.7 copy-start.11
  168.4 1.7 copy-start.12
  168.4 3.5 %copy-start.3 = (bf16[256,768]{1,0:T(8,128)(2,1)S(1)}, bf16[256,768]{1,0:T(8,128)(2,1)}, u32[]{:S(2)}) copy-start(bf16[256,768]{1,0:T(8,128)(2,1)} %get-tuple-element.21) | copy-start | bytes 1179652
  168.4 4.2 %copy-start.2 = (f32[256,768]{1,0:T(8,128)S(1)}, f32[256,768]{1,0:T(8,128)}, u32[]{:S(2)}) copy-start(f32[256,768]{1,0:T(8,128)} %get-tuple-element.22) | copy-start | bytes 2359300

commit v2 on v1

--- a/solution.py
+++ b/solution.py
@@ -242,8 +242,10 @@
         self.slab = 2 * self.rows
         self.segment = self.zs * self.slab
         self.half = hidden // 2
-        self.chunks = 4
-        self.cols = self.half // self.chunks
+        self.cols = 512
+        self.chunks = self.half // self.cols
+        self.parts = 2
+        self.thin = self.cols // self.parts
         self.packed = width // self.seq
         self.tokens = seqs * block
         self.bias = hidden // self.devices
@@ -256,7 +258,8 @@
             and self.slab % 16 == 0
             and self.packed % 32 == 0
             and self.block % 128 == 0
-            and self.half % (128 * self.chunks) == 0
+            and self.zs == 4
+            and self.half % self.cols == 0
             and self.rows <= 128
             and self.bias <= 128
             and 5 * self.rows <= self.width
@@ -331,6 +334,10 @@
 TABLES = ("tt_f", "by_length", "un_f", "perm", "tt_b", "un_b")
 
 
+FORWARD_TURNS = (0, 1, 1, 1, 0, 1)
+BACK_TURNS = (0, 1, 1, 0, 1, 1, 0, 1, 1, 0, 1, 1)
+
+
 def layer_kernel(n, names, *refs):
     r = types.SimpleNamespace(**dict(zip(names, refs)))
     batch_at, seq_at = lax.axis_index("batch"), lax.axis_index("seq")
@@ -407,29 +414,13 @@
         for m in range(2)
     ]
 
-    tile = r.tile
-    tile[...] = jnp.zeros(tile.shape, F32)
-    tile[0:5, 0 : n.rows] = r.vec[...]
-    tile[5:6, 0 : n.bias] = r.bias[...]
-    small = r.small
-    small_one = [
-        go(
-            remote(
-                tile,
-                small.at[batch_at, seq_at],
-                r.small_send.at[k - 1],
-                r.small_recv.at[k - 1],
-                batch_at,
-                plane(k),
-            )
-        )
-        for k in range(1, n.seq)
-    ]
-    small[batch_at, seq_at] = tile[...]
-
     def mix_start(t, source, table):
         y_ref, l_ref = r.y_buf.at[t], r.l_buf.at[t]
         y_ref[...] = dot(table[...], source, NT).astype(BF16)
+        l_ref[seq_at] = y_ref[rows_of(seq_at, n.packed), :]
+
+    def mix_send(t):
+        y_ref, l_ref = r.y_buf.at[t], r.l_buf.at[t]
         for k in range(1, n.seq):
             go(
                 remote(
@@ -441,7 +432,6 @@
                     plane(k),
                 )
             )
-        l_ref[seq_at] = y_ref[rows_of(seq_at, n.packed), :]
 
     def mix_turn(t):
         l_ref, z_ref, r_ref = r.l_buf.at[t], r.z_buf.at[t], r.r_buf.at[t]
@@ -506,155 +496,184 @@
     mix_start(0, r.x[...], r.tt_f_v)
 
     full = r.full
+    mate_z = z + 1 - 2 * (z % 2)
+    pair_z = z // 2
+    inner = (z > 0) & (z < n.zs - 1)
+
+    def line(to_z):
+        return batch_at, 2 * to_z + y
 
     def seg_rows(sx, sy):
         return rows_of(sy * n.xs + sx, seg)
 
+    def pair_rows(sx, sy, sp):
+        return rows_of((sy * n.xs + sx) * 2 + sp, 2 * slab)
+
     def slab_rows(sx, sy, sz):
         return rows_of((sy * n.xs + sx) * n.zs + sz, slab)
 
-    for m in range(2):
-        r.stage[m, core_rows, :] = weights[m][:, keep]
-        remote(
-            weights[m].at[:, give],
-            r.stage.at[m, pl.ds(aligned(1 - core, n.rows), n.rows)],
-            r.swap_send.at[m],
-            r.swap_recv.at[m],
-            other_core,
-            seq_at,
-        ).wait_recv()
-        for q in range(n.chunks):
-            full[m, q, slab_rows(x, y, z), :] = r.stage[m, :, q * n.cols : (q + 1) * n.cols].astype(
-                BF16
-            )
-
-    def z_copy(m, q, d, source_z):
-        at = slab_rows(x, y, source_z)
+    def peer(t):
+        return (other_y_at, other_x_at)[t == 0]
+
+    other_x_at = (other_x, seq_at)
+    other_y_at = (batch_at, other_y)
+
+    def away(t):
+        return (1 - x, y) if t == 0 else (x, 1 - y)
+
+    def turn_of(c):
+        return FORWARD_TURNS[c]
+
+    def place(c):
+        return c // n.chunks, c % n.chunks
+
+    def stage_weights():
+        for m in range(2):
+            r.stage[m, core_rows, :] = weights[m][:, keep]
+            remote(
+                weights[m].at[:, give],
+                r.stage.at[m, pl.ds(aligned(1 - core, n.rows), n.rows)],
+                r.swap_send.at[m],
+                r.swap_recv.at[m],
+                other_core,
+                seq_at,
+            ).wait_recv()
+            for q in range(n.chunks):
+                full[m, q, slab_rows(x, y, z), :] = r.stage[
+                    m, :, q * n.cols : (q + 1) * n.cols
+                ].astype(BF16)
+
+    def full_copy(c, at, send, recv, to):
+        m, q = place(c)
+        return remote(full.at[m, q, at], full.at[m, q, at], send.at[m, q], recv.at[m, q], *to)
+
+    def rows_at(sx, sy, i):
+        return (slab_rows(sx, sy, z), slab_rows(sx, sy, mate_z), pair_rows(sx, sy, 1 - pair_z))[i]
+
+    def side_copy(c, i, sx, sy, first):
+        t = turn_of(c)
+        recv = r.first_recv.at[i] if first else r.second_recv
+        return full_copy(c, rows_at(sx, sy, i), r.side_send, recv, peer(t if first else 1 - t))
+
+    def to_sides(c, i):
+        side_copy(c, i, x, y, True).start()
+        side_copy(c, i, x, y, False).start()
+
+    def own_to_mate(c):
+        return full_copy(c, rows_at(x, y, 0), r.mate_send, r.mate_recv, line(mate_z))
+
+    def pair_across(c):
+        at = pair_rows(x, y, pair_z)
+        return full_copy(c, at, r.across_send, r.pair_recv, line(n.zs - 1 - z))
+
+    def pair_out(c):
+        return full_copy(c, rows_at(x, y, 2), r.out_send, r.pair_recv, line(mate_z))
+
+    def own_sides(c):
+        to_sides(c, 0)
+
+    def own_line(c):
+        own_to_mate(c).start()
+
+    def mate_in(c):
+        full_copy(c, rows_at(x, y, 1), r.mate_send, r.mate_recv, line(mate_z)).wait_recv()
+
+        @pl.when(inner)
+        def _():
+            pair_across(c).start()
+
+        to_sides(c, 1)
+
+    def pair_in(c):
+        pair_out(c).wait_recv()
+
+        @pl.when(inner)
+        def _():
+            pair_out(c).start()
+
+        to_sides(c, 2)
+
+    def pass_on(c, i):
+        t = turn_of(c)
+        ax, ay = away(t)
+        side_copy(c, i, ax, ay, True).wait_recv()
+        side_copy(c, i, ax, ay, False).start()
+
+    def slabs_of(c, count, recv):
+        return full_copy(c, pl.ds(0, count * slab), r.side_send, recv, other_x_at)
+
+    def weights_here(c):
+        slabs_of(c, 2 * n.zs, r.second_recv).wait_recv()
+
+    def small_tiles():
+        tile = r.tile
+        tile[...] = jnp.zeros(tile.shape, F32)
+        for i in range(5):
+            tile[i : i + 1, 0 : n.rows] = r.vec[i]
+        tile[5:6, 0 : n.bias] = r.bias[...]
+        small[batch_at, seq_at] = tile[...]
+        for k in range(1, n.seq):
+            go(small_copy(k, seq_at))
+
+    def small_copy(k, at):
         return remote(
-            full.at[m, q, at],
-            full.at[m, q, at],
-            r.z_send.at[m, q, d - 1],
-            r.z_recv.at[m, q, d - 1],
-            batch_at,
-            2 * ((z + d) % n.zs) + y,
-        )
-
-    def weights_along_z(q):
-        for m in range(2):
-            for d in range(1, n.zs):
-                go(z_copy(m, q, d, z))
-
-    def turn_of(m, q):
-        return (m + q) % 2
-
-    def peer(t):
-        return (
-            batch_at + (1 - t) * (other_x - batch_at),
-            seq_at + t * (other_y - seq_at),
-        )
-
-    def away(t):
-        return x + (1 - t) * (1 - 2 * x), y + t * (1 - 2 * y)
-
-    def seg_copy(m, q, i, t, sx, sy):
-        at = seg_rows(sx, sy)
-        return remote(
-            full.at[m, q, at],
-            full.at[m, q, at],
-            r.seg_send.at[m, q, i],
-            r.seg_recv.at[m, q, i],
-            *peer(t),
-        )
-
-    def weights_one(q):
-        for m in range(2):
-            t = turn_of(m, q)
-            for d in range(1, n.zs):
-                z_copy(m, q, d, (z + n.zs - d) % n.zs).wait_recv()
-            go(seg_copy(m, q, 0, t, x, y))
-            go(seg_copy(m, q, 1, 1 - t, x, y))
-
-    def weights_two(q):
-        for m in range(2):
-            t = turn_of(m, q)
-            ax, ay = away(t)
-            seg_copy(m, q, 0, t, ax, ay).wait_recv()
-            go(seg_copy(m, q, 2, 1 - t, ax, ay))
-
-    def weights_here(m, q):
-        t = (m + q) % 2
-        bx, by = away(1 - t)
-        seg_copy(m, q, 1, 1 - t, bx, by).wait_recv()
-        seg_copy(m, q, 2, 1 - t, 1 - x, 1 - y).wait_recv()
-
-    weights_along_z(0)
-    weights_along_z(1)
-
-    for k in range(1, n.seq):
-        remote(
-            tile,
-            small.at[batch_at, plane_from(k)],
+            r.tile,
+            small.at[batch_at, at],
             r.small_send.at[k - 1],
             r.small_recv.at[k - 1],
             batch_at,
             plane(k),
-        ).wait_recv()
-    for k in range(1, n.batch):
-        go(
-            remote(
-                small.at[batch_at],
-                small.at[batch_at],
-                r.row_send.at[k - 1],
-                r.row_recv.at[k - 1],
-                across(k),
-                seq_at,
-            )
-        )
-
-    loads.by_length.wait()
-    mix_turn(0)
-    weights_along_z(2)
-    weights_along_z(3)
-    weights_one(0)
-
-    loads.perm.wait()
-    r.x_place[...] = dot(r.x[...], r.perm_v[...])
-    r.dy_place[...] = dot(r.dy[...], r.perm_v[...])
-    for k in range(1, n.batch):
-        remote(
+        )
+
+    def row_copy(k, at):
+        return remote(
             small.at[batch_at],
-            small.at[across_from(k)],
+            small.at[at],
             r.row_send.at[k - 1],
             r.row_recv.at[k - 1],
             across(k),
             seq_at,
-        ).wait_recv()
-    vec_rows = []
-    for i in range(5):
-        held = small[:, :, i, :].reshape(n.devices, 128).astype(BF16)
-        spread = dot(held, r.vec_spread[...]) * r.vec_mask[...]
-        vec_rows.append(jnp.sum(spread, axis=0, keepdims=True))
-    for i in range(5):
-        r.vecs[i : i + 1, :] = vec_rows[i]
+        )
+
+    small = r.small
+
+    def small_rows():
+        for k in range(1, n.seq):
+            small_copy(k, plane_from(k)).wait_recv()
+        for k in range(1, n.batch):
+            go(row_copy(k, batch_at))
+
     half_owners = n.devices // 2
-    held = small[pl.ds(core * (n.batch // 2), n.batch // 2), :, 5, :]
-    held = held.reshape(half_owners, 128).astype(BF16)
     bias_mask = (
         lax.broadcasted_iota(jnp.int32, (half_owners, n.half), 0)
         == lax.broadcasted_iota(jnp.int32, (half_owners, n.half), 1) // n.bias
     )
-    biases = jnp.sum(
-        jnp.where(bias_mask, dot(held, r.bias_spread[...]), 0.0), axis=0, keepdims=True
-    )
-    for q in range(n.chunks):
-        r.biases[q] = biases[:, q * n.cols : (q + 1) * n.cols]
-
-    weights_one(1)
-    weights_two(0)
-    loads.un_f.wait()
-    mix_finish(0, r.un_f_v)
+
+    def small_vectors():
+        for k in range(1, n.batch):
+            row_copy(k, across_from(k)).wait_recv()
+        for i in range(5):
+            held = small[:, :, i, :].reshape(n.devices, 128).astype(BF16)
+            spread = dot(held, r.vec_spread[...]) * r.vec_mask[...]
+            r.vecs[i : i + 1, :] = jnp.sum(spread, axis=0, keepdims=True)
+        held = small[pl.ds(core * (n.batch // 2), n.batch // 2), :, 5, :]
+        held = held.reshape(half_owners, 128).astype(BF16)
+        spread = jnp.where(bias_mask, dot(held, r.bias_spread[...]), 0.0)
+        biases = jnp.sum(spread, axis=0, keepdims=True)
+        for q in range(n.chunks):
+            r.biases[q] = biases[:, q * n.cols : (q + 1) * n.cols]
+
+    def place_inputs():
+        loads.perm.wait()
+        r.x_place[...] = dot(r.x[...], r.perm_v[...])
+        r.dy_place[...] = dot(r.dy[...], r.perm_v[...])
+
+    def turn_forward():
+        loads.by_length.wait()
+        mix_turn(0)
 
     step = 32
+    mine, theirs = pl.ds(0, tokens), pl.ds(tokens, tokens)
 
     def row_loop(body):
         @pl.loop(0, tokens // step)
@@ -675,46 +694,67 @@
         r.h[at, :] = h
         r.h_low[at, :] = h.astype(BF16)
 
-    row_loop(first_norm)
-
-    mine, theirs = pl.ds(0, tokens), pl.ds(tokens, tokens)
-
     def swap(i, src, dst):
-        return remote(
-            src, dst, r.core_send.at[i], r.core_recv.at[i], other_core, seq_at
-        )
-
-    swap_h = go(swap(0, r.h_low.at[mine], r.h_low.at[theirs]))
-    weights_one(2)
-    weights_two(1)
-    weights_one(3)
-    weights_two(2)
-    weights_two(3)
-    swap_h.wait_recv()
-
-    r.total[...] = jnp.zeros(r.total.shape, F32)
+        return remote(src, dst, r.core_send.at[i], r.core_recv.at[i], other_core, seq_at)
+
+    def swap_h():
+        return swap(0, r.h_low.at[mine], r.h_low.at[theirs])
+
+    def norm_forward():
+        loads.un_f.wait()
+        mix_finish(0, r.un_f_v)
+        row_loop(first_norm)
+        go(swap_h())
+
     root = math.sqrt(2.0 / math.pi)
-    part = 128
-
-    @pl.loop(0, n.chunks)
-    def _(q):
-        weights_here(0, q)
-        weights_here(1, q)
-
-        @pl.loop(0, 2 * tokens // part)
+
+    lifted_parts = []
+
+    def lift(q):
+        if not lifted_parts:
+            swap_h().wait_recv()
+        lifted_parts.append(q)
+        weights_here(q)
+        r.lift[...] = dot(r.h_low[...], full[0, q]) + r.biases[q]
+
+        @pl.loop(0, 2 * tokens // step)
         def _(i):
-            at = pl.ds(pl.multiple_of(i * part, part), part)
-            u = dot(r.h_low[at, :], full[0, q]) + r.biases[q]
+            at = pl.ds(pl.multiple_of(i * step, step), step)
+            u = r.lift[at, :]
             square = u * u
-            bent = jnp.tanh(root * u * (1.0 + 0.044715 * square))
-            half_up = 0.5 * (1.0 + bent)
-            act = (u * half_up).astype(BF16)
-            r.slope[q, at, :] = half_up + 0.5 * u * (1.0 - bent * bent) * (
-                root * (1.0 + 3.0 * 0.044715 * square)
+            bent = jnp.tanh(u * (root + (root * 0.044715) * square))
+            half_up = 0.5 + 0.5 * bent
+            r.act[q, at, :] = (u * half_up).astype(BF16)
+            r.slope[q, at, :] = half_up + (u * (1.0 - bent * bent)) * (
+                0.5 * root + (1.5 * root * 0.044715) * square
             )
-            r.act[q, at, :] = act
-            r.total[at, :] = r.total[at, :] + dot(act, full[1, q], NT)
-
+
+    gathered_parts = []
+
+    def drop(q):
+        weights_here(n.chunks + q)
+        part = dot(r.act[q], full[1, q], NT)
+        r.total[...] = r.total[...] + part if gathered_parts else part
+        gathered_parts.append(q)
+
+    def send_forward():
+        mix_send(0)
+
+    forward_steps = (
+        (stage_weights,), (own_line, 1), (small_tiles,), (own_sides, 5), (own_line, 2),
+        (own_line, 4), (own_sides, 2), (own_sides, 1), (own_line, 3), (own_line, 0),
+        (mate_in, 1), (own_line, 5), (pass_on, 5, 0), (own_sides, 0), (mate_in, 2),
+        (own_sides, 4), (pass_on, 2, 0), (pass_on, 1, 0), (mate_in, 4), (mate_in, 0),
+        (send_forward,), (own_sides, 3), (pair_in, 1), (pair_in, 2), (mate_in, 3),
+        (small_rows,), (pass_on, 4, 1), (pair_in, 0), (pair_in, 3), (mate_in, 5),
+        (turn_forward,), (pass_on, 2, 2), (pass_on, 1, 1), (pass_on, 0, 1), (pass_on, 0, 2),
+        (pass_on, 0, 0), (pass_on, 3, 1), (pass_on, 1, 2), (pair_in, 5), (small_vectors,),
+        (pair_in, 4), (pass_on, 5, 1), (place_inputs,), (pass_on, 4, 0), (pass_on, 2, 1),
+        (norm_forward,), (pass_on, 5, 2), (pass_on, 3, 2), (pass_on, 4, 2), (lift, 0),
+        (pass_on, 3, 0), (lift, 1), (lift, 2), (drop, 2), (drop, 1), (drop, 0),
+    )
+    for task, *which in forward_steps:
+        task(*which)
     r.part_low[...] = r.total[theirs, :].astype(BF16)
     swap_ff = go(swap(1, r.part_low, r.part_in))
     swap_ff.wait_recv()
@@ -752,110 +792,123 @@
     swap_dz.wait_recv()
     r.dz_turned[...] = jnp.transpose(r.dz[...])
 
-    acc, out_low, in_one, in_two, in_three = (
-        r.acc,
-        r.give,
-        r.in_one,
-        r.in_two,
-        r.in_three,
-    )
-
-    def first_parts(m, q, t):
-        ax, ay = away(t)
-        return [(j, ax * (1 - t) + j * t, ay * t + j * (1 - t)) for j in range(2)]
-
-    def grad_copy_one(m, q, t, j, sx, sy):
+    acc, out_low = r.acc, r.give
+
+    def wide(c):
+        m, q = c // (n.chunks * n.parts), c % (n.chunks * n.parts)
+        return 1 - m, q // n.parts, pl.ds((q % n.parts) * n.thin, n.thin)
+
+    def grad_copy(c, at, into, i, to):
         return remote(
-            out_low.at[m, q, seg_rows(sx, sy)],
-            in_one.at[m, q, j],
-            r.one_send.at[m, q, j],
-            r.one_recv.at[m, q, j],
-            *peer(t),
-        )
-
-    def grads_one(m, q):
-        t = 1 - (m + q) % 2
-        for j, sx, sy in first_parts(m, q, t):
-            at = seg_rows(sx, sy)
-            out_low[m, q, at, :] = acc[m, q, at, :].astype(BF16)
-            grad_copy_one(m, q, t, j, sx, sy).start()
-
-    def grad_copy_two(m, q, t, sx, sy):
-        return remote(
-            out_low.at[m, q, seg_rows(sx, sy)],
-            in_two.at[m, q],
-            r.two_send.at[m, q],
-            r.two_recv.at[m, q],
-            *peer(t),
-        )
-
-    def grads_two(m, q):
-        t = 1 - (m + q) % 2
-        for j, sx, sy in first_parts(m, q, t):
-            grad_copy_one(m, q, t, j, sx, sy).wait_recv()
-        bx, by = away(1 - t)
-        at = seg_rows(bx, by)
-        away_j = bx * t + by * (1 - t)
-        out_low[m, q, at, :] = (acc[m, q, at, :] + in_one[m, q, away_j].astype(F32)).astype(BF16)
-        grad_copy_two(m, q, 1 - t, bx, by).start()
+            out_low.at[c, at],
+            into.at[c],
+            r.grad_send.at[i, c],
+            r.grad_recv.at[i, c],
+            *to,
+        )
+
+    def back_turn(c):
+        return BACK_TURNS[c]
+
+    def copy_diagonal(c):
+        return grad_copy(c, seg_rows(1 - x, 1 - y), r.in_diagonal, 0, peer(1 - back_turn(c)))
+
+    def copy_near(c):
+        t = 1 - back_turn(c)
+        return grad_copy(c, seg_rows(*away(t)), r.in_near, 1, peer(t))
+
+    def copy_side(c):
+        t = back_turn(c)
+        return grad_copy(c, seg_rows(*away(t)), r.in_side, 2, peer(t))
+
+    def copy_mate(c):
+        return grad_copy(c, slab_rows(x, y, mate_z), r.in_mate, 3, line(mate_z))
+
+    def copy_pair_in(c):
+        return grad_copy(c, pair_rows(x, y, 1 - pair_z), r.in_pair, 4, line(mate_z))
+
+    def copy_pair_across(c):
+        return grad_copy(c, pair_rows(x, y, 1 - pair_z), r.in_across, 5, line(n.zs - 1 - z))
+
+    def round_out(c, at, *more):
+        value = acc[c, at, :]
+        for ref in more:
+            value = value + ref[c].astype(F32)
+        out_low[c, at, :] = value.astype(BF16)
+
+    def grad_product(c):
+        m, q, at = wide(c)
+        if m:
+            acc[c] = dot(r.dz_turned[...], r.act[q, :, at])
+        else:
+            acc[c] = dot(r.h_turned[...], r.dpre[q, :, at])
+        round_out(c, seg_rows(1 - x, 1 - y))
+        copy_diagonal(c).start()
+        round_out(c, seg_rows(*away(1 - back_turn(c))))
+        copy_near(c).start()
+
+    def grad_side(c):
+        copy_diagonal(c).wait_recv()
+        round_out(c, seg_rows(*away(back_turn(c))), r.in_diagonal)
+        copy_side(c).start()
+
+    def grad_line(c):
+        copy_near(c).wait_recv()
+        copy_side(c).wait_recv()
         at = seg_rows(x, y)
-        here_j = x * t + y * (1 - t)
-        acc[m, q, at, :] = acc[m, q, at, :] + in_one[m, q, here_j].astype(F32)
-
-    def grad_copy_three(m, q, d):
-        to_z = (z + d) % n.zs
-        return remote(
-            out_low.at[m, q, slab_rows(x, y, to_z)],
-            in_three.at[m, q, d - 1],
-            r.three_send.at[m, q, d - 1],
-            r.three_recv.at[m, q, d - 1],
-            batch_at,
-            2 * to_z + y,
-        )
-
-    def grads_three(m, q):
-        t = 1 - (m + q) % 2
-        bx, by = away(1 - t)
-        grad_copy_two(m, q, 1 - t, bx, by).wait_recv()
-        at = seg_rows(x, y)
-        acc[m, q, at, :] = acc[m, q, at, :] + in_two[m, q].astype(F32)
-        for d in range(1, n.zs):
-            at = slab_rows(x, y, (z + d) % n.zs)
-            out_low[m, q, at, :] = acc[m, q, at, :].astype(BF16)
-            grad_copy_three(m, q, d).start()
-
-    def grads_four(m, q):
-        at = slab_rows(x, y, z)
-        value = acc[m, q, at, :]
-        for d in range(1, n.zs):
-            grad_copy_three(m, q, d).wait_recv()
-            value = value + in_three[m, q, d - 1].astype(F32)
-        r.final[m, q] = value
-
-    @pl.loop(0, n.chunks)
-    def _(q):
-        acc[1, q] = dot(r.dz_turned[...], r.act[q])
-        grads_one(1, q)
-
-    r.total[...] = jnp.zeros(r.total.shape, F32)
-
-    @pl.loop(0, n.chunks)
-    def _(q):
+        acc[c, at, :] = acc[c, at, :] + (r.in_near[c].astype(F32) + r.in_side[c].astype(F32))
+
+        @pl.when(jnp.logical_not(inner))
+        def _():
+            round_out(c, pair_rows(x, y, 1 - pair_z))
+            copy_pair_in(c).start()
+            round_out(c, slab_rows(x, y, mate_z))
+            copy_mate(c).start()
+
+    def grad_across(c):
+        @pl.when(inner)
+        def _():
+            copy_pair_in(c).wait_recv()
+            round_out(c, pair_rows(x, y, 1 - pair_z), r.in_pair)
+            copy_pair_across(c).start()
+
+    def grad_out(c):
+        @pl.when(inner)
+        def _():
+            copy_pair_across(c).wait_recv()
+            at = pair_rows(x, y, pair_z)
+            acc[c, at, :] = acc[c, at, :] + r.in_across[c].astype(F32)
+            round_out(c, slab_rows(x, y, mate_z))
+            copy_mate(c).start()
+
+    def grad_end(c):
+        m, q, at = wide(c)
+        copy_mate(c).wait_recv()
+        r.final[m, q, :, at] = acc[c, slab_rows(x, y, z), :] + r.in_mate[c].astype(F32)
+
+    back_parts = []
+
+    def slope_back(q):
+        r.lift[...] = dot(r.dz[...], full[1, q])
         r.bias_sum[q] = jnp.zeros((8, n.cols), F32)
 
-        @pl.loop(0, 2 * tokens // part)
+        @pl.loop(0, 2 * tokens // step)
         def _(i):
-            at = pl.ds(pl.multiple_of(i * part, part), part)
-            low = (dot(r.dz[at, :], full[1, q]) * r.slope[q, at, :]).astype(BF16)
+            at = pl.ds(pl.multiple_of(i * step, step), step)
+            low = (r.lift[at, :] * r.slope[q, at, :]).astype(BF16)
             r.dpre[q, at, :] = low
-            r.bias_sum[q] += jnp.sum(low.astype(F32).reshape(part // 8, 8, n.cols), axis=0)
-            r.total[at, :] = r.total[at, :] + dot(low, full[0, q], NT)
-
-    swap_ff.wait_send()
-    started[:] = [copy for copy in started if copy is not swap_ff]
-    r.part_low[...] = r.total[theirs, :].astype(BF16)
-    swap_dh = go(swap(3, r.part_low, r.part_in2))
-    swap_dh.wait_recv()
+            r.bias_sum[q] += jnp.sum(low.astype(F32).reshape(step // 8, 8, n.cols), axis=0)
+
+        part = dot(r.dpre[q], full[0, q], NT)
+        r.total[...] = r.total[...] + part if back_parts else part
+        back_parts.append(q)
+
+    def swap_dh():
+        return swap(3, r.part_low2, r.part_in2)
+
+    def send_dh():
+        r.part_low2[...] = r.total[theirs, :].astype(BF16)
+        go(swap_dh())
 
     def first_norm_back(at):
         dh = r.total[at, :] + r.part_in2[at, :].astype(F32) + r.dr2[at, :]
@@ -868,122 +921,106 @@
         r.dm[at, :] = low
         r.rest[at, :] = (dv - low.astype(F32)).astype(BF16)
 
-    row_loop(first_norm_back)
-    loads.tt_b.wait()
-    mix_start(1, r.dm[...], r.tt_b_v)
-
-    @pl.loop(0, n.chunks)
-    def _(q):
-        acc[0, q] = dot(r.h_turned[...], r.dpre[q])
-        grads_one(0, q)
-
-    for i in range(5):
-        line = jnp.sum(r.sums[i], axis=0, keepdims=True)
-        masked = line * r.vec_mask[...]
-        high = masked.astype(BF16)
-        left = masked - high.astype(F32)
+    def norm_back():
+        swap_dh().wait_recv()
+        row_loop(first_norm_back)
+        loads.tt_b.wait()
+        mix_start(1, r.dm[...], r.tt_b_v)
+        mix_send(1)
+
+    def thirds(v):
+        high = v.astype(BF16)
+        left = v - high.astype(F32)
         mid = left.astype(BF16)
-        low = (left - mid.astype(F32)).astype(BF16)
-        spread = r.vec_spread[...]
-        tiles = dot(high, spread, NT) + dot(mid, spread, NT) + dot(low, spread, NT)
-        r.small_out[:, :, i, :] = tiles.reshape(n.batch, n.seq, 128)
-    line = jnp.concatenate(
-        [jnp.sum(r.bias_sum[q], axis=0, keepdims=True) for q in range(n.chunks)], axis=1
-    )
-    masked = jnp.where(bias_mask, line, 0.0)
-    high = masked.astype(BF16)
-    left = masked - high.astype(F32)
-    mid = left.astype(BF16)
-    low = (left - mid.astype(F32)).astype(BF16)
-    spread = r.bias_spread[...]
-    tiles = dot(high, spread, NT) + dot(mid, spread, NT) + dot(low, spread, NT)
-    r.small_out[:, :, 5, :] = jnp.zeros((n.batch, n.seq, 128), F32)
-    r.small_out[pl.ds(core * (n.batch // 2), n.batch // 2), :, 5, :] = tiles.reshape(
-        n.batch // 2, n.seq, 128
-    )
-    r.small_out[:, :, 6:8, :] = jnp.zeros((n.batch, n.seq, 2, 128), F32)
-    for k in range(1, n.batch):
-        go(
-            remote(
-                r.small_out.at[across(k)],
-                r.small_in.at[k - 1],
-                r.row_send2.at[k - 1],
-                r.row_recv2.at[k - 1],
-                across(k),
-                seq_at,
-            )
-        )
-
-    @pl.loop(0, n.chunks)
-    def _(q):
-        grads_two(1, q)
-
-    mix_turn(1)
-
-    total_small = r.small_out[batch_at]
-    for k in range(1, n.batch):
-        remote(
+        return high, mid, (left - mid.astype(F32)).astype(BF16)
+
+    def small_gather(v, spread):
+        return sum(dot(part, spread, NT) for part in thirds(v))
+
+    def row_sums(k):
+        return remote(
             r.small_out.at[across(k)],
             r.small_in.at[k - 1],
             r.row_send2.at[k - 1],
             r.row_recv2.at[k - 1],
             across(k),
             seq_at,
-        ).wait_recv()
-        total_small = total_small + r.small_in[k - 1]
-    r.small_mid[...] = total_small
-    for k in range(1, n.seq):
-        go(
-            remote(
-                r.small_mid.at[plane(k)],
-                r.small_last.at[k - 1],
-                r.small_send2.at[k - 1],
-                r.small_recv2.at[k - 1],
-                batch_at,
-                plane(k),
-            )
-        )
-
-    @pl.loop(0, n.chunks)
-    def _(q):
-        grads_three(1, q)
-
-    @pl.loop(0, n.chunks)
-    def _(q):
-        grads_two(0, q)
-
-    r.out[...] = dot(r.out_low[...], r.perm_v[...], NT).astype(BF16)
-    r.dx[...] = dot(r.dm[...], r.perm_v[...], NT) + dot(
-        r.rest[...], r.perm_v[...], NT
-    )
-    loads.un_b.wait()
-    mix_finish(1, r.un_b_v)
-    r.dx[...] = r.dx[...] + r.mixed[...]
-
-    value = r.small_mid[seq_at]
-    for k in range(1, n.seq):
-        remote(
+        )
+
+    def tile_sums(k):
+        return remote(
             r.small_mid.at[plane(k)],
             r.small_last.at[k - 1],
             r.small_send2.at[k - 1],
             r.small_recv2.at[k - 1],
             batch_at,
             plane(k),
-        ).wait_recv()
-        value = value + r.small_last[k - 1]
-    r.g_small[...] = value
-
-    @pl.loop(0, n.chunks)
-    def _(q):
-        grads_four(1, q)
-
-    @pl.loop(0, n.chunks)
-    def _(q):
-        grads_three(0, q)
-
-    @pl.loop(0, n.chunks)
-    def _(q):
-        grads_four(0, q)
+        )
+
+    def small_grads():
+        for i in range(5):
+            line_sum = jnp.sum(r.sums[i], axis=0, keepdims=True)
+            tiles = small_gather(line_sum * r.vec_mask[...], r.vec_spread[...])
+            r.small_out[:, :, i, :] = tiles.reshape(n.batch, n.seq, 128)
+        line_sum = jnp.concatenate(
+            [jnp.sum(r.bias_sum[q], axis=0, keepdims=True) for q in range(n.chunks)], axis=1
+        )
+        tiles = small_gather(jnp.where(bias_mask, line_sum, 0.0), r.bias_spread[...])
+        r.small_out[:, :, 5:8, :] = jnp.zeros((n.batch, n.seq, 3, 128), F32)
+        r.small_out[pl.ds(core * (n.batch // 2), n.batch // 2), :, 5, :] = tiles.reshape(
+            n.batch // 2, n.seq, 128
+        )
+        for k in range(1, n.batch):
+            go(row_sums(k))
+
+    def small_rows_back():
+        value = r.small_out[batch_at]
+        for k in range(1, n.batch):
+            row_sums(k).wait_recv()
+            value = value + r.small_in[k - 1]
+        r.small_mid[...] = value
+        for k in range(1, n.seq):
+            go(tile_sums(k))
+
+    def small_end():
+        value = r.small_mid[seq_at]
+        for k in range(1, n.seq):
+            tile_sums(k).wait_recv()
+            value = value + r.small_last[k - 1]
+        r.g_small[...] = value
+
+    def turn_back():
+        mix_turn(1)
+
+    def outputs():
+        r.out[...] = dot(r.out_low[...], r.perm_v[...], NT).astype(BF16)
+        r.dx[...] = dot(r.dm[...], r.perm_v[...], NT) + dot(r.rest[...], r.perm_v[...], NT)
+
+    def mix_back():
+        loads.un_b.wait()
+        mix_finish(1, r.un_b_v)
+        r.dx[...] = r.dx[...] + r.mixed[...]
+
+    for task, *which in (
+        (grad_product, 0), (grad_product, 2), (grad_product, 1), (slope_back, 1),
+        (grad_side, 2), (slope_back, 2), (grad_product, 9), (slope_back, 0), (grad_side, 1),
+        (send_dh,), (grad_line, 2), (grad_product, 4), (norm_back,), (grad_side, 9),
+        (grad_side, 0), (grad_product, 10), (grad_side, 4), (grad_product, 3),
+        (grad_product, 5), (grad_side, 10), (grad_line, 4), (grad_product, 7), (grad_across, 2),
+        (grad_line, 0), (grad_across, 0), (grad_side, 3), (grad_product, 6), (grad_out, 2),
+        (grad_across, 4), (grad_line, 1), (grad_across, 1), (grad_product, 8), (turn_back,),
+        (grad_side, 5), (grad_out, 1), (grad_line, 10), (grad_product, 11), (grad_out, 4),
+        (grad_side, 7), (grad_line, 3), (grad_end, 2), (grad_across, 3), (outputs,),
+        (grad_end, 1), (grad_side, 8), (grad_across, 10), (grad_out, 0), (grad_line, 5),
+        (mix_back,), (grad_line, 9), (grad_side, 11), (grad_across, 9), (grad_line, 7),
+        (grad_side, 6), (grad_across, 5), (grad_end, 4), (grad_out, 10), (small_grads,),
+        (grad_line, 8), (grad_across, 7), (grad_line, 11), (grad_out, 9), (grad_out, 5),
+        (grad_across, 8), (grad_across, 11), (grad_line, 6), (grad_out, 3), (grad_end, 3),
+        (grad_end, 0), (grad_across, 6), (grad_end, 5), (grad_out, 8), (small_rows_back,),
+        (grad_end, 9), (grad_end, 10), (grad_out, 11), (grad_out, 7), (grad_end, 8),
+        (grad_end, 7), (grad_out, 6), (grad_end, 11), (small_end,), (grad_end, 6),
+    ):
+        task(*which)
 
     grads = (r.g1, r.g2)
     for m in range(2):
@@ -1009,7 +1046,7 @@
         v = jnp.sum(v.reshape(v.shape[0] // 8, 8, v.shape[1]), axis=0)
         return sum(v[:, i : i + 128] for i in range(0, v.shape[1], 128))
 
-    squares = squares + value * value
+    squares = squares + r.g_small[...] * r.g_small[...]
     for m in range(2):
         grads[m][:, keep] = r.final_turn[m, core_rows, :]
         back[m].wait_recv()
@@ -1071,21 +1108,32 @@
     for copy in started:
         copy.wait_send()
 
-    @pl.loop(0, n.chunks)
-    def _(q):
-        for m in range(2):
-            t = 1 - (m + q) % 2
-            for j, sx, sy in first_parts(m, q, t):
-                grad_copy_one(m, q, t, j, sx, sy).wait_send()
-            bx, by = away(1 - t)
-            grad_copy_two(m, q, 1 - t, bx, by).wait_send()
-            for d in range(1, n.zs):
-                grad_copy_three(m, q, d).wait_send()
+    for c in range(2 * n.chunks):
+        own_to_mate(c).wait_send()
+        slabs_of(c, 3 * n.zs, r.second_recv).wait_send()
+
+    for c in range(2 * n.chunks * n.parts):
+        for copy in (copy_diagonal(c), copy_near(c), copy_side(c), copy_mate(c)):
+            copy.wait_send()
+
+    @pl.when(inner)
+    def _():
+        for c in range(2 * n.chunks):
+            pair_across(c).wait_send()
+            pair_out(c).wait_send()
+        for c in range(2 * n.chunks * n.parts):
+            copy_pair_across(c).wait_send()
+
+    @pl.when(jnp.logical_not(inner))
+    def _():
+        for c in range(2 * n.chunks * n.parts):
+            copy_pair_in(c).wait_send()
 
 
 def run_layer(n, x, dy, w1, w2, bias, vec):
     tables = host_tables(n)
     tokens, width, cols, q = n.tokens, n.width, n.cols, n.chunks
+    grads = 2 * q * n.parts
     dma = pltpu.SemaphoreType.DMA
     vmem = pltpu.VMEM
     inputs = dict(
@@ -1129,10 +1177,14 @@
         mix_recv=dma((4, n.seq - 1)),
         mixed=vmem((tokens, width), F32),
         full=vmem((2, q, width, cols), BF16),
-        z_send=dma((2, q, n.zs - 1)),
-        z_recv=dma((2, q, n.zs - 1)),
-        seg_send=dma((2, q, 3)),
-        seg_recv=dma((2, q, 3)),
+        mate_send=dma((2, q)),
+        mate_recv=dma((2, q)),
+        across_send=dma((2, q)),
+        out_send=dma((2, q)),
+        pair_recv=dma((2, q)),
+        side_send=dma((2, q)),
+        first_recv=dma((3, 2, q)),
+        second_recv=dma((2, q)),
         x_place=vmem((tokens, width), F32),
         dy_place=vmem((tokens, width), F32),
         vecs=vmem((8, width), F32),
@@ -1145,8 +1197,10 @@
         core_recv=dma((4,)),
         total=vmem((2 * tokens, width), F32),
         act=vmem((q, 2 * tokens, cols), BF16),
+        lift=vmem((2 * tokens, cols), F32),
         slope=vmem((q, 2 * tokens, cols), F32),
         part_low=vmem((tokens, width), BF16),
+        part_low2=vmem((tokens, width), BF16),
         part_in=vmem((tokens, width), BF16),
         part_in2=vmem((tokens, width), BF16),
         sums=vmem((5, 8, width), F32),
@@ -1155,17 +1209,16 @@
         dz=vmem((2 * tokens, width), BF16),
         h_turned=vmem((width, 2 * tokens), BF16),
         dz_turned=vmem((width, 2 * tokens), BF16),
-        acc=vmem((2, q, width, cols), F32),
-        give=vmem((2, q, width, cols), BF16),
-        in_one=vmem((2, q, 2, n.segment, cols), BF16),
-        in_two=vmem((2, q, n.segment, cols), BF16),
-        in_three=vmem((2, q, n.zs - 1, n.slab, cols), BF16),
-        one_send=dma((2, q, 2)),
-        one_recv=dma((2, q, 2)),
-        two_send=dma((2, q)),
-        two_recv=dma((2, q)),
-        three_send=dma((2, q, n.zs - 1)),
-        three_recv=dma((2, q, n.zs - 1)),
+        acc=vmem((grads, width, n.thin), F32),
+        give=vmem((grads, width, n.thin), BF16),
+        in_diagonal=vmem((grads, n.segment, n.thin), BF16),
+        in_near=vmem((grads, n.segment, n.thin), BF16),
+        in_side=vmem((grads, n.segment, n.thin), BF16),
+        in_mate=vmem((grads, n.slab, n.thin), BF16),
+        in_pair=vmem((grads, 2 * n.slab, n.thin), BF16),
+        in_across=vmem((grads, 2 * n.slab, n.thin), BF16),
+        grad_send=dma((6, grads)),
+        grad_recv=dma((6, grads)),
         bias_sum=vmem((q, 8, cols), F32),
         dpre=vmem((q, 2 * tokens, cols), BF16),
         dm=vmem((tokens, width), BF16),
@@ -1209,6 +1262,77 @@
     return types.SimpleNamespace(**dict(zip(outputs, values)))
 
 
+def adam_kernel(n, names, *refs):
+    r = types.SimpleNamespace(**dict(zip(names, refs)))
+    passed = [
+        pltpu.make_async_copy(r.out, r.out_there, r.sem.at[0]),
+        pltpu.make_async_copy(r.dx, r.dx_there, r.sem.at[1]),
+    ]
+    for copy in passed:
+        copy.start()
+    norm_value = r.norm[0:1, 0:1]
+    r.norm_out[...] = norm_value
+    factor = clip_limit / jnp.maximum(norm_value, clip_limit)
+    lanes = n.cols
+
+    def update(gradient, given, made, at, rate):
+        weight, first, second = (ref[at] for ref in given)
+        new = adam_update(weight, factor * gradient, first, second, rate, STEP_COUNT)
+        for ref, value in zip(made, new):
+            ref[at] = value
+
+    weight_in, weight_out = refs[4:7], refs[7:10]
+    made_in, made_out = refs[19:22], refs[22:25]
+
+    @pl.loop(0, n.hidden // lanes)
+    def _(i):
+        at = (slice(None), pl.ds(pl.multiple_of(i * lanes, lanes), lanes))
+        update(r.g1[at], weight_in, made_in, at, rate_matrix)
+        update(r.g2[at], weight_out, made_out, at, rate_matrix)
+
+    update(r.g_small[5:6, 0 : n.bias], refs[10:13], refs[25:28], ..., rate_vector)
+    for i in range(5):
+        update(r.g_small[i : i + 1, 0 : n.rows], refs[13:16], refs[28:31], i, rate_vector)
+    for copy in passed:
+        copy.wait()
+
+
+def run_adam(n, got, given):
+    f32 = functools.partial(jax.ShapeDtypeStruct, dtype=F32)
+    matrix, bias, vec = f32((n.rows, n.hidden)), f32((1, n.bias)), f32((5, 1, n.rows))
+    inputs = dict(g1=got.g1, g2=got.g2, g_small=got.g_small, norm=got.norm)
+    inputs.update({chr(97 + i): array for i, array in enumerate(given)})
+    inputs.update(out=got.out, dx=got.dx)
+    outputs = dict(norm_out=f32((1, 1)))
+    outputs.update({chr(110 + i): matrix for i in range(6)})
+    outputs.update({chr(65 + i): bias for i in range(3)})
+    outputs.update({chr(70 + i): vec for i in range(3)})
+    outputs.update(
+        out_there=jax.ShapeDtypeStruct(got.out.shape, BF16),
+        dx_there=jax.ShapeDtypeStruct(got.dx.shape, F32),
+    )
+    names = tuple(inputs) + tuple(outputs) + ("sem",)
+    in_vmem = pl.BlockSpec(memory_space=pltpu.VMEM)
+    anywhere = pl.BlockSpec(memory_space=pl.ANY)
+    return pl.pallas_call(
+        functools.partial(adam_kernel, n, names),
+        out_shape=list(outputs.values()),
+        in_specs=[in_vmem] * (len(inputs) - 2) + [anywhere] * 2,
+        out_specs=[in_vmem] * (len(outputs) - 2) + [anywhere] * 2,
+        scratch_shapes=[pltpu.SemaphoreType.DMA((2,))],
+        compiler_params=pltpu.CompilerParams(vmem_limit_bytes=32 * 2**20),
+        name="adam",
+    )(*inputs.values())
+
+
+def turned(a):
+    return jnp.swapaxes(a[0], 0, 1)
+
+
+def lined(a):
+    return jnp.transpose(a, (1, 0, 2))
+
+
 def fused_layer(
     n,
     activations,
@@ -1231,36 +1355,25 @@
         activations.reshape(n.tokens, n.width),
         cotangent.reshape(n.tokens, n.width),
         w_in[0],
-        jnp.swapaxes(w_out[0], 0, 1),
+        turned(w_out),
         b_in,
-        vec_params[0],
-    )
-    norm_value = got.norm[0, 0]
-    factor = clip_limit / jnp.maximum(norm_value, clip_limit)
-    grad_w_in = got.g1[None]
-    grad_w_out = jnp.swapaxes(got.g2, 0, 1)[None]
-    grad_b_in = got.g_small[5:6, : n.bias]
-    grad_vec = got.g_small[None, :5, : n.rows]
-    upd_w_in = adam_update(
-        w_in, factor * grad_w_in, first_w_in, second_w_in, rate_matrix, STEP_COUNT
-    )
-    upd_w_out = adam_update(
-        w_out, factor * grad_w_out, first_w_out, second_w_out, rate_matrix, STEP_COUNT
-    )
-    upd_b_in = adam_update(
-        b_in, factor * grad_b_in, first_b_in, second_b_in, rate_vector, STEP_COUNT
-    )
-    upd_vec = adam_update(
-        vec_params, factor * grad_vec, first_vec, second_vec, rate_vector, STEP_COUNT
-    )
+        lined(vec_params),
+    )
+    given = (
+        *(a[0] for a in (w_in, first_w_in, second_w_in)),
+        *(turned(a) for a in (w_out, first_w_out, second_w_out)),
+        *(b_in, first_b_in, second_b_in),
+        *(lined(a) for a in (vec_params, first_vec, second_vec)),
+    )
+    norm_value, *made, out, dx = run_adam(n, got, given)
     return (
-        got.out.reshape(activations.shape),
-        got.dx.reshape(activations.shape),
-        norm_value,
-        *upd_w_in,
-        *upd_w_out,
-        *upd_b_in,
-        *upd_vec,
+        out.reshape(activations.shape),
+        dx.reshape(activations.shape),
+        norm_value.reshape(()),
+        *(a[None] for a in made[:3]),
+        *(jnp.swapaxes(a, 0, 1)[None] for a in made[3:6]),
+        *made[6:9],
+        *(lined(a) for a in made[9:]),
     )
 
 

time: 174 us -> 143 us (0.82)
  Pallas kernels: 162 us -> 136 us
  other arithmetic: 3.65 us -> 0 us
    pallas_call x1, Pallas kernels: 162 us -> 133 us  [run_layer(): pl.pallas_call(functools.partial(layer_kernel, n, names), out_shape=[jax....]
    sub x4 -> x0, other arithmetic: 3.65 us -> none  [adam_update(): weight - rate * (first_hat / (jnp.sqrt(second_hat) + adam_epsilon) + weig...]
    pallas_call x0 -> x1, Pallas kernels: none -> 2.25 us  [run_adam(): pl.pallas_call(functools.partial(adam_kernel, n, names), out_shape=list(o...]
    unnamed x38 -> x36, local copies, waits for them, and re-layouts: 4.73 us -> 5.45 us
where the time goes in v2:
time: 143 us; the launch traced here: 142 us
  Pallas kernels  136 us (95%)
  local copies, waits for them, and re-layouts  5.45 us (4%)
    pallas_call x1, Pallas kernels, run_layer(): pl.pallas_call(functools.partial(layer_kernel, n, names), out_shape=[jax....  133 us
    unnamed x36, local copies, waits for them, and re-layouts  5.45 us

profile of v2, /device:TPU:0, one launch (start us, length us, event | category | flops | bytes accessed | tf_op | source)
XLA Modules:
  0.0 142.2 jit_solution(9465742509950428495)
XLA Ops:
  0.7 0.0 copy-start
  0.7 0.0 copy-start.1
  0.7 0.0 copy-start.4
  0.7 0.0 copy-start.5
  0.7 0.0 copy-start.6
  0.7 0.0 copy-start.7
  0.7 0.0 copy-start.10
  0.7 0.0 copy-start.13
  0.7 0.0 copy-start.14
  0.7 0.0 copy-start.15
  0.8 0.0 copy-start.16
  0.8 0.0 copy-start.17
  0.8 133.4 %fused_layer.1 = (bf16[256,768]{1,0:T(8,128)(2,1)}, f32[256,768]{1,0:T(8,128)}, f32[24,3072]{1,0:T(8,128)}, f32[24,3072]{1,0:T(8,128)}, f32[8,128]{1,0:T(8,128)}, /*index=5*/f32[8,128]{1,0:T(8,128)}) custom-call(bf16[256,768]{1,0:T(8,128)(2,1)} %bitcast.47, bf16[256,768]{1,0:T(8,128)(2,1)} %bitcast.48, f32[24,3072]{1,0:T(8,128)} %bitcast.35, ...), custom_call_target="tpu_custom_call" | custom-call | tf_op jit(solution)/shard_map/fused_layer/pallas_call | solution.py:1251
  134.2 0.0 copy-done
  134.2 0.0 copy-done.1
  134.2 0.0 copy-done.4
  134.3 0.0 copy-done.5
  134.4 1.1 copy-done.2
  135.5 1.0 copy-done.3
  136.5 1.0 copy-done.8
  137.4 1.0 copy-done.9
  138.4 0.7 copy-done.11
  139.1 0.7 copy-done.12
  139.8 2.2 %adam.1 = (f32[1,1]{1,0:T(1,128)}, f32[24,3072]{1,0:T(8,128)}, f32[24,3072]{1,0:T(8,128)}, f32[24,3072]{1,0:T(8,128)}, f32[24,3072]{1,0:T(8,128)}, /*index=5*/f3...) custom-call(f32[24,3072]{1,0:T(8,128)S(1)} %copy-done.8, ...), custom_call_target="tpu_custom_call" | custom-call | tf_op jit(solution)/shard_map/adam/pallas_call | solution.py:1317
  (14 shorter events, 0.0 us)
Async XLA Ops:
  0.7 133.6 %copy-start = (f32[1,24,3072]{2,1,0:T(8,128)S(1)}, f32[1,24,3072]{2,1,0:T(8,128)}, u32[]{:S(2)}) copy-start(f32[1,24,3072]{2,1,0:T(8,128)} %param.25) | copy-start | bytes 884740
  0.7 133.6 %copy-start.1 = (f32[1,3072,24]{1,2,0:T(8,128)S(1)}, f32[1,3072,24]{1,2,0:T(8,128)}, u32[]{:S(2)}) copy-start(f32[1,3072,24]{1,2,0:T(8,128)} %param.26) | copy-start | bytes 884740
  0.7 133.6 %copy-start.4 = (f32[1,24,3072]{2,1,0:T(8,128)S(1)}, f32[1,24,3072]{2,1,0:T(8,128)}, u32[]{:S(2)}) copy-start(f32[1,24,3072]{2,1,0:T(8,128)} %param.29) | copy-start | bytes 884740
  0.7 133.6 %copy-start.5 = (f32[1,24,3072]{2,1,0:T(8,128)S(1)}, f32[1,24,3072]{2,1,0:T(8,128)}, u32[]{:S(2)}) copy-start(f32[1,24,3072]{2,1,0:T(8,128)} %param.30) | copy-start | bytes 884740
  0.7 133.6 %copy-start.6 = (f32[1,3072,24]{1,2,0:T(8,128)S(1)}, f32[1,3072,24]{1,2,0:T(8,128)}, u32[]{:S(2)}) copy-start(f32[1,3072,24]{1,2,0:T(8,128)} %param.31) | copy-start | bytes 884740
  0.7 133.6 %copy-start.7 = (f32[1,3072,24]{1,2,0:T(8,128)S(1)}, f32[1,3072,24]{1,2,0:T(8,128)}, u32[]{:S(2)}) copy-start(f32[1,3072,24]{1,2,0:T(8,128)} %param.32) | copy-start | bytes 884740
  0.7 133.6 %copy-start.10 = (f32[1,5,24]{2,0,1:T(1,128)S(1)}, f32[1,5,24]{2,0,1:T(1,128)}, u32[]{:S(2)}) copy-start(f32[1,5,24]{2,0,1:T(1,128)} %param.28) | copy-start | bytes 1444
  0.7 133.6 %copy-start.13 = (f32[1,5,24]{2,0,1:T(1,128)S(1)}, f32[1,5,24]{2,0,1:T(1,128)}, u32[]{:S(2)}) copy-start(f32[1,5,24]{2,0,1:T(1,128)} %param.35) | copy-start | bytes 1444
  0.7 133.6 %copy-start.14 = (f32[1,5,24]{2,0,1:T(1,128)S(1)}, f32[1,5,24]{2,0,1:T(1,128)}, u32[]{:S(2)}) copy-start(f32[1,5,24]{2,0,1:T(1,128)} %param.36) | copy-start | bytes 1444
  0.7 133.6 %copy-start.15 = (f32[1,96]{1,0:T(1,128)S(1)}, f32[1,96]{1,0:T(1,128)}, u32[]{:S(2)}) copy-start(f32[1,96]{1,0:T(1,128)} %refs_10_.2) | copy-start | bytes 1156
  0.8 133.6 %copy-start.16 = (f32[1,96]{1,0:T(1,128)S(1)}, f32[1,96]{1,0:T(1,128)}, u32[]{:S(2)}) copy-start(f32[1,96]{1,0:T(1,128)} %refs_11_.2) | copy-start | bytes 1156
  0.8 133.6 %copy-start.17 = (f32[1,96]{1,0:T(1,128)S(1)}, f32[1,96]{1,0:T(1,128)}, u32[]{:S(2)}) copy-start(f32[1,96]{1,0:T(1,128)} %refs_12_.2) | copy-start | bytes 1156
  134.3 1.1 copy-start.2
  135.5 1.0 copy-start.3
  136.5 1.0 copy-start.8
  137.4 1.0 copy-start.9
  138.4 0.7 copy-start.11
  139.1 0.7 copy-start.12

commit v3 on v2

--- a/solution.py
+++ b/solution.py
@@ -331,11 +331,24 @@
     )
 
 
-TABLES = ("tt_f", "by_length", "un_f", "perm", "tt_b", "un_b")
-
-
-FORWARD_TURNS = (0, 1, 1, 1, 0, 1)
-BACK_TURNS = (0, 1, 1, 0, 1, 1, 0, 1, 1, 0, 1, 1)
+LOADS = dict(
+    w1="w1_v",
+    w2="w2_v",
+    x="x_v",
+    tt_f="tt_v",
+    dy="dy_v",
+    vec_spread="vec_spread_v",
+    bias_spread="bias_spread_v",
+    vec_mask="vec_mask_v",
+    by_length="by_length_v",
+    perm="perm_v",
+    un_f="un_v",
+    tt_b="tt_v",
+    un_b="un_v",
+)
+LATER = ("tt_b", "un_b")
+FORWARD_KINDS = (1, 2, 1, 3, 1, 0)
+BACK_KINDS = (1, 1, 4, 3, 5, 4, 3, 0, 0, 0, 3, 4)
 
 
 def layer_kernel(n, names, *refs):
@@ -384,22 +397,28 @@
         return (batch_at + n.batch - k) % n.batch
 
     loads = types.SimpleNamespace()
-    for i, name in enumerate(TABLES):
-        load = pltpu.make_async_copy(getattr(r, name), getattr(r, name + "_v"), r.load_sem.at[i])
+    for i, (name, held) in enumerate(LOADS.items()):
+        load = pltpu.make_async_copy(getattr(r, name), getattr(r, held), r.load_sem.at[i])
         setattr(loads, name, load)
-        load.start()
-
+        if name not in LATER:
+            load.start()
+
+    everyone = [
+        ((batch_at + i // n.seq) % n.batch, (seq_at + i % n.seq) % n.seq)
+        for i in range(1, n.devices)
+    ]
     barrier = pltpu.get_barrier_semaphore()
-    for k in range(1, n.seq):
-        pl.semaphore_signal(barrier, inc=1, device_id=(batch_at, plane(k)), device_id_type=MESH)
-    for k in range(1, n.batch):
-        pl.semaphore_signal(barrier, inc=1, device_id=(across(k), seq_at), device_id_type=MESH)
-    pl.semaphore_wait(barrier, n.seq + n.batch - 2)
-
-    weights = (r.w1, r.w2)
+    for device in everyone:
+        pl.semaphore_signal(barrier, inc=1, device_id=device, device_id_type=MESH)
+    pl.semaphore_wait(barrier, n.devices - 1)
+
+    loads.w1.wait()
+    loads.w2.wait()
+    weights = (r.w1_v, r.w2_v)
     give = pl.ds(aligned(1 - core, n.half), n.half)
     keep = pl.ds(aligned(core, n.half), n.half)
     core_rows = pl.ds(aligned(core, n.rows), n.rows)
+    their_rows = pl.ds(aligned(1 - core, n.rows), n.rows)
     swaps = [
         go(
             remote(
@@ -457,11 +476,13 @@
         inner = lax.broadcasted_iota(jnp.int32, (n.seqs * n.packed, 1), 0) % n.packed
         first = (inner < n.packed // 2) | ((inner == n.packed // 2) & (seq_at == 0))
         scale = 1.0 / math.sqrt(n.length * n.width)
-        for e in range(n.seq):
-            at = slice(e * n.block, (e + 1) * n.block)
+        for e in range(0, n.seq, 2):
+            at = slice(e * n.block, (e + 2) * n.block)
             by_cos = dot(r.left[...], r.by_length_v[0, :, at])
             by_sin = dot(r.left[...], r.by_length_v[1, :, at])
-            z_ref[e] = (jnp.where(first, by_cos, by_sin) * scale).astype(BF16)
+            value = (jnp.where(first, by_cos, by_sin) * scale).astype(BF16)
+            z_ref[e] = value[:, : n.block]
+            z_ref[e + 1] = value[:, n.block :]
         for k in range(1, n.seq):
             go(
                 remote(
@@ -493,7 +514,8 @@
         r.mixed[...] = dot(jnp.concatenate(parts, axis=1), table[...], TN)
 
     loads.tt_f.wait()
-    mix_start(0, r.x[...], r.tt_f_v)
+    loads.x.wait()
+    mix_start(0, r.x_v[...], r.tt_v)
 
     full = r.full
     mate_z = z + 1 - 2 * (z % 2)
@@ -522,7 +544,10 @@
         return (1 - x, y) if t == 0 else (x, 1 - y)
 
     def turn_of(c):
-        return FORWARD_TURNS[c]
+        return FORWARD_KINDS[c] % 2
+
+    def split(c):
+        return FORWARD_KINDS[c] // 2 == 1
 
     def place(c):
         return c // n.chunks, c % n.chunks
@@ -532,7 +557,7 @@
             r.stage[m, core_rows, :] = weights[m][:, keep]
             remote(
                 weights[m].at[:, give],
-                r.stage.at[m, pl.ds(aligned(1 - core, n.rows), n.rows)],
+                r.stage.at[m, their_rows],
                 r.swap_send.at[m],
                 r.swap_recv.at[m],
                 other_core,
@@ -556,47 +581,66 @@
         return full_copy(c, rows_at(sx, sy, i), r.side_send, recv, peer(t if first else 1 - t))
 
     def to_sides(c, i):
-        side_copy(c, i, x, y, True).start()
+        if i == 0 or not split(c):
+            side_copy(c, i, x, y, True).start()
         side_copy(c, i, x, y, False).start()
 
-    def own_to_mate(c):
-        return full_copy(c, rows_at(x, y, 0), r.mate_send, r.mate_recv, line(mate_z))
-
-    def pair_across(c):
-        at = pair_rows(x, y, pair_z)
-        return full_copy(c, at, r.across_send, r.pair_recv, line(n.zs - 1 - z))
-
-    def pair_out(c):
-        return full_copy(c, rows_at(x, y, 2), r.out_send, r.pair_recv, line(mate_z))
+    def line_seg(c, far):
+        return away(turn_of(c)) if far else (x, y)
+
+    def own_to_mate(c, far):
+        at = rows_at(*line_seg(c, far), 0)
+        return full_copy(c, at, r.mate_send.at[far], r.mate_recv.at[far], line(mate_z))
+
+    def mate_arrives(c, far):
+        at = rows_at(*line_seg(c, far), 1)
+        full_copy(c, at, r.mate_send.at[far], r.mate_recv.at[far], line(mate_z)).wait_recv()
+
+    def pair_across(c, far):
+        at = pair_rows(*line_seg(c, far), pair_z)
+        return full_copy(c, at, r.across_send.at[far], r.pair_recv.at[far], line(n.zs - 1 - z))
+
+    def pair_out(c, far):
+        at = rows_at(*line_seg(c, far), 2)
+        return full_copy(c, at, r.out_send.at[far], r.pair_recv.at[far], line(mate_z))
 
     def own_sides(c):
         to_sides(c, 0)
 
     def own_line(c):
-        own_to_mate(c).start()
-
-    def mate_in(c):
-        full_copy(c, rows_at(x, y, 1), r.mate_send, r.mate_recv, line(mate_z)).wait_recv()
+        own_to_mate(c, 0).start()
+
+    def from_mate(c, far):
+        mate_arrives(c, far)
 
         @pl.when(inner)
         def _():
-            pair_across(c).start()
-
-        to_sides(c, 1)
-
-    def pair_in(c):
-        pair_out(c).wait_recv()
+            pair_across(c, far).start()
+
+    def from_pair(c, far):
+        pair_out(c, far).wait_recv()
 
         @pl.when(inner)
         def _():
-            pair_out(c).start()
-
+            pair_out(c, far).start()
+
+    def mate_in(c):
+        from_mate(c, 0)
+        to_sides(c, 1)
+
+    def pair_in(c):
+        from_pair(c, 0)
         to_sides(c, 2)
 
     def pass_on(c, i):
-        t = turn_of(c)
-        ax, ay = away(t)
-        side_copy(c, i, ax, ay, True).wait_recv()
+        ax, ay = away(turn_of(c))
+        if i == 0 or not split(c):
+            side_copy(c, i, ax, ay, True).wait_recv()
+        if split(c):
+            if i == 0:
+                own_to_mate(c, 1).start()
+            else:
+                (from_mate, from_pair)[i - 1](c, 1)
         side_copy(c, i, ax, ay, False).start()
 
     def slabs_of(c, count, recv):
@@ -652,33 +696,37 @@
     def small_vectors():
         for k in range(1, n.batch):
             row_copy(k, across_from(k)).wait_recv()
+        for load in (loads.vec_spread, loads.bias_spread, loads.vec_mask):
+            load.wait()
         for i in range(5):
             held = small[:, :, i, :].reshape(n.devices, 128).astype(BF16)
-            spread = dot(held, r.vec_spread[...]) * r.vec_mask[...]
+            spread = dot(held, r.vec_spread_v[...]) * r.vec_mask_v[...]
             r.vecs[i : i + 1, :] = jnp.sum(spread, axis=0, keepdims=True)
         held = small[pl.ds(core * (n.batch // 2), n.batch // 2), :, 5, :]
         held = held.reshape(half_owners, 128).astype(BF16)
-        spread = jnp.where(bias_mask, dot(held, r.bias_spread[...]), 0.0)
+        spread = jnp.where(bias_mask, dot(held, r.bias_spread_v[...]), 0.0)
         biases = jnp.sum(spread, axis=0, keepdims=True)
         for q in range(n.chunks):
             r.biases[q] = biases[:, q * n.cols : (q + 1) * n.cols]
 
     def place_inputs():
         loads.perm.wait()
-        r.x_place[...] = dot(r.x[...], r.perm_v[...])
-        r.dy_place[...] = dot(r.dy[...], r.perm_v[...])
+        loads.dy.wait()
+        r.x_place[...] = dot(r.x_v[...], r.perm_v[...])
+        r.dy_place[...] = dot(r.dy_v[...], r.perm_v[...])
 
     def turn_forward():
         loads.by_length.wait()
         mix_turn(0)
 
     step = 32
+    tall = 64
     mine, theirs = pl.ds(0, tokens), pl.ds(tokens, tokens)
 
     def row_loop(body):
-        @pl.loop(0, tokens // step)
+        @pl.loop(0, tokens // tall, unroll=True)
         def _(i):
-            body(pl.ds(pl.multiple_of(i * step, step), step))
+            body(pl.ds(pl.multiple_of(i * tall, tall), tall))
 
     def mean(v):
         return jnp.mean(v, axis=-1, keepdims=True)
@@ -690,7 +738,7 @@
         unit = centred * scale
         h = unit * r.vecs[0:1, :] + r.vecs[1:2, :]
         r.unit1[at, :] = unit
-        r.scale1[at, :] = jnp.broadcast_to(scale, (step, 128))
+        r.scale1[at, :] = jnp.broadcast_to(scale, (tall, 128))
         r.h[at, :] = h
         r.h_low[at, :] = h.astype(BF16)
 
@@ -702,7 +750,9 @@
 
     def norm_forward():
         loads.un_f.wait()
-        mix_finish(0, r.un_f_v)
+        mix_finish(0, r.un_v)
+        loads.tt_b.start()
+        loads.un_b.start()
         row_loop(first_norm)
         go(swap_h())
 
@@ -731,38 +781,40 @@
 
     gathered_parts = []
 
+    def swap_ff():
+        return swap(1, r.part_low, r.part_in)
+
     def drop(q):
         weights_here(n.chunks + q)
-        part = dot(r.act[q], full[1, q], NT)
-        r.total[...] = r.total[...] + part if gathered_parts else part
         gathered_parts.append(q)
+        for half in (theirs, mine):
+            part = dot(r.act[q, half, :], full[1, q], NT)
+            part = r.total[half, :] + part if len(gathered_parts) > 1 else part
+            if len(gathered_parts) == n.chunks and half is theirs:
+                r.part_low[...] = part.astype(BF16)
+                go(swap_ff())
+            else:
+                r.total[half, :] = part
 
     def send_forward():
         mix_send(0)
 
     forward_steps = (
-        (stage_weights,), (own_line, 1), (small_tiles,), (own_sides, 5), (own_line, 2),
-        (own_line, 4), (own_sides, 2), (own_sides, 1), (own_line, 3), (own_line, 0),
-        (mate_in, 1), (own_line, 5), (pass_on, 5, 0), (own_sides, 0), (mate_in, 2),
-        (own_sides, 4), (pass_on, 2, 0), (pass_on, 1, 0), (mate_in, 4), (mate_in, 0),
-        (send_forward,), (own_sides, 3), (pair_in, 1), (pair_in, 2), (mate_in, 3),
-        (small_rows,), (pass_on, 4, 1), (pair_in, 0), (pair_in, 3), (mate_in, 5),
-        (turn_forward,), (pass_on, 2, 2), (pass_on, 1, 1), (pass_on, 0, 1), (pass_on, 0, 2),
-        (pass_on, 0, 0), (pass_on, 3, 1), (pass_on, 1, 2), (pair_in, 5), (small_vectors,),
-        (pair_in, 4), (pass_on, 5, 1), (place_inputs,), (pass_on, 4, 0), (pass_on, 2, 1),
-        (norm_forward,), (pass_on, 5, 2), (pass_on, 3, 2), (pass_on, 4, 2), (lift, 0),
-        (pass_on, 3, 0), (lift, 1), (lift, 2), (drop, 2), (drop, 1), (drop, 0),
+        (send_forward,), (stage_weights,), (own_line, 2), (own_line, 0), (own_line, 5),
+        (own_sides, 4), (place_inputs,), (small_tiles,), (own_sides, 3), (own_sides, 2),
+        (own_line, 4), (own_sides, 5), (mate_in, 2), (pass_on, 4, 0), (own_sides, 0),
+        (mate_in, 5), (pass_on, 5, 0), (pass_on, 3, 0), (own_line, 1), (own_sides, 1),
+        (mate_in, 0), (pass_on, 2, 0), (pass_on, 2, 1), (mate_in, 4), (pair_in, 2),
+        (pass_on, 5, 1), (pass_on, 0, 0), (pass_on, 3, 1), (pass_on, 1, 0), (turn_forward,),
+        (pair_in, 0), (small_rows,), (pair_in, 5), (pass_on, 2, 2), (pair_in, 4),
+        (pass_on, 3, 2), (pass_on, 0, 1), (pass_on, 4, 1), (small_vectors,), (pass_on, 1, 1),
+        (pass_on, 0, 2), (own_line, 3), (pass_on, 5, 2), (mate_in, 1), (norm_forward,),
+        (mate_in, 3), (pass_on, 1, 2), (pass_on, 4, 2), (pair_in, 1), (lift, 2), (pair_in, 3),
+        (lift, 0), (lift, 1), (drop, 2), (drop, 1), (drop, 0),
     )
     for task, *which in forward_steps:
         task(*which)
-    r.part_low[...] = r.total[theirs, :].astype(BF16)
-    swap_ff = go(swap(1, r.part_low, r.part_in))
-    swap_ff.wait_recv()
-
-    r.sums[...] = jnp.zeros(r.sums.shape, F32)
-
-    def fold(v):
-        return jnp.sum(v.reshape(step // 8, 8, width), axis=0)
+    swap_ff().wait_recv()
 
     def second_norm(at):
         v = (
@@ -775,22 +827,16 @@
         scale = lax.rsqrt(mean(centred * centred) + norm_epsilon)
         unit = centred * scale
         gain = r.vecs[3:4, :]
+        r.h[at, :] = unit
         r.out_low[at, :] = (unit * gain + r.vecs[4:5, :]).astype(BF16)
-        dy = r.dy_place[at, :]
-        r.sums[3] += fold(dy * unit)
-        r.sums[4] += fold(dy)
-        du = dy * gain
+        du = r.dy_place[at, :] * gain
         dv = scale * (du - mean(du) - unit * mean(du * unit))
         r.dr2[at, :] = dv
-        low = dv.astype(BF16)
-        r.dz[at, :] = low
-        r.sums[2] += fold(low.astype(F32))
+        r.dz[at, :] = dv.astype(BF16)
 
     row_loop(second_norm)
     swap_dz = go(swap(2, r.dz.at[mine], r.dz.at[theirs]))
-    r.h_turned[...] = jnp.transpose(r.h_low[...])
     swap_dz.wait_recv()
-    r.dz_turned[...] = jnp.transpose(r.dz[...])
 
     acc, out_low = r.acc, r.give
 
@@ -798,17 +844,23 @@
         m, q = c // (n.chunks * n.parts), c % (n.chunks * n.parts)
         return 1 - m, q // n.parts, pl.ds((q % n.parts) * n.thin, n.thin)
 
-    def grad_copy(c, at, into, i, to):
+    def grad_copy(c, at, into, i, to, slot=None):
         return remote(
             out_low.at[c, at],
-            into.at[c],
+            into.at[c if slot is None else slot],
             r.grad_send.at[i, c],
             r.grad_recv.at[i, c],
             *to,
         )
 
     def back_turn(c):
-        return BACK_TURNS[c]
+        return BACK_KINDS[c] % 2
+
+    def back_mode(c):
+        return BACK_KINDS[c] // 2
+
+    def back_slot(c):
+        return [d for d, kind in enumerate(BACK_KINDS) if kind // 2 == back_mode(c)].index(c)
 
     def copy_diagonal(c):
         return grad_copy(c, seg_rows(1 - x, 1 - y), r.in_diagonal, 0, peer(1 - back_turn(c)))
@@ -821,70 +873,162 @@
         t = back_turn(c)
         return grad_copy(c, seg_rows(*away(t)), r.in_side, 2, peer(t))
 
-    def copy_mate(c):
-        return grad_copy(c, slab_rows(x, y, mate_z), r.in_mate, 3, line(mate_z))
-
-    def copy_pair_in(c):
-        return grad_copy(c, pair_rows(x, y, 1 - pair_z), r.in_pair, 4, line(mate_z))
-
-    def copy_pair_across(c):
-        return grad_copy(c, pair_rows(x, y, 1 - pair_z), r.in_across, 5, line(n.zs - 1 - z))
+    def back_seg(c, far):
+        return away(back_turn(c)) if far else (x, y)
+
+    def line_into(c, far, i):
+        if far:
+            return (r.far_mate, r.far_pair, r.far_across)[i].at[back_slot(c)]
+        return (r.in_mate, r.in_pair, r.in_across)[i].at[c]
+
+    def line_copy(c, at, far, i, to):
+        return remote(
+            out_low.at[c, at],
+            line_into(c, far, i),
+            r.grad_send.at[3 + 3 * far + i, c],
+            r.grad_recv.at[3 + 3 * far + i, c],
+            *to,
+        )
+
+    def copy_mate(c, far):
+        at = slab_rows(*back_seg(c, far), mate_z)
+        return line_copy(c, at, far, 0, line(mate_z))
+
+    def copy_pair_in(c, far):
+        at = pair_rows(*back_seg(c, far), 1 - pair_z)
+        return line_copy(c, at, far, 1, line(mate_z))
+
+    def copy_pair_across(c, far):
+        at = pair_rows(*back_seg(c, far), 1 - pair_z)
+        return line_copy(c, at, far, 2, line(n.zs - 1 - z))
+
+    def copy_far(c):
+        t = back_turn(c)
+        return grad_copy(c, slab_rows(*away(t), z), r.in_far, 2, peer(t), back_slot(c))
+
+    def copy_direct(c, d):
+        to_z = (z + d) % n.zs
+        into = r.in_direct.at[d - 1]
+        return grad_copy(c, slab_rows(x, y, to_z), into, 8 + d, line(to_z), back_slot(c))
 
     def round_out(c, at, *more):
         value = acc[c, at, :]
         for ref in more:
-            value = value + ref[c].astype(F32)
+            value = value + ref[...].astype(F32)
         out_low[c, at, :] = value.astype(BF16)
 
     def grad_product(c):
         m, q, at = wide(c)
         if m:
-            acc[c] = dot(r.dz_turned[...], r.act[q, :, at])
+            acc[c] = dot(r.dz[...], r.act[q, :, at], TN)
         else:
-            acc[c] = dot(r.h_turned[...], r.dpre[q, :, at])
+            acc[c] = dot(r.h_low[...], r.dpre[q, :, at], TN)
         round_out(c, seg_rows(1 - x, 1 - y))
         copy_diagonal(c).start()
         round_out(c, seg_rows(*away(1 - back_turn(c))))
         copy_near(c).start()
 
+    def line_start(c, far):
+        @pl.when(jnp.logical_not(inner))
+        def _():
+            sx, sy = back_seg(c, far)
+            round_out(c, pair_rows(sx, sy, 1 - pair_z))
+            copy_pair_in(c, far).start()
+            round_out(c, slab_rows(sx, sy, mate_z))
+            copy_mate(c, far).start()
+
     def grad_side(c):
         copy_diagonal(c).wait_recv()
-        round_out(c, seg_rows(*away(back_turn(c))), r.in_diagonal)
-        copy_side(c).start()
+        at = seg_rows(*away(back_turn(c)))
+        if back_mode(c) == 1:
+            acc[c, at, :] = acc[c, at, :] + r.in_diagonal[c].astype(F32)
+            line_start(c, 1)
+        else:
+            round_out(c, at, r.in_diagonal.at[c])
+            copy_side(c).start()
 
     def grad_line(c):
         copy_near(c).wait_recv()
-        copy_side(c).wait_recv()
+        more = r.in_near[c].astype(F32)
+        if back_mode(c) != 1:
+            copy_side(c).wait_recv()
+            more = more + r.in_side[c].astype(F32)
         at = seg_rows(x, y)
-        acc[c, at, :] = acc[c, at, :] + (r.in_near[c].astype(F32) + r.in_side[c].astype(F32))
-
-        @pl.when(jnp.logical_not(inner))
-        def _():
-            round_out(c, pair_rows(x, y, 1 - pair_z))
-            copy_pair_in(c).start()
-            round_out(c, slab_rows(x, y, mate_z))
-            copy_mate(c).start()
+        acc[c, at, :] = acc[c, at, :] + more
+        if back_mode(c) == 2:
+            for d in range(1, n.zs):
+                round_out(c, slab_rows(x, y, (z + d) % n.zs))
+                copy_direct(c, d).start()
+        else:
+            line_start(c, 0)
+
+    def fars(c):
+        return range((1, 2, 0)[back_mode(c)])
 
     def grad_across(c):
-        @pl.when(inner)
-        def _():
-            copy_pair_in(c).wait_recv()
-            round_out(c, pair_rows(x, y, 1 - pair_z), r.in_pair)
-            copy_pair_across(c).start()
+        for far in fars(c):
+
+            @pl.when(inner)
+            def _(far=far):
+                copy_pair_in(c, far).wait_recv()
+                at = pair_rows(*back_seg(c, far), 1 - pair_z)
+                round_out(c, at, line_into(c, far, 1))
+                copy_pair_across(c, far).start()
 
     def grad_out(c):
-        @pl.when(inner)
-        def _():
-            copy_pair_across(c).wait_recv()
-            at = pair_rows(x, y, pair_z)
-            acc[c, at, :] = acc[c, at, :] + r.in_across[c].astype(F32)
-            round_out(c, slab_rows(x, y, mate_z))
-            copy_mate(c).start()
+        for far in fars(c):
+
+            @pl.when(inner)
+            def _(far=far):
+                copy_pair_across(c, far).wait_recv()
+                sx, sy = back_seg(c, far)
+                at = pair_rows(sx, sy, pair_z)
+                acc[c, at, :] = acc[c, at, :] + line_into(c, far, 2)[...].astype(F32)
+                round_out(c, slab_rows(sx, sy, mate_z))
+                copy_mate(c, far).start()
+
+    def grad_far(c):
+        if back_mode(c) == 1:
+            copy_mate(c, 1).wait_recv()
+            round_out(c, slab_rows(*away(back_turn(c)), z), line_into(c, 1, 0))
+            copy_far(c).start()
+
+    grads_out = (r.g1, r.g2)
+    r.squares[...] = jnp.zeros((8, 128), F32)
+
+    def squares_of(v):
+        v = v * v
+        v = jnp.sum(v.reshape(v.shape[0] // 8, 8, v.shape[1]), axis=0)
+        return sum(v[:, i : i + 128] for i in range(0, v.shape[1], 128))
+
+    def copy_back(c):
+        return remote(
+            r.final.at[c, their_rows],
+            r.final_in.at[c],
+            r.back_send.at[c],
+            r.back_recv.at[c],
+            other_core,
+            seq_at,
+        )
 
     def grad_end(c):
         m, q, at = wide(c)
-        copy_mate(c).wait_recv()
-        r.final[m, q, :, at] = acc[c, slab_rows(x, y, z), :] + r.in_mate[c].astype(F32)
+        value = acc[c, slab_rows(x, y, z), :]
+        if back_mode(c) == 2:
+            for d in range(1, n.zs):
+                copy_direct(c, d).wait_recv()
+                value = value + r.in_direct[d - 1, back_slot(c)].astype(F32)
+        else:
+            copy_mate(c, 0).wait_recv()
+            value = value + r.in_mate[c].astype(F32)
+        if back_mode(c) == 1:
+            copy_far(c).wait_recv()
+            value = value + r.in_far[back_slot(c)].astype(F32)
+        r.squares[...] += squares_of(value)
+        r.final[c] = value
+        own_at = pl.ds(aligned(core, n.half) + q * n.cols + at.start, n.thin)
+        grads_out[m][:, own_at] = r.final[c, core_rows, :]
+        copy_back(c).start()
 
     back_parts = []
 
@@ -899,22 +1043,23 @@
             r.dpre[q, at, :] = low
             r.bias_sum[q] += jnp.sum(low.astype(F32).reshape(step // 8, 8, n.cols), axis=0)
 
-        part = dot(r.dpre[q], full[0, q], NT)
-        r.total[...] = r.total[...] + part if back_parts else part
         back_parts.append(q)
+        for half in (theirs, mine):
+            part = dot(r.dpre[q, half, :], full[0, q], NT)
+            part = r.total[half, :] + part if len(back_parts) > 1 else part
+            if len(back_parts) == n.chunks and half is theirs:
+                r.part_low2[...] = part.astype(BF16)
+                go(swap_dh())
+            else:
+                r.total[half, :] = part
 
     def swap_dh():
         return swap(3, r.part_low2, r.part_in2)
-
-    def send_dh():
-        r.part_low2[...] = r.total[theirs, :].astype(BF16)
-        go(swap_dh())
 
     def first_norm_back(at):
         dh = r.total[at, :] + r.part_in2[at, :].astype(F32) + r.dr2[at, :]
         unit = r.unit1[at, :]
-        r.sums[0] += fold(dh * unit)
-        r.sums[1] += fold(dh)
+        r.x_place[at, :] = dh
         du = dh * r.vecs[0:1, :]
         dv = r.scale1[at, 0:1] * (du - mean(du) - unit * mean(du * unit))
         low = dv.astype(BF16)
@@ -925,7 +1070,7 @@
         swap_dh().wait_recv()
         row_loop(first_norm_back)
         loads.tt_b.wait()
-        mix_start(1, r.dm[...], r.tt_b_v)
+        mix_start(1, r.dm[...], r.tt_v)
         mix_send(1)
 
     def thirds(v):
@@ -957,15 +1102,28 @@
             plane(k),
         )
 
+    def fold(v):
+        return jnp.sum(v.reshape(tall // 8, 8, width), axis=0)
+
+    def vector_sums(at):
+        dh, dy = r.x_place[at, :], r.dy_place[at, :]
+        r.sums[0] += fold(dh * r.unit1[at, :])
+        r.sums[1] += fold(dh)
+        r.sums[2] += fold(r.dz[at, :].astype(F32))
+        r.sums[3] += fold(dy * r.h[at, :])
+        r.sums[4] += fold(dy)
+
     def small_grads():
+        r.sums[...] = jnp.zeros(r.sums.shape, F32)
+        row_loop(vector_sums)
         for i in range(5):
             line_sum = jnp.sum(r.sums[i], axis=0, keepdims=True)
-            tiles = small_gather(line_sum * r.vec_mask[...], r.vec_spread[...])
+            tiles = small_gather(line_sum * r.vec_mask_v[...], r.vec_spread_v[...])
             r.small_out[:, :, i, :] = tiles.reshape(n.batch, n.seq, 128)
         line_sum = jnp.concatenate(
             [jnp.sum(r.bias_sum[q], axis=0, keepdims=True) for q in range(n.chunks)], axis=1
         )
-        tiles = small_gather(jnp.where(bias_mask, line_sum, 0.0), r.bias_spread[...])
+        tiles = small_gather(jnp.where(bias_mask, line_sum, 0.0), r.bias_spread_v[...])
         r.small_out[:, :, 5:8, :] = jnp.zeros((n.batch, n.seq, 3, 128), F32)
         r.small_out[pl.ds(core * (n.batch // 2), n.batch // 2), :, 5, :] = tiles.reshape(
             n.batch // 2, n.seq, 128
@@ -998,156 +1156,101 @@
 
     def mix_back():
         loads.un_b.wait()
-        mix_finish(1, r.un_b_v)
+        mix_finish(1, r.un_v)
         r.dx[...] = r.dx[...] + r.mixed[...]
 
     for task, *which in (
-        (grad_product, 0), (grad_product, 2), (grad_product, 1), (slope_back, 1),
-        (grad_side, 2), (slope_back, 2), (grad_product, 9), (slope_back, 0), (grad_side, 1),
-        (send_dh,), (grad_line, 2), (grad_product, 4), (norm_back,), (grad_side, 9),
-        (grad_side, 0), (grad_product, 10), (grad_side, 4), (grad_product, 3),
-        (grad_product, 5), (grad_side, 10), (grad_line, 4), (grad_product, 7), (grad_across, 2),
-        (grad_line, 0), (grad_across, 0), (grad_side, 3), (grad_product, 6), (grad_out, 2),
-        (grad_across, 4), (grad_line, 1), (grad_across, 1), (grad_product, 8), (turn_back,),
-        (grad_side, 5), (grad_out, 1), (grad_line, 10), (grad_product, 11), (grad_out, 4),
-        (grad_side, 7), (grad_line, 3), (grad_end, 2), (grad_across, 3), (outputs,),
-        (grad_end, 1), (grad_side, 8), (grad_across, 10), (grad_out, 0), (grad_line, 5),
-        (mix_back,), (grad_line, 9), (grad_side, 11), (grad_across, 9), (grad_line, 7),
-        (grad_side, 6), (grad_across, 5), (grad_end, 4), (grad_out, 10), (small_grads,),
-        (grad_line, 8), (grad_across, 7), (grad_line, 11), (grad_out, 9), (grad_out, 5),
-        (grad_across, 8), (grad_across, 11), (grad_line, 6), (grad_out, 3), (grad_end, 3),
-        (grad_end, 0), (grad_across, 6), (grad_end, 5), (grad_out, 8), (small_rows_back,),
-        (grad_end, 9), (grad_end, 10), (grad_out, 11), (grad_out, 7), (grad_end, 8),
-        (grad_end, 7), (grad_out, 6), (grad_end, 11), (small_end,), (grad_end, 6),
+        (grad_product, 5), (grad_product, 3), (slope_back, 0), (grad_product, 2),
+        (slope_back, 1), (grad_side, 5), (grad_side, 3), (slope_back, 2), (grad_line, 3),
+        (grad_product, 10), (grad_product, 1), (grad_product, 7), (grad_line, 5),
+        (grad_across, 3), (norm_back,), (grad_out, 3), (grad_side, 10), (grad_side, 1),
+        (grad_side, 7), (grad_product, 9), (grad_side, 2), (grad_line, 10), (grad_product, 8),
+        (grad_product, 6), (grad_line, 7), (grad_across, 10), (grad_line, 1), (grad_line, 2),
+        (grad_product, 0), (grad_across, 7), (grad_across, 5), (grad_side, 6), (turn_back,),
+        (grad_side, 9), (grad_product, 4), (outputs,), (grad_across, 1), (grad_side, 0),
+        (grad_line, 6), (grad_line, 9), (grad_across, 2), (grad_side, 8), (grad_side, 4),
+        (small_grads,), (grad_across, 6), (grad_product, 11), (grad_across, 9), (grad_out, 2),
+        (grad_line, 0), (grad_out, 10), (grad_line, 8), (grad_out, 5), (grad_out, 1),
+        (grad_line, 4), (grad_out, 6), (grad_out, 7), (grad_across, 0), (grad_side, 11),
+        (small_rows_back,), (grad_far, 7), (grad_far, 10), (grad_across, 8), (grad_out, 9),
+        (grad_far, 9), (grad_far, 3), (grad_out, 0), (grad_line, 11), (grad_across, 4),
+        (grad_out, 8), (grad_far, 5), (grad_end, 3), (grad_end, 9), (grad_far, 6), (mix_back,),
+        (grad_end, 7), (grad_out, 4), (small_end,), (grad_far, 4), (grad_end, 5), (grad_far, 0),
+        (grad_across, 11), (grad_end, 10), (grad_out, 11), (grad_far, 1), (grad_far, 2),
+        (grad_end, 4), (grad_far, 8), (grad_far, 11), (grad_end, 2), (grad_end, 0),
+        (grad_end, 6), (grad_end, 1), (grad_end, 8), (grad_end, 11),
     ):
         task(*which)
 
-    grads = (r.g1, r.g2)
-    for m in range(2):
-        r.final_turn[m] = jnp.concatenate([r.final[m, q] for q in range(n.chunks)], axis=1)
-    their_rows = pl.ds(aligned(1 - core, n.rows), n.rows)
-    back = [
-        go(
-            remote(
-                r.final_turn.at[m, their_rows],
-                r.final_in.at[m],
-                r.back_send.at[m],
-                r.back_recv.at[m],
-                other_core,
-                seq_at,
-            )
-        )
-        for m in range(2)
-    ]
-    squares = jnp.zeros((8, 128), F32)
-
-    def squares_of(v):
-        v = v * v
-        v = jnp.sum(v.reshape(v.shape[0] // 8, 8, v.shape[1]), axis=0)
-        return sum(v[:, i : i + 128] for i in range(0, v.shape[1], 128))
-
-    squares = squares + r.g_small[...] * r.g_small[...]
-    for m in range(2):
-        grads[m][:, keep] = r.final_turn[m, core_rows, :]
-        back[m].wait_recv()
-        grads[m][:, give] = r.final_in[m]
-        squares = squares + squares_of(grads[m][...])
-    r.norm_own[...] = squares
-    r.norm_plane[seq_at] = squares
-    for k in range(1, n.seq):
-        go(
-            remote(
-                r.norm_own,
-                r.norm_plane.at[seq_at],
-                r.norm_send.at[k - 1],
-                r.norm_recv.at[k - 1],
-                batch_at,
-                plane(k),
-            )
-        )
-    for k in range(1, n.seq):
-        remote(
-            r.norm_own,
-            r.norm_plane.at[plane_from(k)],
-            r.norm_send.at[k - 1],
-            r.norm_recv.at[k - 1],
-            batch_at,
-            plane(k),
-        ).wait_recv()
-    squares = r.norm_plane[0]
-    for k in range(1, n.seq):
-        squares = squares + r.norm_plane[k]
-    r.norm_sum[...] = squares
-    r.norm_all[batch_at] = squares
-    for k in range(1, n.batch):
-        go(
-            remote(
-                r.norm_sum,
-                r.norm_all.at[batch_at],
-                r.norm_send2.at[k - 1],
-                r.norm_recv2.at[k - 1],
-                across(k),
-                seq_at,
-            )
-        )
-    for k in range(1, n.batch):
-        remote(
-            r.norm_sum,
-            r.norm_all.at[across_from(k)],
-            r.norm_send2.at[k - 1],
-            r.norm_recv2.at[k - 1],
-            across(k),
-            seq_at,
-        ).wait_recv()
-    squares = r.norm_all[0]
-    for k in range(1, n.batch):
-        squares = squares + r.norm_all[k]
-    whole = jnp.sum(jnp.sum(squares, axis=1, keepdims=True), axis=0, keepdims=True)
+    squares = r.squares[...] + r.g_small[...] * r.g_small[...]
+    r.norm_own[...] = jnp.sum(squares, axis=0, keepdims=True)
+    r.norm_all[batch_at * n.seq + seq_at] = r.norm_own[...]
+
+    def norm_copy(i, at):
+        return remote(
+            r.norm_own, r.norm_all.at[at], r.norm_send.at[i], r.norm_recv.at[i], *everyone[i]
+        )
+
+    for i in range(n.devices - 1):
+        go(norm_copy(i, batch_at * n.seq + seq_at))
+    for c in range(2 * n.chunks * n.parts):
+        m, q, at = wide(c)
+        copy_back(c).wait_recv()
+        their_at = pl.ds(aligned(1 - core, n.half) + q * n.cols + at.start, n.thin)
+        grads_out[m][:, their_at] = r.final_in[c]
+    for i in range(n.devices - 1):
+        j = i + 1
+        batch_from = (batch_at + n.batch - j // n.seq) % n.batch
+        seq_from = (seq_at + n.seq - j % n.seq) % n.seq
+        norm_copy(i, batch_from * n.seq + seq_from).wait_recv()
+    squares = jnp.sum(r.norm_all[...].reshape(n.devices, 128), axis=0, keepdims=True)
+    whole = jnp.sum(squares, axis=1, keepdims=True)
     r.norm[...] = jnp.broadcast_to(jnp.sqrt(whole), (8, 128))
 
     for copy in started:
         copy.wait_send()
 
     for c in range(2 * n.chunks):
-        own_to_mate(c).wait_send()
-        slabs_of(c, 3 * n.zs, r.second_recv).wait_send()
+        moved = 2 * n.zs + (1 if split(c) else n.zs)
+        slabs_of(c, moved, r.second_recv).wait_send()
+        for far in range(1 + split(c)):
+            own_to_mate(c, far).wait_send()
+
+            @pl.when(inner)
+            def _(c=c, far=far):
+                pair_across(c, far).wait_send()
+                pair_out(c, far).wait_send()
 
     for c in range(2 * n.chunks * n.parts):
-        for copy in (copy_diagonal(c), copy_near(c), copy_side(c), copy_mate(c)):
-            copy.wait_send()
-
-    @pl.when(inner)
-    def _():
-        for c in range(2 * n.chunks):
-            pair_across(c).wait_send()
-            pair_out(c).wait_send()
-        for c in range(2 * n.chunks * n.parts):
-            copy_pair_across(c).wait_send()
-
-    @pl.when(jnp.logical_not(inner))
-    def _():
-        for c in range(2 * n.chunks * n.parts):
-            copy_pair_in(c).wait_send()
+        copy_back(c).wait_send()
+        copy_diagonal(c).wait_send()
+        copy_near(c).wait_send()
+        (copy_far if back_mode(c) == 1 else copy_side)(c).wait_send()
+        if back_mode(c) == 2:
+            for d in range(1, n.zs):
+                copy_direct(c, d).wait_send()
+        for far in fars(c):
+            copy_mate(c, far).wait_send()
+
+            @pl.when(inner)
+            def _(c=c, far=far):
+                copy_pair_across(c, far).wait_send()
+
+            @pl.when(jnp.logical_not(inner))
+            def _(c=c, far=far):
+                copy_pair_in(c, far).wait_send()
 
 
 def run_layer(n, x, dy, w1, w2, bias, vec):
     tables = host_tables(n)
     tokens, width, cols, q = n.tokens, n.width, n.cols, n.chunks
     grads = 2 * q * n.parts
+    splits = max(1, sum(kind // 2 == 1 for kind in BACK_KINDS))
+    directs = max(1, sum(kind // 2 == 2 for kind in BACK_KINDS))
     dma = pltpu.SemaphoreType.DMA
     vmem = pltpu.VMEM
-    inputs = dict(
-        x=x,
-        dy=dy,
-        w1=w1,
-        w2=w2,
-        bias=bias,
-        vec=vec,
-        vec_mask=tables.vec_mask,
-        vec_spread=tables.vec_spread,
-        bias_spread=tables.bias_spread,
-    )
-    inputs.update({name: getattr(tables, name) for name in TABLES})
+    inputs = dict(bias=bias, vec=vec, x=x, dy=dy, w1=w1, w2=w2)
+    inputs.update({name: getattr(tables, name) for name in LOADS if name not in inputs})
     outputs = dict(
         out=((tokens, width), BF16),
         dx=((tokens, width), F32),
@@ -1156,9 +1259,9 @@
         g_small=((8, 128), F32),
         norm=((8, 128), F32),
     )
-    scratch = {name + "_v": vmem(getattr(tables, name).shape, BF16) for name in TABLES}
+    scratch = {held: vmem(inputs[name].shape, inputs[name].dtype) for name, held in LOADS.items()}
     scratch.update(
-        load_sem=dma((len(TABLES),)),
+        load_sem=dma((len(LOADS),)),
         stage=vmem((2, n.slab, n.half), F32),
         swap_send=dma((2,)),
         swap_recv=dma((2,)),
@@ -1177,11 +1280,11 @@
         mix_recv=dma((4, n.seq - 1)),
         mixed=vmem((tokens, width), F32),
         full=vmem((2, q, width, cols), BF16),
-        mate_send=dma((2, q)),
-        mate_recv=dma((2, q)),
-        across_send=dma((2, q)),
-        out_send=dma((2, q)),
-        pair_recv=dma((2, q)),
+        mate_send=dma((2, 2, q)),
+        mate_recv=dma((2, 2, q)),
+        across_send=dma((2, 2, q)),
+        out_send=dma((2, 2, q)),
+        pair_recv=dma((2, 2, q)),
         side_send=dma((2, q)),
         first_recv=dma((3, 2, q)),
         second_recv=dma((2, q)),
@@ -1207,8 +1310,6 @@
         out_low=vmem((tokens, width), BF16),
         dr2=vmem((tokens, width), F32),
         dz=vmem((2 * tokens, width), BF16),
-        h_turned=vmem((width, 2 * tokens), BF16),
-        dz_turned=vmem((width, 2 * tokens), BF16),
         acc=vmem((grads, width, n.thin), F32),
         give=vmem((grads, width, n.thin), BF16),
         in_diagonal=vmem((grads, n.segment, n.thin), BF16),
@@ -1217,8 +1318,13 @@
         in_mate=vmem((grads, n.slab, n.thin), BF16),
         in_pair=vmem((grads, 2 * n.slab, n.thin), BF16),
         in_across=vmem((grads, 2 * n.slab, n.thin), BF16),
-        grad_send=dma((6, grads)),
-        grad_recv=dma((6, grads)),
+        far_mate=vmem((splits, n.slab, n.thin), BF16),
+        far_pair=vmem((splits, 2 * n.slab, n.thin), BF16),
+        far_across=vmem((splits, 2 * n.slab, n.thin), BF16),
+        in_far=vmem((splits, n.slab, n.thin), BF16),
+        in_direct=vmem((n.zs - 1, directs, n.slab, n.thin), BF16),
+        grad_send=dma((8 + n.zs, grads)),
+        grad_recv=dma((8 + n.zs, grads)),
         bias_sum=vmem((q, 8, cols), F32),
         dpre=vmem((q, 2 * tokens, cols), BF16),
         dm=vmem((tokens, width), BF16),
@@ -1231,31 +1337,27 @@
         small_last=vmem((n.seq - 1, 8, 128), F32),
         small_send2=dma((n.seq - 1,)),
         small_recv2=dma((n.seq - 1,)),
-        final=vmem((2, q, n.slab, cols), F32),
-        final_turn=vmem((2, n.slab, n.half), F32),
-        final_in=vmem((2, n.rows, n.half), F32),
-        back_send=dma((2,)),
-        back_recv=dma((2,)),
-        norm_own=vmem((8, 128), F32),
-        norm_plane=vmem((n.seq, 8, 128), F32),
-        norm_sum=vmem((8, 128), F32),
-        norm_all=vmem((n.batch, 8, 128), F32),
-        norm_send=dma((n.seq - 1,)),
-        norm_recv=dma((n.seq - 1,)),
-        norm_send2=dma((n.batch - 1,)),
-        norm_recv2=dma((n.batch - 1,)),
+        final=vmem((grads, n.slab, n.thin), F32),
+        final_in=vmem((grads, n.rows, n.thin), F32),
+        back_send=dma((grads,)),
+        back_recv=dma((grads,)),
+        squares=vmem((8, 128), F32),
+        norm_own=vmem((1, 128), F32),
+        norm_all=vmem((n.devices, 1, 128), F32),
+        norm_send=dma((n.devices - 1,)),
+        norm_recv=dma((n.devices - 1,)),
     )
     names = tuple(inputs) + tuple(outputs) + tuple(scratch)
     in_vmem = pl.BlockSpec(memory_space=pltpu.VMEM)
     anywhere = pl.BlockSpec(memory_space=pl.ANY)
     values = pl.pallas_call(
         functools.partial(layer_kernel, n, names),
-        out_shape=[jax.ShapeDtypeStruct(*shape) for shape in outputs.values()],
-        in_specs=[anywhere if name in TABLES else in_vmem for name in inputs],
+        out_shape=[vmem(*shape) for shape in outputs.values()],
+        in_specs=[anywhere if name in LOADS else in_vmem for name in inputs],
         out_specs=[in_vmem] * len(outputs),
         scratch_shapes=list(scratch.values()),
         compiler_params=pltpu.CompilerParams(
-            collective_id=0, has_side_effects=True, vmem_limit_bytes=62 * 2**20
+            collective_id=0, has_side_effects=True, vmem_limit_bytes=58 * 2**20
         ),
         name="fused_layer",
     )(*inputs.values())

time: 143 us -> 128 us (0.90)
  Pallas kernels: 136 us -> 127 us
  local copies, waits for them, and re-layouts: 5.45 us -> 0.05 us
    pallas_call x1, Pallas kernels: 133 us -> 124 us  [run_layer(): pl.pallas_call(functools.partial(layer_kernel, n, names), out_shape=[vmem...]
    unnamed x36 -> x24, local copies, waits for them, and re-layouts: 5.45 us -> 0.05 us
where the time goes in v3:
time: 128 us
  Pallas kernels  127 us (99%)
    pallas_call x1, Pallas kernels, run_layer(): pl.pallas_call(functools.partial(layer_kernel, n, names), out_shape=[vmem...  124 us

profile of v3, /device:TPU:0, one launch (start us, length us, event | category | flops | bytes accessed | tf_op | source)
XLA Modules:
  0.0 127.7 jit_solution(3774413579869932364)
XLA Ops:
  0.7 0.0 copy-start
  0.7 0.0 copy-start.1
  0.7 0.0 copy-start.2
  0.7 0.0 copy-start.3
  0.7 0.0 copy-start.4
  0.7 0.0 copy-start.5
  0.7 0.0 copy-start.6
  0.7 0.0 copy-start.7
  0.7 0.0 copy-start.8
  0.7 0.0 copy-start.9
  0.8 0.0 copy-start.10
  0.8 0.0 copy-start.11
  0.8 124.3 %fused_layer.1 = (bf16[256,768]{1,0:T(8,128)(2,1)S(1)}, f32[256,768]{1,0:T(8,128)S(1)}, f32[24,3072]{1,0:T(8,128)S(1)}, f32[24,3072]{1,0:T(8,128)S(1)}, f32[8,128]{1,0:T(8,128)S(1)}, /*index=5*/f32[8,128]{1,0:T(8,128)S(1)}) custom-call(f32[1,96]{1,0:T(1,128)} %refs_10_.2, f32[5,1,24]{2,1,0:T(1,128)} %bitcast.43, bf16[256,768]{1,0:T(8,128)(2,1)} %bitcast.47, ...), custom_call_target="tpu_custom_call" | custom-call | tf_op jit(solution)/shard_map/fused_layer/pallas_call | solution.py:1353
  125.1 0.0 copy-done
  125.1 0.0 copy-done.1
  125.1 0.0 copy-done.2
  125.1 0.0 copy-done.3
  125.1 0.0 copy-done.4
  125.1 0.0 copy-done.5
  125.1 0.0 copy-done.6
  125.2 0.0 copy-done.7
  125.2 0.0 copy-done.8
  125.2 0.0 copy-done.9
  125.2 2.3 %adam.1 = (f32[1,1]{1,0:T(1,128)}, f32[24,3072]{1,0:T(8,128)}, f32[24,3072]{1,0:T(8,128)}, f32[24,3072]{1,0:T(8,128)}, f32[24,3072]{1,0:T(8,128)}, /*index=5*/f3...) custom-call(f32[24,3072]{1,0:T(8,128)S(1)} %get-tuple-element.36.ref, ...), custom_call_target="tpu_custom_call" | custom-call | tf_op jit(solution)/shard_map/adam/pallas_call | solution.py:1419
  (2 shorter events, 0.0 us)
Async XLA Ops:
  0.7 124.4 %copy-start = (f32[1,24,3072]{2,1,0:T(8,128)S(1)}, f32[1,24,3072]{2,1,0:T(8,128)}, u32[]{:S(2)}) copy-start(f32[1,24,3072]{2,1,0:T(8,128)} %param.25) | copy-start | bytes 884740
  0.7 124.4 %copy-start.1 = (f32[1,3072,24]{1,2,0:T(8,128)S(1)}, f32[1,3072,24]{1,2,0:T(8,128)}, u32[]{:S(2)}) copy-start(f32[1,3072,24]{1,2,0:T(8,128)} %param.26) | copy-start | bytes 884740
  0.7 124.4 %copy-start.2 = (f32[1,24,3072]{2,1,0:T(8,128)S(1)}, f32[1,24,3072]{2,1,0:T(8,128)}, u32[]{:S(2)}) copy-start(f32[1,24,3072]{2,1,0:T(8,128)} %param.29) | copy-start | bytes 884740
  0.7 124.4 %copy-start.3 = (f32[1,24,3072]{2,1,0:T(8,128)S(1)}, f32[1,24,3072]{2,1,0:T(8,128)}, u32[]{:S(2)}) copy-start(f32[1,24,3072]{2,1,0:T(8,128)} %param.30) | copy-start | bytes 884740
  0.7 124.4 %copy-start.4 = (f32[1,3072,24]{1,2,0:T(8,128)S(1)}, f32[1,3072,24]{1,2,0:T(8,128)}, u32[]{:S(2)}) copy-start(f32[1,3072,24]{1,2,0:T(8,128)} %param.31) | copy-start | bytes 884740
  0.7 124.4 %copy-start.5 = (f32[1,3072,24]{1,2,0:T(8,128)S(1)}, f32[1,3072,24]{1,2,0:T(8,128)}, u32[]{:S(2)}) copy-start(f32[1,3072,24]{1,2,0:T(8,128)} %param.32) | copy-start | bytes 884740
  0.7 124.4 %copy-start.6 = (f32[1,5,24]{2,0,1:T(1,128)S(1)}, f32[1,5,24]{2,0,1:T(1,128)}, u32[]{:S(2)}) copy-start(f32[1,5,24]{2,0,1:T(1,128)} %param.28) | copy-start | bytes 1444
  0.7 124.4 %copy-start.7 = (f32[1,5,24]{2,0,1:T(1,128)S(1)}, f32[1,5,24]{2,0,1:T(1,128)}, u32[]{:S(2)}) copy-start(f32[1,5,24]{2,0,1:T(1,128)} %param.35) | copy-start | bytes 1444
  0.7 124.4 %copy-start.8 = (f32[1,5,24]{2,0,1:T(1,128)S(1)}, f32[1,5,24]{2,0,1:T(1,128)}, u32[]{:S(2)}) copy-start(f32[1,5,24]{2,0,1:T(1,128)} %param.36) | copy-start | bytes 1444
  0.7 124.4 %copy-start.9 = (f32[1,96]{1,0:T(1,128)S(1)}, f32[1,96]{1,0:T(1,128)}, u32[]{:S(2)}) copy-start(f32[1,96]{1,0:T(1,128)} %refs_10_.2) | copy-start | bytes 1156
  0.8 124.4 %copy-start.10 = (f32[1,96]{1,0:T(1,128)S(1)}, f32[1,96]{1,0:T(1,128)}, u32[]{:S(2)}) copy-start(f32[1,96]{1,0:T(1,128)} %refs_11_.2) | copy-start | bytes 1156
  0.8 124.4 %copy-start.11 = (f32[1,96]{1,0:T(1,128)S(1)}, f32[1,96]{1,0:T(1,128)}, u32[]{:S(2)}) copy-start(f32[1,96]{1,0:T(1,128)} %refs_12_.2) | copy-start | bytes 1156

commit v4 on v3

--- a/solution.py
+++ b/solution.py
@@ -332,6 +332,8 @@
 
 
 LOADS = dict(
+    bias="bias_v",
+    vec="vec_v",
     w1="w1_v",
     w2="w2_v",
     x="x_v",
@@ -347,8 +349,8 @@
     un_b="un_v",
 )
 LATER = ("tt_b", "un_b")
-FORWARD_KINDS = (1, 2, 1, 3, 1, 0)
-BACK_KINDS = (1, 1, 4, 3, 5, 4, 3, 0, 0, 0, 3, 4)
+FORWARD_KINDS = (1, 1, 0, 0, 0, 3)
+BACK_KINDS = (0, 5, 0, 5, 2, 1, 1, 5, 3, 5, 5, 4, 0)
 
 
 def layer_kernel(n, names, *refs):
@@ -380,6 +382,9 @@
         started.append(copy)
         return copy
 
+    def bytes_of(view, send, recv):
+        return remote(view, view, send, recv, other_core, seq_at)
+
     other_core = 2 * x + 1 - core
     other_x = 2 * (1 - x) + core
     other_y = 2 * z + 1 - y
@@ -419,19 +424,16 @@
     keep = pl.ds(aligned(core, n.half), n.half)
     core_rows = pl.ds(aligned(core, n.rows), n.rows)
     their_rows = pl.ds(aligned(1 - core, n.rows), n.rows)
-    swaps = [
-        go(
-            remote(
-                weights[m].at[:, give],
-                r.stage.at[m, core_rows],
-                r.swap_send.at[m],
-                r.swap_recv.at[m],
-                other_core,
-                seq_at,
-            )
-        )
-        for m in range(2)
-    ]
+    for m in range(2):
+        remote(
+            weights[m].at[:, give],
+            r.stage.at[m, core_rows],
+            r.swap_send,
+            r.swap_recv,
+            other_core,
+            seq_at,
+        ).start()
+    swapped = bytes_of(r.stage.at[:, pl.ds(0, n.rows)], r.swap_send, r.swap_recv)
 
     def mix_start(t, source, table):
         y_ref, l_ref = r.y_buf.at[t], r.l_buf.at[t]
@@ -441,28 +443,22 @@
     def mix_send(t):
         y_ref, l_ref = r.y_buf.at[t], r.l_buf.at[t]
         for k in range(1, n.seq):
-            go(
-                remote(
-                    y_ref.at[rows_of(plane(k), n.packed)],
-                    l_ref.at[seq_at],
-                    r.mix_send.at[2 * t, k - 1],
-                    r.mix_recv.at[2 * t, k - 1],
-                    batch_at,
-                    plane(k),
-                )
-            )
+            remote(
+                y_ref.at[rows_of(plane(k), n.packed)],
+                l_ref.at[seq_at],
+                r.mix_send.at[2 * t],
+                r.mix_recv.at[2 * t],
+                batch_at,
+                plane(k),
+            ).start()
+
+    def mixed_bytes(i):
+        into = (r.l_buf, r.r_buf)[i % 2].at[i // 2, pl.ds(0, n.seq - 1)]
+        return bytes_of(into, r.mix_send.at[i], r.mix_recv.at[i])
 
     def mix_turn(t):
         l_ref, z_ref, r_ref = r.l_buf.at[t], r.z_buf.at[t], r.r_buf.at[t]
-        for k in range(1, n.seq):
-            remote(
-                r.y_buf.at[t, rows_of(plane(k), n.packed)],
-                l_ref.at[plane_from(k)],
-                r.mix_send.at[2 * t, k - 1],
-                r.mix_recv.at[2 * t, k - 1],
-                batch_at,
-                plane(k),
-            ).wait_recv()
+        mixed_bytes(2 * t).wait_recv()
         left = jnp.concatenate(
             [
                 jnp.concatenate(
@@ -484,29 +480,19 @@
             z_ref[e] = value[:, : n.block]
             z_ref[e + 1] = value[:, n.block :]
         for k in range(1, n.seq):
-            go(
-                remote(
-                    z_ref.at[plane(k)],
-                    r_ref.at[seq_at],
-                    r.mix_send.at[2 * t + 1, k - 1],
-                    r.mix_recv.at[2 * t + 1, k - 1],
-                    batch_at,
-                    plane(k),
-                )
-            )
+            remote(
+                z_ref.at[plane(k)],
+                r_ref.at[seq_at],
+                r.mix_send.at[2 * t + 1],
+                r.mix_recv.at[2 * t + 1],
+                batch_at,
+                plane(k),
+            ).start()
         r_ref[seq_at] = z_ref[seq_at]
 
     def mix_finish(t, table):
         r_ref = r.r_buf.at[t]
-        for k in range(1, n.seq):
-            remote(
-                r.z_buf.at[t, plane(k)],
-                r_ref.at[plane_from(k)],
-                r.mix_send.at[2 * t + 1, k - 1],
-                r.mix_recv.at[2 * t + 1, k - 1],
-                batch_at,
-                plane(k),
-            ).wait_recv()
+        mixed_bytes(2 * t + 1).wait_recv()
         parts = [
             r_ref[:, g * n.packed : (g + 1) * n.packed, :].reshape(width, n.block)
             for g in range(n.seqs)
@@ -555,14 +541,8 @@
     def stage_weights():
         for m in range(2):
             r.stage[m, core_rows, :] = weights[m][:, keep]
-            remote(
-                weights[m].at[:, give],
-                r.stage.at[m, their_rows],
-                r.swap_send.at[m],
-                r.swap_recv.at[m],
-                other_core,
-                seq_at,
-            ).wait_recv()
+        swapped.wait_recv()
+        for m in range(2):
             for q in range(n.chunks):
                 full[m, q, slab_rows(x, y, z), :] = r.stage[
                     m, :, q * n.cols : (q + 1) * n.cols
@@ -570,14 +550,14 @@
 
     def full_copy(c, at, send, recv, to):
         m, q = place(c)
-        return remote(full.at[m, q, at], full.at[m, q, at], send.at[m, q], recv.at[m, q], *to)
+        return remote(full.at[m, q, at], full.at[m, q, at], send.at[c], recv, *to)
 
     def rows_at(sx, sy, i):
         return (slab_rows(sx, sy, z), slab_rows(sx, sy, mate_z), pair_rows(sx, sy, 1 - pair_z))[i]
 
     def side_copy(c, i, sx, sy, first):
         t = turn_of(c)
-        recv = r.first_recv.at[i] if first else r.second_recv
+        recv = r.first_recv.at[i, c] if first else r.second_recv.at[c]
         return full_copy(c, rows_at(sx, sy, i), r.side_send, recv, peer(t if first else 1 - t))
 
     def to_sides(c, i):
@@ -590,19 +570,19 @@
 
     def own_to_mate(c, far):
         at = rows_at(*line_seg(c, far), 0)
-        return full_copy(c, at, r.mate_send.at[far], r.mate_recv.at[far], line(mate_z))
+        return full_copy(c, at, r.side_send, r.mate_recv.at[far, c], line(mate_z))
 
     def mate_arrives(c, far):
         at = rows_at(*line_seg(c, far), 1)
-        full_copy(c, at, r.mate_send.at[far], r.mate_recv.at[far], line(mate_z)).wait_recv()
+        full_copy(c, at, r.side_send, r.mate_recv.at[far, c], line(mate_z)).wait_recv()
 
     def pair_across(c, far):
         at = pair_rows(*line_seg(c, far), pair_z)
-        return full_copy(c, at, r.across_send.at[far], r.pair_recv.at[far], line(n.zs - 1 - z))
+        return full_copy(c, at, r.inner_send, r.pair_recv.at[far, c], line(n.zs - 1 - z))
 
     def pair_out(c, far):
         at = rows_at(*line_seg(c, far), 2)
-        return full_copy(c, at, r.out_send.at[far], r.pair_recv.at[far], line(mate_z))
+        return full_copy(c, at, r.inner_send, r.pair_recv.at[far, c], line(mate_z))
 
     def own_sides(c):
         to_sides(c, 0)
@@ -643,28 +623,31 @@
                 (from_mate, from_pair)[i - 1](c, 1)
         side_copy(c, i, ax, ay, False).start()
 
-    def slabs_of(c, count, recv):
-        return full_copy(c, pl.ds(0, count * slab), r.side_send, recv, other_x_at)
+    def slabs_of(c, count, send):
+        m, q = place(c)
+        return bytes_of(full.at[m, q, pl.ds(0, count * slab)], send.at[c], r.second_recv.at[c])
 
     def weights_here(c):
-        slabs_of(c, 2 * n.zs, r.second_recv).wait_recv()
+        slabs_of(c, 2 * n.zs, r.side_send).wait_recv()
 
     def small_tiles():
+        loads.bias.wait()
+        loads.vec.wait()
         tile = r.tile
         tile[...] = jnp.zeros(tile.shape, F32)
         for i in range(5):
-            tile[i : i + 1, 0 : n.rows] = r.vec[i]
-        tile[5:6, 0 : n.bias] = r.bias[...]
+            tile[i : i + 1, 0 : n.rows] = r.vec_v[i]
+        tile[5:6, 0 : n.bias] = r.bias_v[...]
         small[batch_at, seq_at] = tile[...]
         for k in range(1, n.seq):
-            go(small_copy(k, seq_at))
+            small_copy(k, seq_at).start()
 
     def small_copy(k, at):
         return remote(
             r.tile,
             small.at[batch_at, at],
-            r.small_send.at[k - 1],
-            r.small_recv.at[k - 1],
+            r.small_send,
+            r.small_recv,
             batch_at,
             plane(k),
         )
@@ -673,19 +656,24 @@
         return remote(
             small.at[batch_at],
             small.at[at],
-            r.row_send.at[k - 1],
-            r.row_recv.at[k - 1],
+            r.row_send,
+            r.row_recv,
             across(k),
             seq_at,
         )
 
     small = r.small
 
+    def tiles_bytes():
+        return bytes_of(small.at[0, pl.ds(0, n.seq - 1)], r.small_send, r.small_recv)
+
+    def rows_bytes():
+        return bytes_of(small.at[pl.ds(0, n.batch - 1)], r.row_send, r.row_recv)
+
     def small_rows():
-        for k in range(1, n.seq):
-            small_copy(k, plane_from(k)).wait_recv()
+        tiles_bytes().wait_recv()
         for k in range(1, n.batch):
-            go(row_copy(k, batch_at))
+            row_copy(k, batch_at).start()
 
     half_owners = n.devices // 2
     bias_mask = (
@@ -694,8 +682,7 @@
     )
 
     def small_vectors():
-        for k in range(1, n.batch):
-            row_copy(k, across_from(k)).wait_recv()
+        rows_bytes().wait_recv()
         for load in (loads.vec_spread, loads.bias_spread, loads.vec_mask):
             load.wait()
         for i in range(5):
@@ -800,17 +787,17 @@
         mix_send(0)
 
     forward_steps = (
-        (send_forward,), (stage_weights,), (own_line, 2), (own_line, 0), (own_line, 5),
-        (own_sides, 4), (place_inputs,), (small_tiles,), (own_sides, 3), (own_sides, 2),
-        (own_line, 4), (own_sides, 5), (mate_in, 2), (pass_on, 4, 0), (own_sides, 0),
-        (mate_in, 5), (pass_on, 5, 0), (pass_on, 3, 0), (own_line, 1), (own_sides, 1),
-        (mate_in, 0), (pass_on, 2, 0), (pass_on, 2, 1), (mate_in, 4), (pair_in, 2),
-        (pass_on, 5, 1), (pass_on, 0, 0), (pass_on, 3, 1), (pass_on, 1, 0), (turn_forward,),
-        (pair_in, 0), (small_rows,), (pair_in, 5), (pass_on, 2, 2), (pair_in, 4),
-        (pass_on, 3, 2), (pass_on, 0, 1), (pass_on, 4, 1), (small_vectors,), (pass_on, 1, 1),
-        (pass_on, 0, 2), (own_line, 3), (pass_on, 5, 2), (mate_in, 1), (norm_forward,),
-        (mate_in, 3), (pass_on, 1, 2), (pass_on, 4, 2), (pair_in, 1), (lift, 2), (pair_in, 3),
-        (lift, 0), (lift, 1), (drop, 2), (drop, 1), (drop, 0),
+        (send_forward,), (stage_weights,), (own_sides, 0), (own_sides, 1), (own_line, 1),
+        (own_sides, 4), (own_sides, 2), (own_line, 0), (own_line, 2), (place_inputs,),
+        (own_sides, 3), (own_sides, 5), (small_tiles,), (own_line, 4), (own_line, 5),
+        (pass_on, 0, 0), (mate_in, 1), (mate_in, 0), (pass_on, 3, 0), (mate_in, 2),
+        (own_line, 3), (mate_in, 4), (pass_on, 1, 0), (small_rows,), (pass_on, 5, 0),
+        (pass_on, 0, 1), (pass_on, 4, 0), (pass_on, 2, 0), (pair_in, 1), (mate_in, 3),
+        (pair_in, 0), (pair_in, 2), (mate_in, 5), (pass_on, 1, 1), (pass_on, 4, 1),
+        (small_vectors,), (turn_forward,), (pass_on, 2, 1), (pass_on, 1, 2), (pair_in, 3),
+        (pass_on, 5, 1), (pass_on, 2, 2), (pass_on, 3, 1), (pair_in, 4), (pair_in, 5),
+        (pass_on, 0, 2), (norm_forward,), (pass_on, 5, 2), (pass_on, 4, 2), (lift, 1),
+        (lift, 2), (pass_on, 3, 2), (lift, 0), (drop, 1), (drop, 2), (drop, 0),
     )
     for task, *which in forward_steps:
         task(*which)
@@ -840,18 +827,19 @@
 
     acc, out_low = r.acc, r.give
 
+    pieces = grad_pieces(n)
+
     def wide(c):
-        m, q = c // (n.chunks * n.parts), c % (n.chunks * n.parts)
-        return 1 - m, q // n.parts, pl.ds((q % n.parts) * n.thin, n.thin)
-
-    def grad_copy(c, at, into, i, to, slot=None):
-        return remote(
-            out_low.at[c, at],
-            into.at[c if slot is None else slot],
-            r.grad_send.at[i, c],
-            r.grad_recv.at[i, c],
-            *to,
-        )
+        slot, start, width_of = pieces[c]
+        m, q = slot // (n.chunks * n.parts), slot % (n.chunks * n.parts)
+        return 1 - m, q // n.parts, pl.ds((q % n.parts) * n.thin + start, width_of)
+
+    def held(c, at=slice(None), lead=()):
+        slot, start, width_of = pieces[c]
+        return (slot, *lead, at, pl.ds(start, width_of))
+
+    def grad_copy(c, at, into, recv, to):
+        return remote(out_low.at[held(c, at)], into, r.grad_send, recv, *to)
 
     def back_turn(c):
         return BACK_KINDS[c] % 2
@@ -863,32 +851,35 @@
         return [d for d, kind in enumerate(BACK_KINDS) if kind // 2 == back_mode(c)].index(c)
 
     def copy_diagonal(c):
-        return grad_copy(c, seg_rows(1 - x, 1 - y), r.in_diagonal, 0, peer(1 - back_turn(c)))
+        at = seg_rows(1 - x, 1 - y)
+        return grad_copy(c, at, r.in_diagonal.at[held(c)], r.diagonal_recv.at[c], peer(1 - back_turn(c)))
 
     def copy_near(c):
         t = 1 - back_turn(c)
-        return grad_copy(c, seg_rows(*away(t)), r.in_near, 1, peer(t))
+        into = r.in_sides.at[held(c, lead=(0,))]
+        return grad_copy(c, seg_rows(*away(t)), into, r.sides_recv.at[c], peer(t))
 
     def copy_side(c):
         t = back_turn(c)
-        return grad_copy(c, seg_rows(*away(t)), r.in_side, 2, peer(t))
+        into = r.in_sides.at[held(c, lead=(1,))]
+        return grad_copy(c, seg_rows(*away(t)), into, r.sides_recv.at[c], peer(t))
 
     def back_seg(c, far):
         return away(back_turn(c)) if far else (x, y)
 
     def line_into(c, far, i):
         if far:
-            return (r.far_mate, r.far_pair, r.far_across)[i].at[back_slot(c)]
-        return (r.in_mate, r.in_pair, r.in_across)[i].at[c]
+            into = (r.far_mate, r.far_pair, r.far_across)[i]
+            return into.at[back_slot(c), :, pl.ds(0, pieces[c][2])]
+        into, lead = ((r.in_end, (0,)), (r.in_pair, ()), (r.in_across, ()))[i]
+        return into.at[held(c, lead=lead)]
 
     def line_copy(c, at, far, i, to):
-        return remote(
-            out_low.at[c, at],
-            line_into(c, far, i),
-            r.grad_send.at[3 + 3 * far + i, c],
-            r.grad_recv.at[3 + 3 * far + i, c],
-            *to,
-        )
+        if far:
+            recv = r.far_recv.at[i, back_slot(c)]
+        else:
+            recv = (r.end_recv, r.pair_in_recv, r.across_recv)[i].at[c]
+        return grad_copy(c, at, line_into(c, far, i), recv, to)
 
     def copy_mate(c, far):
         at = slab_rows(*back_seg(c, far), mate_z)
@@ -904,25 +895,26 @@
 
     def copy_far(c):
         t = back_turn(c)
-        return grad_copy(c, slab_rows(*away(t), z), r.in_far, 2, peer(t), back_slot(c))
+        at = slab_rows(*away(t), z)
+        return grad_copy(c, at, r.in_end.at[held(c, lead=(1,))], r.end_recv.at[c], peer(t))
 
     def copy_direct(c, d):
         to_z = (z + d) % n.zs
-        into = r.in_direct.at[d - 1]
-        return grad_copy(c, slab_rows(x, y, to_z), into, 8 + d, line(to_z), back_slot(c))
+        at = slab_rows(x, y, to_z)
+        return grad_copy(c, at, r.in_end.at[held(c, lead=(d - 1,))], r.end_recv.at[c], line(to_z))
 
     def round_out(c, at, *more):
-        value = acc[c, at, :]
+        value = acc[held(c, at)]
         for ref in more:
             value = value + ref[...].astype(F32)
-        out_low[c, at, :] = value.astype(BF16)
+        out_low[held(c, at)] = value.astype(BF16)
 
     def grad_product(c):
         m, q, at = wide(c)
         if m:
-            acc[c] = dot(r.dz[...], r.act[q, :, at], TN)
+            acc[held(c)] = dot(r.dz[...], r.act[q, :, at], TN)
         else:
-            acc[c] = dot(r.h_low[...], r.dpre[q, :, at], TN)
+            acc[held(c)] = dot(r.h_low[...], r.dpre[q, :, at], TN)
         round_out(c, seg_rows(1 - x, 1 - y))
         copy_diagonal(c).start()
         round_out(c, seg_rows(*away(1 - back_turn(c))))
@@ -941,20 +933,19 @@
         copy_diagonal(c).wait_recv()
         at = seg_rows(*away(back_turn(c)))
         if back_mode(c) == 1:
-            acc[c, at, :] = acc[c, at, :] + r.in_diagonal[c].astype(F32)
+            acc[held(c, at)] = acc[held(c, at)] + r.in_diagonal[held(c)].astype(F32)
             line_start(c, 1)
         else:
-            round_out(c, at, r.in_diagonal.at[c])
+            round_out(c, at, r.in_diagonal.at[held(c)])
             copy_side(c).start()
 
     def grad_line(c):
-        copy_near(c).wait_recv()
-        more = r.in_near[c].astype(F32)
-        if back_mode(c) != 1:
-            copy_side(c).wait_recv()
-            more = more + r.in_side[c].astype(F32)
+        sides = 1 if back_mode(c) == 1 else 2
+        both = r.in_sides.at[held(c, lead=(pl.ds(0, sides),))]
+        bytes_of(both, r.grad_send, r.sides_recv.at[c]).wait_recv()
+        more = sum(r.in_sides[held(c, lead=(i,))].astype(F32) for i in range(sides))
         at = seg_rows(x, y)
-        acc[c, at, :] = acc[c, at, :] + more
+        acc[held(c, at)] = acc[held(c, at)] + more
         if back_mode(c) == 2:
             for d in range(1, n.zs):
                 round_out(c, slab_rows(x, y, (z + d) % n.zs))
@@ -983,7 +974,7 @@
                 copy_pair_across(c, far).wait_recv()
                 sx, sy = back_seg(c, far)
                 at = pair_rows(sx, sy, pair_z)
-                acc[c, at, :] = acc[c, at, :] + line_into(c, far, 2)[...].astype(F32)
+                acc[held(c, at)] = acc[held(c, at)] + line_into(c, far, 2)[...].astype(F32)
                 round_out(c, slab_rows(sx, sy, mate_z))
                 copy_mate(c, far).start()
 
@@ -1003,31 +994,26 @@
 
     def copy_back(c):
         return remote(
-            r.final.at[c, their_rows],
-            r.final_in.at[c],
-            r.back_send.at[c],
-            r.back_recv.at[c],
+            r.final.at[held(c, their_rows)],
+            r.final_in.at[held(c)],
+            r.back_send,
+            r.back_recv,
             other_core,
             seq_at,
         )
 
     def grad_end(c):
         m, q, at = wide(c)
-        value = acc[c, slab_rows(x, y, z), :]
-        if back_mode(c) == 2:
-            for d in range(1, n.zs):
-                copy_direct(c, d).wait_recv()
-                value = value + r.in_direct[d - 1, back_slot(c)].astype(F32)
-        else:
-            copy_mate(c, 0).wait_recv()
-            value = value + r.in_mate[c].astype(F32)
-        if back_mode(c) == 1:
-            copy_far(c).wait_recv()
-            value = value + r.in_far[back_slot(c)].astype(F32)
+        value = acc[held(c, slab_rows(x, y, z))]
+        ends = back_mode(c) + 1
+        all_ends = r.in_end.at[held(c, lead=(pl.ds(0, ends),))]
+        bytes_of(all_ends, r.grad_send, r.end_recv.at[c]).wait_recv()
+        for i in range(ends):
+            value = value + r.in_end[held(c, lead=(i,))].astype(F32)
         r.squares[...] += squares_of(value)
-        r.final[c] = value
-        own_at = pl.ds(aligned(core, n.half) + q * n.cols + at.start, n.thin)
-        grads_out[m][:, own_at] = r.final[c, core_rows, :]
+        r.final[held(c)] = value
+        own_at = pl.ds(aligned(core, n.half) + q * n.cols + at.start, at.size)
+        grads_out[m][:, own_at] = r.final[held(c, core_rows)]
         copy_back(c).start()
 
     back_parts = []
@@ -1086,8 +1072,8 @@
         return remote(
             r.small_out.at[across(k)],
             r.small_in.at[k - 1],
-            r.row_send2.at[k - 1],
-            r.row_recv2.at[k - 1],
+            r.row_send2,
+            r.row_recv2,
             across(k),
             seq_at,
         )
@@ -1096,11 +1082,14 @@
         return remote(
             r.small_mid.at[plane(k)],
             r.small_last.at[k - 1],
-            r.small_send2.at[k - 1],
-            r.small_recv2.at[k - 1],
+            r.small_send2,
+            r.small_recv2,
             batch_at,
             plane(k),
         )
+
+    row_sums_bytes = bytes_of(r.small_in, r.row_send2, r.row_recv2)
+    tile_sums_bytes = bytes_of(r.small_last, r.small_send2, r.small_recv2)
 
     def fold(v):
         return jnp.sum(v.reshape(tall // 8, 8, width), axis=0)
@@ -1129,21 +1118,21 @@
             n.batch // 2, n.seq, 128
         )
         for k in range(1, n.batch):
-            go(row_sums(k))
+            row_sums(k).start()
 
     def small_rows_back():
         value = r.small_out[batch_at]
+        row_sums_bytes.wait_recv()
         for k in range(1, n.batch):
-            row_sums(k).wait_recv()
             value = value + r.small_in[k - 1]
         r.small_mid[...] = value
         for k in range(1, n.seq):
-            go(tile_sums(k))
+            tile_sums(k).start()
 
     def small_end():
         value = r.small_mid[seq_at]
+        tile_sums_bytes.wait_recv()
         for k in range(1, n.seq):
-            tile_sums(k).wait_recv()
             value = value + r.small_last[k - 1]
         r.g_small[...] = value
 
@@ -1160,25 +1149,27 @@
         r.dx[...] = r.dx[...] + r.mixed[...]
 
     for task, *which in (
-        (grad_product, 5), (grad_product, 3), (slope_back, 0), (grad_product, 2),
-        (slope_back, 1), (grad_side, 5), (grad_side, 3), (slope_back, 2), (grad_line, 3),
-        (grad_product, 10), (grad_product, 1), (grad_product, 7), (grad_line, 5),
-        (grad_across, 3), (norm_back,), (grad_out, 3), (grad_side, 10), (grad_side, 1),
-        (grad_side, 7), (grad_product, 9), (grad_side, 2), (grad_line, 10), (grad_product, 8),
-        (grad_product, 6), (grad_line, 7), (grad_across, 10), (grad_line, 1), (grad_line, 2),
-        (grad_product, 0), (grad_across, 7), (grad_across, 5), (grad_side, 6), (turn_back,),
-        (grad_side, 9), (grad_product, 4), (outputs,), (grad_across, 1), (grad_side, 0),
-        (grad_line, 6), (grad_line, 9), (grad_across, 2), (grad_side, 8), (grad_side, 4),
-        (small_grads,), (grad_across, 6), (grad_product, 11), (grad_across, 9), (grad_out, 2),
-        (grad_line, 0), (grad_out, 10), (grad_line, 8), (grad_out, 5), (grad_out, 1),
-        (grad_line, 4), (grad_out, 6), (grad_out, 7), (grad_across, 0), (grad_side, 11),
-        (small_rows_back,), (grad_far, 7), (grad_far, 10), (grad_across, 8), (grad_out, 9),
-        (grad_far, 9), (grad_far, 3), (grad_out, 0), (grad_line, 11), (grad_across, 4),
-        (grad_out, 8), (grad_far, 5), (grad_end, 3), (grad_end, 9), (grad_far, 6), (mix_back,),
-        (grad_end, 7), (grad_out, 4), (small_end,), (grad_far, 4), (grad_end, 5), (grad_far, 0),
-        (grad_across, 11), (grad_end, 10), (grad_out, 11), (grad_far, 1), (grad_far, 2),
-        (grad_end, 4), (grad_far, 8), (grad_far, 11), (grad_end, 2), (grad_end, 0),
-        (grad_end, 6), (grad_end, 1), (grad_end, 8), (grad_end, 11),
+        (grad_product, 3), (grad_product, 4), (slope_back, 2), (grad_product, 10),
+        (slope_back, 0), (grad_side, 4), (grad_side, 3), (slope_back, 1), (grad_line, 4),
+        (grad_product, 2), (grad_product, 8), (grad_line, 3), (norm_back,), (grad_across, 3),
+        (grad_side, 10), (grad_product, 5), (grad_side, 2), (small_grads,), (grad_product, 6),
+        (grad_side, 8), (grad_line, 8), (outputs,), (grad_product, 0), (grad_across, 4),
+        (grad_product, 12), (grad_line, 10), (grad_line, 2), (grad_out, 3), (turn_back,),
+        (grad_side, 0), (grad_across, 10), (grad_product, 9), (grad_side, 12), (grad_side, 6),
+        (grad_out, 10), (grad_line, 0), (grad_across, 2), (grad_side, 5), (grad_out, 4),
+        (grad_across, 8), (grad_product, 1), (grad_far, 3), (grad_side, 9), (grad_product, 11),
+        (grad_line, 6), (grad_across, 6), (grad_line, 12), (small_rows_back,), (grad_across, 0),
+        (grad_product, 7), (grad_line, 5), (grad_side, 11), (grad_line, 9), (grad_far, 4),
+        (grad_side, 1), (grad_out, 8), (grad_across, 5), (grad_across, 9), (grad_out, 6),
+        (grad_side, 7), (grad_out, 0), (grad_across, 12), (grad_line, 1), (grad_out, 2),
+        (grad_out, 9), (grad_across, 1), (grad_far, 8), (grad_far, 0), (grad_far, 10),
+        (grad_end, 0), (grad_out, 5), (mix_back,), (grad_out, 12), (grad_line, 11),
+        (grad_line, 7), (small_end,), (grad_far, 5), (grad_across, 7), (grad_across, 11),
+        (grad_far, 6), (grad_out, 1), (grad_end, 6), (grad_far, 2), (grad_far, 12),
+        (grad_end, 2), (grad_far, 1), (grad_far, 9), (grad_out, 7), (grad_end, 10),
+        (grad_end, 4), (grad_far, 7), (grad_end, 1), (grad_end, 5), (grad_end, 8),
+        (grad_out, 11), (grad_end, 12), (grad_far, 11), (grad_end, 9), (grad_end, 3),
+        (grad_end, 11), (grad_end, 7),
     ):
         task(*which)
 
@@ -1186,59 +1177,50 @@
     r.norm_own[...] = jnp.sum(squares, axis=0, keepdims=True)
     r.norm_all[batch_at * n.seq + seq_at] = r.norm_own[...]
 
-    def norm_copy(i, at):
-        return remote(
-            r.norm_own, r.norm_all.at[at], r.norm_send.at[i], r.norm_recv.at[i], *everyone[i]
-        )
-
-    for i in range(n.devices - 1):
-        go(norm_copy(i, batch_at * n.seq + seq_at))
-    for c in range(2 * n.chunks * n.parts):
+    for device in everyone:
+        remote(
+            r.norm_own,
+            r.norm_all.at[batch_at * n.seq + seq_at],
+            r.norm_send,
+            r.norm_recv,
+            *device,
+        ).start()
+    back_bytes = bytes_of(r.final_in, r.back_send, r.back_recv)
+    back_bytes.wait_recv()
+    for c in range(len(pieces)):
         m, q, at = wide(c)
-        copy_back(c).wait_recv()
-        their_at = pl.ds(aligned(1 - core, n.half) + q * n.cols + at.start, n.thin)
-        grads_out[m][:, their_at] = r.final_in[c]
-    for i in range(n.devices - 1):
-        j = i + 1
-        batch_from = (batch_at + n.batch - j // n.seq) % n.batch
-        seq_from = (seq_at + n.seq - j % n.seq) % n.seq
-        norm_copy(i, batch_from * n.seq + seq_from).wait_recv()
+        their_at = pl.ds(aligned(1 - core, n.half) + q * n.cols + at.start, at.size)
+        grads_out[m][:, their_at] = r.final_in[held(c)]
+    norm_bytes = bytes_of(r.norm_all.at[pl.ds(0, n.devices - 1)], r.norm_send, r.norm_recv)
+    norm_bytes.wait_recv()
     squares = jnp.sum(r.norm_all[...].reshape(n.devices, 128), axis=0, keepdims=True)
     whole = jnp.sum(squares, axis=1, keepdims=True)
     r.norm[...] = jnp.broadcast_to(jnp.sqrt(whole), (8, 128))
 
     for copy in started:
         copy.wait_send()
-
+    for copy in (swapped, tiles_bytes(), rows_bytes(), *(mixed_bytes(i) for i in range(4))):
+        copy.wait_send()
+    for copy in (row_sums_bytes, tile_sums_bytes, back_bytes, norm_bytes):
+        copy.wait_send()
     for c in range(2 * n.chunks):
-        moved = 2 * n.zs + (1 if split(c) else n.zs)
-        slabs_of(c, moved, r.second_recv).wait_send()
-        for far in range(1 + split(c)):
-            own_to_mate(c, far).wait_send()
-
-            @pl.when(inner)
-            def _(c=c, far=far):
-                pair_across(c, far).wait_send()
-                pair_out(c, far).wait_send()
-
-    for c in range(2 * n.chunks * n.parts):
-        copy_back(c).wait_send()
-        copy_diagonal(c).wait_send()
-        copy_near(c).wait_send()
-        (copy_far if back_mode(c) == 1 else copy_side)(c).wait_send()
-        if back_mode(c) == 2:
-            for d in range(1, n.zs):
-                copy_direct(c, d).wait_send()
-        for far in fars(c):
-            copy_mate(c, far).wait_send()
-
-            @pl.when(inner)
-            def _(c=c, far=far):
-                copy_pair_across(c, far).wait_send()
-
-            @pl.when(jnp.logical_not(inner))
-            def _(c=c, far=far):
-                copy_pair_in(c, far).wait_send()
+        slabs_of(c, 2 * n.zs + (3 if split(c) else n.zs + 1), r.side_send).wait_send()
+
+    @pl.when(inner)
+    def _():
+        for c in range(2 * n.chunks):
+            slabs_of(c, 8 if split(c) else 4, r.inner_send).wait_send()
+
+    moved = 2 * n.zs + n.zs + 3
+    bytes_of(out_low.at[:, pl.ds(0, moved * slab)], r.grad_send, r.sides_recv.at[0]).wait_send()
+
+
+def grad_pieces(n):
+    slots = 2 * n.chunks * n.parts
+    halved = len(BACK_KINDS) - slots
+    whole = [(slot, 0, n.thin) for slot in range(slots - halved)]
+    thin = n.thin // 2
+    return whole + [(slot, i * thin, thin) for slot in range(slots - halved, slots) for i in range(2)]
 
 
 def run_layer(n, x, dy, w1, w2, bias, vec):
@@ -1246,7 +1228,6 @@
     tokens, width, cols, q = n.tokens, n.width, n.cols, n.chunks
     grads = 2 * q * n.parts
     splits = max(1, sum(kind // 2 == 1 for kind in BACK_KINDS))
-    directs = max(1, sum(kind // 2 == 2 for kind in BACK_KINDS))
     dma = pltpu.SemaphoreType.DMA
     vmem = pltpu.VMEM
     inputs = dict(bias=bias, vec=vec, x=x, dy=dy, w1=w1, w2=w2)
@@ -1263,31 +1244,29 @@
     scratch.update(
         load_sem=dma((len(LOADS),)),
         stage=vmem((2, n.slab, n.half), F32),
-        swap_send=dma((2,)),
-        swap_recv=dma((2,)),
+        swap_send=dma,
+        swap_recv=dma,
         tile=vmem((8, 128), F32),
         small=vmem((n.batch, n.seq, 8, 128), F32),
-        small_send=dma((n.seq - 1,)),
-        small_recv=dma((n.seq - 1,)),
-        row_send=dma((n.batch - 1,)),
-        row_recv=dma((n.batch - 1,)),
+        small_send=dma,
+        small_recv=dma,
+        row_send=dma,
+        row_recv=dma,
         y_buf=vmem((2, width, tokens), BF16),
         l_buf=vmem((2, n.seq, n.packed, tokens), BF16),
         left=vmem((n.seqs * n.packed, n.length), BF16),
         z_buf=vmem((2, n.seq, n.seqs * n.packed, n.block), BF16),
         r_buf=vmem((2, n.seq, n.seqs * n.packed, n.block), BF16),
-        mix_send=dma((4, n.seq - 1)),
-        mix_recv=dma((4, n.seq - 1)),
+        mix_send=dma((4,)),
+        mix_recv=dma((4,)),
         mixed=vmem((tokens, width), F32),
         full=vmem((2, q, width, cols), BF16),
-        mate_send=dma((2, 2, q)),
-        mate_recv=dma((2, 2, q)),
-        across_send=dma((2, 2, q)),
-        out_send=dma((2, 2, q)),
-        pair_recv=dma((2, 2, q)),
-        side_send=dma((2, q)),
-        first_recv=dma((3, 2, q)),
-        second_recv=dma((2, q)),
+        side_send=dma((2 * q,)),
+        inner_send=dma((2 * q,)),
+        mate_recv=dma((2, 2 * q)),
+        pair_recv=dma((2, 2 * q)),
+        first_recv=dma((3, 2 * q)),
+        second_recv=dma((2 * q,)),
         x_place=vmem((tokens, width), F32),
         dy_place=vmem((tokens, width), F32),
         vecs=vmem((8, width), F32),
@@ -1313,39 +1292,41 @@
         acc=vmem((grads, width, n.thin), F32),
         give=vmem((grads, width, n.thin), BF16),
         in_diagonal=vmem((grads, n.segment, n.thin), BF16),
-        in_near=vmem((grads, n.segment, n.thin), BF16),
-        in_side=vmem((grads, n.segment, n.thin), BF16),
-        in_mate=vmem((grads, n.slab, n.thin), BF16),
+        in_sides=vmem((grads, 2, n.segment, n.thin), BF16),
+        in_end=vmem((grads, n.zs - 1, n.slab, n.thin), BF16),
         in_pair=vmem((grads, 2 * n.slab, n.thin), BF16),
         in_across=vmem((grads, 2 * n.slab, n.thin), BF16),
         far_mate=vmem((splits, n.slab, n.thin), BF16),
         far_pair=vmem((splits, 2 * n.slab, n.thin), BF16),
         far_across=vmem((splits, 2 * n.slab, n.thin), BF16),
-        in_far=vmem((splits, n.slab, n.thin), BF16),
-        in_direct=vmem((n.zs - 1, directs, n.slab, n.thin), BF16),
-        grad_send=dma((8 + n.zs, grads)),
-        grad_recv=dma((8 + n.zs, grads)),
+        grad_send=dma,
+        diagonal_recv=dma((len(BACK_KINDS),)),
+        sides_recv=dma((len(BACK_KINDS),)),
+        end_recv=dma((len(BACK_KINDS),)),
+        pair_in_recv=dma((len(BACK_KINDS),)),
+        across_recv=dma((len(BACK_KINDS),)),
+        far_recv=dma((3, splits)),
         bias_sum=vmem((q, 8, cols), F32),
         dpre=vmem((q, 2 * tokens, cols), BF16),
         dm=vmem((tokens, width), BF16),
         rest=vmem((tokens, width), BF16),
         small_out=vmem((n.batch, n.seq, 8, 128), F32),
         small_in=vmem((n.batch - 1, n.seq, 8, 128), F32),
-        row_send2=dma((n.batch - 1,)),
-        row_recv2=dma((n.batch - 1,)),
+        row_send2=dma,
+        row_recv2=dma,
         small_mid=vmem((n.seq, 8, 128), F32),
         small_last=vmem((n.seq - 1, 8, 128), F32),
-        small_send2=dma((n.seq - 1,)),
-        small_recv2=dma((n.seq - 1,)),
+        small_send2=dma,
+        small_recv2=dma,
         final=vmem((grads, n.slab, n.thin), F32),
         final_in=vmem((grads, n.rows, n.thin), F32),
-        back_send=dma((grads,)),
-        back_recv=dma((grads,)),
+        back_send=dma,
+        back_recv=dma,
         squares=vmem((8, 128), F32),
         norm_own=vmem((1, 128), F32),
         norm_all=vmem((n.devices, 1, 128), F32),
-        norm_send=dma((n.devices - 1,)),
-        norm_recv=dma((n.devices - 1,)),
+        norm_send=dma,
+        norm_recv=dma,
     )
     names = tuple(inputs) + tuple(outputs) + tuple(scratch)
     in_vmem = pl.BlockSpec(memory_space=pltpu.VMEM)

time: 128 us -> 118 us (0.922)
  Pallas kernels: 127 us -> 117 us
    pallas_call x1, Pallas kernels: 124 us -> 114 us  [run_layer(): pl.pallas_call(functools.partial(layer_kernel, n, names), out_shape=[vmem...]
where the time goes in v4:
time: 118 us
  Pallas kernels  117 us (99%)
    pallas_call x1, Pallas kernels, run_layer(): pl.pallas_call(functools.partial(layer_kernel, n, names), out_shape=[vmem...  114 us

profile of v4, /device:TPU:0, one launch (start us, length us, event | category | flops | bytes accessed | tf_op | source)
XLA Modules:
  0.0 117.6 jit_solution(12585953489419419750)
XLA Ops:
  0.7 0.0 copy-start
  0.7 0.0 copy-start.1
  0.7 0.0 copy-start.2
  0.7 0.0 copy-start.3
  0.7 0.0 copy-start.4
  0.7 0.0 copy-start.5
  0.7 0.0 copy-start.6
  0.7 0.0 copy-start.7
  0.7 0.0 copy-start.8
  0.7 0.0 copy-start.9
  0.8 0.0 copy-start.10
  0.8 0.0 copy-start.11
  0.8 114.2 %fused_layer.1 = (bf16[256,768]{1,0:T(8,128)(2,1)S(1)}, f32[256,768]{1,0:T(8,128)S(1)}, f32[24,3072]{1,0:T(8,128)S(1)}, f32[24,3072]{1,0:T(8,128)S(1)}, f32[8,128]{1,0:T(8,128)S(1)}, /*index=5*/f32[8,128]{1,0:T(8,128)S(1)}) custom-call(f32[1,96]{1,0:T(1,128)} %refs_10_.2, f32[5,1,24]{2,1,0:T(1,128)} %bitcast.43, bf16[256,768]{1,0:T(8,128)(2,1)} %bitcast.47, ...), custom_call_target="tpu_custom_call" | custom-call | tf_op jit(solution)/shard_map/fused_layer/pallas_call | solution.py:1334
  115.0 0.0 copy-done
  115.0 0.0 copy-done.1
  115.0 0.0 copy-done.2
  115.0 0.0 copy-done.3
  115.0 0.0 copy-done.4
  115.1 0.0 copy-done.5
  115.1 0.0 copy-done.6
  115.1 0.0 copy-done.7
  115.1 0.0 copy-done.8
  115.1 0.0 copy-done.9
  115.1 2.3 %adam.1 = (f32[1,1]{1,0:T(1,128)}, f32[24,3072]{1,0:T(8,128)}, f32[24,3072]{1,0:T(8,128)}, f32[24,3072]{1,0:T(8,128)}, f32[24,3072]{1,0:T(8,128)}, /*index=5*/f3...) custom-call(f32[24,3072]{1,0:T(8,128)S(1)} %get-tuple-element.36.ref, ...), custom_call_target="tpu_custom_call" | custom-call | tf_op jit(solution)/shard_map/adam/pallas_call | solution.py:1400
  (2 shorter events, 0.0 us)
Async XLA Ops:
  0.7 114.4 %copy-start = (f32[1,24,3072]{2,1,0:T(8,128)S(1)}, f32[1,24,3072]{2,1,0:T(8,128)}, u32[]{:S(2)}) copy-start(f32[1,24,3072]{2,1,0:T(8,128)} %param.25) | copy-start | bytes 884740
  0.7 114.4 %copy-start.1 = (f32[1,3072,24]{1,2,0:T(8,128)S(1)}, f32[1,3072,24]{1,2,0:T(8,128)}, u32[]{:S(2)}) copy-start(f32[1,3072,24]{1,2,0:T(8,128)} %param.26) | copy-start | bytes 884740
  0.7 114.4 %copy-start.2 = (f32[1,24,3072]{2,1,0:T(8,128)S(1)}, f32[1,24,3072]{2,1,0:T(8,128)}, u32[]{:S(2)}) copy-start(f32[1,24,3072]{2,1,0:T(8,128)} %param.29) | copy-start | bytes 884740
  0.7 114.4 %copy-start.3 = (f32[1,24,3072]{2,1,0:T(8,128)S(1)}, f32[1,24,3072]{2,1,0:T(8,128)}, u32[]{:S(2)}) copy-start(f32[1,24,3072]{2,1,0:T(8,128)} %param.30) | copy-start | bytes 884740
  0.7 114.4 %copy-start.4 = (f32[1,3072,24]{1,2,0:T(8,128)S(1)}, f32[1,3072,24]{1,2,0:T(8,128)}, u32[]{:S(2)}) copy-start(f32[1,3072,24]{1,2,0:T(8,128)} %param.31) | copy-start | bytes 884740
  0.7 114.4 %copy-start.5 = (f32[1,3072,24]{1,2,0:T(8,128)S(1)}, f32[1,3072,24]{1,2,0:T(8,128)}, u32[]{:S(2)}) copy-start(f32[1,3072,24]{1,2,0:T(8,128)} %param.32) | copy-start | bytes 884740
  0.7 114.4 %copy-start.6 = (f32[1,5,24]{2,0,1:T(1,128)S(1)}, f32[1,5,24]{2,0,1:T(1,128)}, u32[]{:S(2)}) copy-start(f32[1,5,24]{2,0,1:T(1,128)} %param.28) | copy-start | bytes 1444
  0.7 114.4 %copy-start.7 = (f32[1,5,24]{2,0,1:T(1,128)S(1)}, f32[1,5,24]{2,0,1:T(1,128)}, u32[]{:S(2)}) copy-start(f32[1,5,24]{2,0,1:T(1,128)} %param.35) | copy-start | bytes 1444
  0.7 114.4 %copy-start.8 = (f32[1,5,24]{2,0,1:T(1,128)S(1)}, f32[1,5,24]{2,0,1:T(1,128)}, u32[]{:S(2)}) copy-start(f32[1,5,24]{2,0,1:T(1,128)} %param.36) | copy-start | bytes 1444
  0.7 114.4 %copy-start.9 = (f32[1,96]{1,0:T(1,128)S(1)}, f32[1,96]{1,0:T(1,128)}, u32[]{:S(2)}) copy-start(f32[1,96]{1,0:T(1,128)} %refs_10_.2) | copy-start | bytes 1156
  0.8 114.4 %copy-start.10 = (f32[1,96]{1,0:T(1,128)S(1)}, f32[1,96]{1,0:T(1,128)}, u32[]{:S(2)}) copy-start(f32[1,96]{1,0:T(1,128)} %refs_11_.2) | copy-start | bytes 1156
  0.8 114.4 %copy-start.11 = (f32[1,96]{1,0:T(1,128)S(1)}, f32[1,96]{1,0:T(1,128)}, u32[]{:S(2)}) copy-start(f32[1,96]{1,0:T(1,128)} %refs_12_.2) | copy-start | bytes 1156

commit v5 on v4

--- a/solution.py
+++ b/solution.py
@@ -263,6 +263,7 @@
             and self.rows <= 128
             and self.bias <= 128
             and 5 * self.rows <= self.width
+            and self.hidden == 4 * self.width
         )
 
     def owner(self, x, core, z, y):
@@ -349,8 +350,8 @@
     un_b="un_v",
 )
 LATER = ("tt_b", "un_b")
-FORWARD_KINDS = (1, 1, 0, 0, 0, 3)
-BACK_KINDS = (0, 5, 0, 5, 2, 1, 1, 5, 3, 5, 5, 4, 0)
+FORWARD_KINDS = (1, 1, 1, 1, 0, 2)
+BACK_KINDS = (4, 6, 1, 1, 0, 0, 5, 5, 5, 1, 5, 0)
 
 
 def layer_kernel(n, names, *refs):
@@ -359,7 +360,6 @@
     x, core = batch_at // 2, batch_at % 2
     z, y = seq_at // 2, seq_at % 2
     tokens, width, seg, slab = n.tokens, n.width, n.segment, n.slab
-    started = []
 
     def aligned(at, by):
         return pl.multiple_of(at * by, by)
@@ -377,11 +377,6 @@
             device_id_type=MESH,
         )
 
-    def go(copy):
-        copy.start()
-        started.append(copy)
-        return copy
-
     def bytes_of(view, send, recv):
         return remote(view, view, send, recv, other_core, seq_at)
 
@@ -402,8 +397,10 @@
         return (batch_at + n.batch - k) % n.batch
 
     loads = types.SimpleNamespace()
-    for i, (name, held) in enumerate(LOADS.items()):
-        load = pltpu.make_async_copy(getattr(r, name), getattr(r, held), r.load_sem.at[i])
+    for name, held in LOADS.items():
+        load = pltpu.make_async_copy(
+            getattr(r, name), getattr(r, held), r.load_sem.at[sorted(set(LOADS.values())).index(held)]
+        )
         setattr(loads, name, load)
         if name not in LATER:
             load.start()
@@ -428,12 +425,14 @@
         remote(
             weights[m].at[:, give],
             r.stage.at[m, core_rows],
-            r.swap_send,
-            r.swap_recv,
+            r.swap_send.at[m],
+            r.swap_recv.at[m],
             other_core,
             seq_at,
         ).start()
-    swapped = bytes_of(r.stage.at[:, pl.ds(0, n.rows)], r.swap_send, r.swap_recv)
+
+    def swapped(m):
+        return bytes_of(r.stage.at[m, pl.ds(0, n.rows)], r.swap_send.at[m], r.swap_recv.at[m])
 
     def mix_start(t, source, table):
         y_ref, l_ref = r.y_buf.at[t], r.l_buf.at[t]
@@ -446,7 +445,7 @@
             remote(
                 y_ref.at[rows_of(plane(k), n.packed)],
                 l_ref.at[seq_at],
-                r.mix_send.at[2 * t],
+                r.mix_send.at[0],
                 r.mix_recv.at[2 * t],
                 batch_at,
                 plane(k),
@@ -454,7 +453,7 @@
 
     def mixed_bytes(i):
         into = (r.l_buf, r.r_buf)[i % 2].at[i // 2, pl.ds(0, n.seq - 1)]
-        return bytes_of(into, r.mix_send.at[i], r.mix_recv.at[i])
+        return bytes_of(into, r.mix_send.at[i % 2], r.mix_recv.at[i])
 
     def mix_turn(t):
         l_ref, z_ref, r_ref = r.l_buf.at[t], r.z_buf.at[t], r.r_buf.at[t]
@@ -483,7 +482,7 @@
             remote(
                 z_ref.at[plane(k)],
                 r_ref.at[seq_at],
-                r.mix_send.at[2 * t + 1],
+                r.mix_send.at[1],
                 r.mix_recv.at[2 * t + 1],
                 batch_at,
                 plane(k),
@@ -538,19 +537,16 @@
     def place(c):
         return c // n.chunks, c % n.chunks
 
-    def stage_weights():
-        for m in range(2):
-            r.stage[m, core_rows, :] = weights[m][:, keep]
-        swapped.wait_recv()
-        for m in range(2):
-            for q in range(n.chunks):
-                full[m, q, slab_rows(x, y, z), :] = r.stage[
-                    m, :, q * n.cols : (q + 1) * n.cols
-                ].astype(BF16)
+    def stage_weights(m):
+        r.stage[m, core_rows, :] = weights[m][:, keep]
+        swapped(m).wait_recv()
+        for q in range(n.chunks):
+            columns = r.stage[m, :, q * n.cols : (q + 1) * n.cols]
+            full[m, q, slab_rows(x, y, z), :] = columns.astype(BF16)
 
     def full_copy(c, at, send, recv, to):
         m, q = place(c)
-        return remote(full.at[m, q, at], full.at[m, q, at], send.at[c], recv, *to)
+        return remote(full.at[m, q, at], full.at[m, q, at], send, recv, *to)
 
     def rows_at(sx, sy, i):
         return (slab_rows(sx, sy, z), slab_rows(sx, sy, mate_z), pair_rows(sx, sy, 1 - pair_z))[i]
@@ -565,24 +561,27 @@
             side_copy(c, i, x, y, True).start()
         side_copy(c, i, x, y, False).start()
 
+    def line_slot(c, far):
+        return 2 * n.chunks + sum(split(d) for d in range(c)) if far else c
+
     def line_seg(c, far):
         return away(turn_of(c)) if far else (x, y)
 
     def own_to_mate(c, far):
         at = rows_at(*line_seg(c, far), 0)
-        return full_copy(c, at, r.side_send, r.mate_recv.at[far, c], line(mate_z))
+        return full_copy(c, at, r.side_send, r.mate_recv.at[line_slot(c, far)], line(mate_z))
 
     def mate_arrives(c, far):
         at = rows_at(*line_seg(c, far), 1)
-        full_copy(c, at, r.side_send, r.mate_recv.at[far, c], line(mate_z)).wait_recv()
+        full_copy(c, at, r.side_send, r.mate_recv.at[line_slot(c, far)], line(mate_z)).wait_recv()
 
     def pair_across(c, far):
         at = pair_rows(*line_seg(c, far), pair_z)
-        return full_copy(c, at, r.inner_send, r.pair_recv.at[far, c], line(n.zs - 1 - z))
+        return full_copy(c, at, r.inner_send, r.pair_recv.at[line_slot(c, far)], line(n.zs - 1 - z))
 
     def pair_out(c, far):
         at = rows_at(*line_seg(c, far), 2)
-        return full_copy(c, at, r.inner_send, r.pair_recv.at[far, c], line(mate_z))
+        return full_copy(c, at, r.inner_send, r.pair_recv.at[line_slot(c, far)], line(mate_z))
 
     def own_sides(c):
         to_sides(c, 0)
@@ -623,12 +622,14 @@
                 (from_mate, from_pair)[i - 1](c, 1)
         side_copy(c, i, ax, ay, False).start()
 
-    def slabs_of(c, count, send):
+    def weights_here(c):
         m, q = place(c)
-        return bytes_of(full.at[m, q, pl.ds(0, count * slab)], send.at[c], r.second_recv.at[c])
-
-    def weights_here(c):
-        slabs_of(c, 2 * n.zs, r.side_send).wait_recv()
+        second = full.at[m, q, pl.ds(0, 2 * n.zs * slab)]
+        bytes_of(second, r.side_send, r.second_recv.at[c]).wait_recv()
+
+    def all_slabs(counts, send):
+        rows = sum(counts) * slab // (2 * n.chunks)
+        return bytes_of(full.at[:, :, pl.ds(0, rows)], send, r.second_recv.at[0])
 
     def small_tiles():
         loads.bias.wait()
@@ -730,7 +731,7 @@
         r.h_low[at, :] = h.astype(BF16)
 
     def swap(i, src, dst):
-        return remote(src, dst, r.core_send.at[i], r.core_recv.at[i], other_core, seq_at)
+        return remote(src, dst, r.core_send, r.core_recv.at[i], other_core, seq_at)
 
     def swap_h():
         return swap(0, r.h_low.at[mine], r.h_low.at[theirs])
@@ -741,7 +742,7 @@
         loads.tt_b.start()
         loads.un_b.start()
         row_loop(first_norm)
-        go(swap_h())
+        swap_h().start()
 
     root = math.sqrt(2.0 / math.pi)
 
@@ -779,7 +780,7 @@
             part = r.total[half, :] + part if len(gathered_parts) > 1 else part
             if len(gathered_parts) == n.chunks and half is theirs:
                 r.part_low[...] = part.astype(BF16)
-                go(swap_ff())
+                swap_ff().start()
             else:
                 r.total[half, :] = part
 
@@ -787,17 +788,17 @@
         mix_send(0)
 
     forward_steps = (
-        (send_forward,), (stage_weights,), (own_sides, 0), (own_sides, 1), (own_line, 1),
-        (own_sides, 4), (own_sides, 2), (own_line, 0), (own_line, 2), (place_inputs,),
-        (own_sides, 3), (own_sides, 5), (small_tiles,), (own_line, 4), (own_line, 5),
-        (pass_on, 0, 0), (mate_in, 1), (mate_in, 0), (pass_on, 3, 0), (mate_in, 2),
-        (own_line, 3), (mate_in, 4), (pass_on, 1, 0), (small_rows,), (pass_on, 5, 0),
-        (pass_on, 0, 1), (pass_on, 4, 0), (pass_on, 2, 0), (pair_in, 1), (mate_in, 3),
-        (pair_in, 0), (pair_in, 2), (mate_in, 5), (pass_on, 1, 1), (pass_on, 4, 1),
-        (small_vectors,), (turn_forward,), (pass_on, 2, 1), (pass_on, 1, 2), (pair_in, 3),
-        (pass_on, 5, 1), (pass_on, 2, 2), (pass_on, 3, 1), (pair_in, 4), (pair_in, 5),
-        (pass_on, 0, 2), (norm_forward,), (pass_on, 5, 2), (pass_on, 4, 2), (lift, 1),
-        (lift, 2), (pass_on, 3, 2), (lift, 0), (drop, 1), (drop, 2), (drop, 0),
+        (send_forward,), (stage_weights, 0), (own_sides, 1), (own_sides, 0), (own_line, 2),
+        (own_sides, 2), (own_line, 1), (own_line, 0), (stage_weights, 1), (own_sides, 4),
+        (own_sides, 3), (place_inputs,), (own_line, 3), (own_sides, 5), (own_line, 4),
+        (pass_on, 1, 0), (small_tiles,), (pass_on, 0, 0), (mate_in, 2), (mate_in, 1),
+        (pass_on, 5, 0), (pass_on, 2, 0), (own_line, 5), (mate_in, 0), (pass_on, 4, 0),
+        (mate_in, 3), (mate_in, 4), (pass_on, 2, 1), (pass_on, 3, 0), (pair_in, 2),
+        (small_rows,), (pass_on, 1, 1), (pair_in, 1), (pass_on, 5, 1), (turn_forward,),
+        (pass_on, 0, 1), (mate_in, 5), (pass_on, 3, 1), (pair_in, 0), (pass_on, 4, 1),
+        (pass_on, 2, 2), (pair_in, 4), (small_vectors,), (pass_on, 1, 2), (pair_in, 3),
+        (pass_on, 5, 2), (pass_on, 0, 2), (norm_forward,), (pass_on, 4, 2), (pair_in, 5),
+        (pass_on, 3, 2), (lift, 1), (lift, 2), (lift, 0), (drop, 1), (drop, 0), (drop, 2),
     )
     for task, *which in forward_steps:
         task(*which)
@@ -822,7 +823,8 @@
         r.dz[at, :] = dv.astype(BF16)
 
     row_loop(second_norm)
-    swap_dz = go(swap(2, r.dz.at[mine], r.dz.at[theirs]))
+    swap_dz = swap(2, r.dz.at[mine], r.dz.at[theirs])
+    swap_dz.start()
     swap_dz.wait_recv()
 
     acc, out_low = r.acc, r.give
@@ -866,6 +868,9 @@
 
     def back_seg(c, far):
         return away(back_turn(c)) if far else (x, y)
+
+    def tree_slot(c):
+        return sum(kind // 2 < 2 for kind in BACK_KINDS[:c])
 
     def line_into(c, far, i):
         if far:
@@ -878,7 +883,7 @@
         if far:
             recv = r.far_recv.at[i, back_slot(c)]
         else:
-            recv = (r.end_recv, r.pair_in_recv, r.across_recv)[i].at[c]
+            recv = r.end_recv.at[c] if i == 0 else r.tree_recv.at[i - 1, tree_slot(c)]
         return grad_copy(c, at, line_into(c, far, i), recv, to)
 
     def copy_mate(c, far):
@@ -908,6 +913,88 @@
         for ref in more:
             value = value + ref[...].astype(F32)
         out_low[held(c, at)] = value.astype(BF16)
+
+    four = [(sx, sy) for sy in range(n.ys) for sx in range(n.xs)]
+
+    def first_copy(c, i, which):
+        sx, sy = four[i]
+        slot, lanes = back_slot(c), pl.ds(0, pieces[c][2])
+        if which == 0:
+            at, to = slab_rows(sx, sy, mate_z), line(mate_z)
+        else:
+            at, to = pair_rows(sx, sy, 1 - pair_z), line((0, mate_z, n.zs - 1 - z)[which])
+        into = (r.first_mate, r.first_pair, r.first_across)[which].at[slot, i, :, lanes]
+        return grad_copy(c, at, into, r.line_recv.at[which, slot], to)
+
+    def first_wait(c, which):
+        slot, lanes = back_slot(c), pl.ds(0, pieces[c][2])
+        into = (r.first_mate, r.first_pair, r.first_across)[which].at[slot, :, :, lanes]
+        bytes_of(into, r.grad_send, r.line_recv.at[which, slot]).wait_recv()
+
+    def first_start(c):
+        @pl.when(jnp.logical_not(inner))
+        def _():
+            for i, (sx, sy) in enumerate(four):
+                round_out(c, pair_rows(sx, sy, 1 - pair_z))
+                first_copy(c, i, 1).start()
+            for i, (sx, sy) in enumerate(four):
+                round_out(c, slab_rows(sx, sy, mate_z))
+                first_copy(c, i, 0).start()
+
+    def first_across(c):
+        @pl.when(inner)
+        def _():
+            first_wait(c, 1)
+            for i, (sx, sy) in enumerate(four):
+                lanes = pl.ds(0, pieces[c][2])
+                more = r.first_pair.at[back_slot(c), i, :, lanes]
+                round_out(c, pair_rows(sx, sy, 1 - pair_z), more)
+                first_copy(c, i, 2).start()
+
+    def first_out(c):
+        @pl.when(inner)
+        def _():
+            first_wait(c, 2)
+            for i, (sx, sy) in enumerate(four):
+                at = held(c, pair_rows(sx, sy, pair_z))
+                lanes = pl.ds(0, pieces[c][2])
+                acc[at] = acc[at] + r.first_across[back_slot(c), i, :, lanes].astype(F32)
+                round_out(c, slab_rows(sx, sy, mate_z))
+                first_copy(c, i, 0).start()
+
+    def slab_copy(c, i):
+        t = back_turn(c)
+        sx, sy = ((1 - x, 1 - y), away(1 - t), away(t))[i]
+        own = pl.ds(0, slab)
+        into = (
+            r.in_diagonal.at[held(c, own)] if i == 0 else r.in_sides.at[held(c, own, lead=(i - 1,))]
+        )
+        recv = r.diagonal_recv if i == 0 else r.sides_recv
+        return grad_copy(c, slab_rows(sx, sy, z), into, recv.at[c], peer(t if i == 2 else 1 - t))
+
+    def slabs_near(c):
+        first_wait(c, 0)
+        lanes = pl.ds(0, pieces[c][2])
+        for i, (sx, sy) in enumerate(four):
+            at = held(c, slab_rows(sx, sy, z))
+            acc[at] = acc[at] + r.first_mate[back_slot(c), i, :, lanes].astype(F32)
+        t = back_turn(c)
+        for i, seg_at in enumerate(((1 - x, 1 - y), away(1 - t))):
+            round_out(c, slab_rows(*seg_at, z))
+            slab_copy(c, i).start()
+
+    def slabs_side(c):
+        slab_copy(c, 0).wait_recv()
+        own = pl.ds(0, slab)
+        round_out(c, slab_rows(*away(back_turn(c)), z), r.in_diagonal.at[held(c, own)])
+        slab_copy(c, 2).start()
+
+    def slabs_end(c):
+        own = pl.ds(0, slab)
+        both = r.in_sides.at[held(c, own, lead=(pl.ds(0, 2),))]
+        bytes_of(both, r.grad_send, r.sides_recv.at[c]).wait_recv()
+        value = acc[held(c, slab_rows(x, y, z))]
+        return value + sum(r.in_sides[held(c, own, lead=(i,))].astype(F32) for i in range(2))
 
     def grad_product(c):
         m, q, at = wide(c)
@@ -915,6 +1002,9 @@
             acc[held(c)] = dot(r.dz[...], r.act[q, :, at], TN)
         else:
             acc[held(c)] = dot(r.h_low[...], r.dpre[q, :, at], TN)
+        if back_mode(c) == 3:
+            first_start(c)
+            return
         round_out(c, seg_rows(1 - x, 1 - y))
         copy_diagonal(c).start()
         round_out(c, seg_rows(*away(1 - back_turn(c))))
@@ -930,6 +1020,9 @@
             copy_mate(c, far).start()
 
     def grad_side(c):
+        if back_mode(c) == 3:
+            first_across(c)
+            return
         copy_diagonal(c).wait_recv()
         at = seg_rows(*away(back_turn(c)))
         if back_mode(c) == 1:
@@ -940,6 +1033,9 @@
             copy_side(c).start()
 
     def grad_line(c):
+        if back_mode(c) == 3:
+            first_out(c)
+            return
         sides = 1 if back_mode(c) == 1 else 2
         both = r.in_sides.at[held(c, lead=(pl.ds(0, sides),))]
         bytes_of(both, r.grad_send, r.sides_recv.at[c]).wait_recv()
@@ -954,9 +1050,11 @@
             line_start(c, 0)
 
     def fars(c):
-        return range((1, 2, 0)[back_mode(c)])
+        return range((1, 2, 0, 0)[back_mode(c)])
 
     def grad_across(c):
+        if back_mode(c) == 3:
+            slabs_near(c)
         for far in fars(c):
 
             @pl.when(inner)
@@ -967,6 +1065,8 @@
                 copy_pair_across(c, far).start()
 
     def grad_out(c):
+        if back_mode(c) == 3:
+            slabs_side(c)
         for far in fars(c):
 
             @pl.when(inner)
@@ -1004,12 +1104,15 @@
 
     def grad_end(c):
         m, q, at = wide(c)
-        value = acc[held(c, slab_rows(x, y, z))]
-        ends = back_mode(c) + 1
-        all_ends = r.in_end.at[held(c, lead=(pl.ds(0, ends),))]
-        bytes_of(all_ends, r.grad_send, r.end_recv.at[c]).wait_recv()
-        for i in range(ends):
-            value = value + r.in_end[held(c, lead=(i,))].astype(F32)
+        if back_mode(c) == 3:
+            value = slabs_end(c)
+        else:
+            value = acc[held(c, slab_rows(x, y, z))]
+            ends = back_mode(c) + 1
+            all_ends = r.in_end.at[held(c, lead=(pl.ds(0, ends),))]
+            bytes_of(all_ends, r.grad_send, r.end_recv.at[c]).wait_recv()
+            for i in range(ends):
+                value = value + r.in_end[held(c, lead=(i,))].astype(F32)
         r.squares[...] += squares_of(value)
         r.final[held(c)] = value
         own_at = pl.ds(aligned(core, n.half) + q * n.cols + at.start, at.size)
@@ -1035,7 +1138,7 @@
             part = r.total[half, :] + part if len(back_parts) > 1 else part
             if len(back_parts) == n.chunks and half is theirs:
                 r.part_low2[...] = part.astype(BF16)
-                go(swap_dh())
+                swap_dh().start()
             else:
                 r.total[half, :] = part
 
@@ -1149,27 +1252,25 @@
         r.dx[...] = r.dx[...] + r.mixed[...]
 
     for task, *which in (
-        (grad_product, 3), (grad_product, 4), (slope_back, 2), (grad_product, 10),
-        (slope_back, 0), (grad_side, 4), (grad_side, 3), (slope_back, 1), (grad_line, 4),
-        (grad_product, 2), (grad_product, 8), (grad_line, 3), (norm_back,), (grad_across, 3),
-        (grad_side, 10), (grad_product, 5), (grad_side, 2), (small_grads,), (grad_product, 6),
-        (grad_side, 8), (grad_line, 8), (outputs,), (grad_product, 0), (grad_across, 4),
-        (grad_product, 12), (grad_line, 10), (grad_line, 2), (grad_out, 3), (turn_back,),
-        (grad_side, 0), (grad_across, 10), (grad_product, 9), (grad_side, 12), (grad_side, 6),
-        (grad_out, 10), (grad_line, 0), (grad_across, 2), (grad_side, 5), (grad_out, 4),
-        (grad_across, 8), (grad_product, 1), (grad_far, 3), (grad_side, 9), (grad_product, 11),
-        (grad_line, 6), (grad_across, 6), (grad_line, 12), (small_rows_back,), (grad_across, 0),
-        (grad_product, 7), (grad_line, 5), (grad_side, 11), (grad_line, 9), (grad_far, 4),
-        (grad_side, 1), (grad_out, 8), (grad_across, 5), (grad_across, 9), (grad_out, 6),
-        (grad_side, 7), (grad_out, 0), (grad_across, 12), (grad_line, 1), (grad_out, 2),
-        (grad_out, 9), (grad_across, 1), (grad_far, 8), (grad_far, 0), (grad_far, 10),
-        (grad_end, 0), (grad_out, 5), (mix_back,), (grad_out, 12), (grad_line, 11),
-        (grad_line, 7), (small_end,), (grad_far, 5), (grad_across, 7), (grad_across, 11),
-        (grad_far, 6), (grad_out, 1), (grad_end, 6), (grad_far, 2), (grad_far, 12),
-        (grad_end, 2), (grad_far, 1), (grad_far, 9), (grad_out, 7), (grad_end, 10),
-        (grad_end, 4), (grad_far, 7), (grad_end, 1), (grad_end, 5), (grad_end, 8),
-        (grad_out, 11), (grad_end, 12), (grad_far, 11), (grad_end, 9), (grad_end, 3),
-        (grad_end, 11), (grad_end, 7),
+        (grad_product, 4), (grad_product, 2), (grad_product, 1), (slope_back, 2),
+        (grad_product, 11), (grad_product, 3), (slope_back, 1), (slope_back, 0), (grad_side, 1),
+        (grad_side, 2), (grad_product, 6), (norm_back,), (grad_side, 3), (grad_product, 7),
+        (grad_line, 2), (grad_side, 4), (grad_side, 6), (outputs,), (grad_product, 10),
+        (grad_side, 7), (grad_product, 5), (grad_line, 3), (grad_line, 1), (grad_across, 2),
+        (grad_line, 6), (grad_product, 9), (grad_line, 4), (grad_across, 3), (grad_line, 7),
+        (grad_side, 11), (grad_side, 10), (grad_across, 6), (grad_across, 7), (grad_out, 6),
+        (turn_back,), (grad_out, 3), (grad_across, 4), (grad_side, 5), (grad_product, 8),
+        (grad_side, 9), (grad_out, 7), (grad_far, 7), (grad_product, 0), (grad_out, 2),
+        (grad_far, 2), (grad_line, 11), (grad_line, 5), (small_grads,), (grad_across, 11),
+        (grad_line, 9), (grad_far, 6), (grad_side, 8), (grad_line, 10), (grad_across, 5),
+        (grad_across, 10), (grad_side, 0), (grad_out, 11), (grad_out, 10), (grad_end, 2),
+        (grad_far, 10), (small_rows_back,), (grad_across, 9), (grad_across, 1), (grad_out, 4),
+        (grad_line, 8), (grad_across, 8), (grad_end, 10), (grad_out, 5), (small_end,),
+        (grad_end, 7), (grad_line, 0), (grad_out, 8), (grad_out, 1), (grad_out, 9),
+        (grad_far, 11), (grad_far, 4), (grad_far, 8), (grad_far, 3), (grad_far, 1),
+        (grad_far, 5), (grad_across, 0), (grad_end, 1), (grad_end, 4), (grad_far, 9),
+        (grad_end, 6), (grad_end, 8), (grad_out, 0), (grad_end, 5), (grad_far, 0),
+        (grad_end, 3), (mix_back,), (grad_end, 11), (grad_end, 9), (grad_end, 0),
     ):
         task(*which)
 
@@ -1197,19 +1298,21 @@
     whole = jnp.sum(squares, axis=1, keepdims=True)
     r.norm[...] = jnp.broadcast_to(jnp.sqrt(whole), (8, 128))
 
-    for copy in started:
+    bytes_of(r.act, r.core_send, r.core_recv.at[0]).wait_send()
+    for copy in (tiles_bytes(), rows_bytes(), *(swapped(m) for m in range(2))):
         copy.wait_send()
-    for copy in (swapped, tiles_bytes(), rows_bytes(), *(mixed_bytes(i) for i in range(4))):
-        copy.wait_send()
+    for i, into in enumerate((r.l_buf, r.r_buf)):
+        both = into.at[:, pl.ds(0, n.seq - 1)]
+        bytes_of(both, r.mix_send.at[i], r.mix_recv.at[i]).wait_send()
     for copy in (row_sums_bytes, tile_sums_bytes, back_bytes, norm_bytes):
         copy.wait_send()
-    for c in range(2 * n.chunks):
-        slabs_of(c, 2 * n.zs + (3 if split(c) else n.zs + 1), r.side_send).wait_send()
+    weight_chunks = range(2 * n.chunks)
+    sent = [2 * n.zs + (3 if split(c) else n.zs + 1) for c in weight_chunks]
+    all_slabs(sent, r.side_send).wait_send()
 
     @pl.when(inner)
     def _():
-        for c in range(2 * n.chunks):
-            slabs_of(c, 8 if split(c) else 4, r.inner_send).wait_send()
+        all_slabs([8 if split(c) else 4 for c in weight_chunks], r.inner_send).wait_send()
 
     moved = 2 * n.zs + n.zs + 3
     bytes_of(out_low.at[:, pl.ds(0, moved * slab)], r.grad_send, r.sides_recv.at[0]).wait_send()
@@ -1227,7 +1330,9 @@
     tables = host_tables(n)
     tokens, width, cols, q = n.tokens, n.width, n.cols, n.chunks
     grads = 2 * q * n.parts
+    far_chunks = sum(kind // 2 == 1 for kind in FORWARD_KINDS)
     splits = max(1, sum(kind // 2 == 1 for kind in BACK_KINDS))
+    firsts = max(1, sum(kind // 2 == 3 for kind in BACK_KINDS))
     dma = pltpu.SemaphoreType.DMA
     vmem = pltpu.VMEM
     inputs = dict(bias=bias, vec=vec, x=x, dy=dy, w1=w1, w2=w2)
@@ -1242,10 +1347,10 @@
     )
     scratch = {held: vmem(inputs[name].shape, inputs[name].dtype) for name, held in LOADS.items()}
     scratch.update(
-        load_sem=dma((len(LOADS),)),
+        load_sem=dma((len(set(LOADS.values())),)),
         stage=vmem((2, n.slab, n.half), F32),
-        swap_send=dma,
-        swap_recv=dma,
+        swap_send=dma((2,)),
+        swap_recv=dma((2,)),
         tile=vmem((8, 128), F32),
         small=vmem((n.batch, n.seq, 8, 128), F32),
         small_send=dma,
@@ -1257,14 +1362,14 @@
         left=vmem((n.seqs * n.packed, n.length), BF16),
         z_buf=vmem((2, n.seq, n.seqs * n.packed, n.block), BF16),
         r_buf=vmem((2, n.seq, n.seqs * n.packed, n.block), BF16),
-        mix_send=dma((4,)),
+        mix_send=dma((2,)),
         mix_recv=dma((4,)),
         mixed=vmem((tokens, width), F32),
         full=vmem((2, q, width, cols), BF16),
-        side_send=dma((2 * q,)),
-        inner_send=dma((2 * q,)),
-        mate_recv=dma((2, 2 * q)),
-        pair_recv=dma((2, 2 * q)),
+        side_send=dma,
+        inner_send=dma,
+        mate_recv=dma((2 * q + far_chunks,)),
+        pair_recv=dma((2 * q + far_chunks,)),
         first_recv=dma((3, 2 * q)),
         second_recv=dma((2 * q,)),
         x_place=vmem((tokens, width), F32),
@@ -1275,7 +1380,7 @@
         scale1=vmem((tokens, 128), F32),
         h=vmem((tokens, width), F32),
         h_low=vmem((2 * tokens, width), BF16),
-        core_send=dma((4,)),
+        core_send=dma,
         core_recv=dma((4,)),
         total=vmem((2 * tokens, width), F32),
         act=vmem((q, 2 * tokens, cols), BF16),
@@ -1299,12 +1404,15 @@
         far_mate=vmem((splits, n.slab, n.thin), BF16),
         far_pair=vmem((splits, 2 * n.slab, n.thin), BF16),
         far_across=vmem((splits, 2 * n.slab, n.thin), BF16),
+        first_mate=vmem((firsts, 4, n.slab, n.thin), BF16),
+        first_pair=vmem((firsts, 4, 2 * n.slab, n.thin), BF16),
+        first_across=vmem((firsts, 4, 2 * n.slab, n.thin), BF16),
+        line_recv=dma((3, firsts)),
         grad_send=dma,
         diagonal_recv=dma((len(BACK_KINDS),)),
         sides_recv=dma((len(BACK_KINDS),)),
         end_recv=dma((len(BACK_KINDS),)),
-        pair_in_recv=dma((len(BACK_KINDS),)),
-        across_recv=dma((len(BACK_KINDS),)),
+        tree_recv=dma((2, max(1, sum(kind // 2 < 2 for kind in BACK_KINDS)))),
         far_recv=dma((3, splits)),
         bias_sum=vmem((q, 8, cols), F32),
         dpre=vmem((q, 2 * tokens, cols), BF16),

time: 118 us -> 115 us (0.975)
  Pallas kernels: 117 us -> 113 us
    pallas_call x1, Pallas kernels: 114 us -> 111 us  [run_layer(): pl.pallas_call(functools.partial(layer_kernel, n, names), out_shape=[vmem...]
where the time goes in v5:
time: 115 us
  Pallas kernels  113 us (98%)
    pallas_call x1, Pallas kernels, run_layer(): pl.pallas_call(functools.partial(layer_kernel, n, names), out_shape=[vmem...  111 us

profile of v5, /device:TPU:0, one launch (start us, length us, event | category | flops | bytes accessed | tf_op | source)
XLA Modules:
  0.0 114.5 jit_solution(8193105584776427231)
XLA Ops:
  0.7 0.0 copy-start
  0.7 0.0 copy-start.1
  0.7 0.0 copy-start.2
  0.7 0.0 copy-start.3
  0.7 0.0 copy-start.4
  0.7 0.0 copy-start.5
  0.7 0.0 copy-start.6
  0.7 0.0 copy-start.7
  0.7 0.0 copy-start.8
  0.7 0.0 copy-start.9
  0.8 111.2 %fused_layer.1 = (bf16[256,768]{1,0:T(8,128)(2,1)S(1)}, f32[256,768]{1,0:T(8,128)S(1)}, f32[24,3072]{1,0:T(8,128)S(1)}, f32[24,3072]{1,0:T(8,128)S(1)}, f32[8,128]{1,0:T(8,128)S(1)}, /*index=5*/f32[8,128]{1,0:T(8,128)S(1)}) custom-call(f32[1,96]{1,0:T(1,128)} %refs_10_.2, f32[5,1,24]{2,1,0:T(1,128)} %bitcast.43, bf16[256,768]{1,0:T(8,128)(2,1)} %bitcast.47, ...), custom_call_target="tpu_custom_call" | custom-call | tf_op jit(solution)/shard_map/fused_layer/pallas_call | solution.py:1442
  111.9 0.0 copy-done
  111.9 0.0 copy-done.1
  111.9 0.0 copy-done.2
  112.0 0.0 copy-done.3
  112.0 0.0 copy-done.4
  112.0 0.0 copy-done.5
  112.0 0.0 copy-done.6
  112.0 0.0 copy-done.7
  112.0 0.0 copy-done.8
  112.0 0.0 copy-done.9
  112.0 0.0 copy-done.10
  112.0 0.0 copy-done.11
  112.0 2.3 %adam.1 = (f32[1,1]{1,0:T(1,128)}, f32[24,3072]{1,0:T(8,128)}, f32[24,3072]{1,0:T(8,128)}, f32[24,3072]{1,0:T(8,128)}, f32[24,3072]{1,0:T(8,128)}, /*index=5*/f3...) custom-call(f32[24,3072]{1,0:T(8,128)S(1)} %get-tuple-element.36.ref, ...), custom_call_target="tpu_custom_call" | custom-call | tf_op jit(solution)/shard_map/adam/pallas_call | solution.py:1508
  (2 shorter events, 0.0 us)
Async XLA Ops:
  0.7 111.3 %copy-start = (f32[1,24,3072]{2,1,0:T(8,128)S(1)}, f32[1,24,3072]{2,1,0:T(8,128)}, u32[]{:S(2)}) copy-start(f32[1,24,3072]{2,1,0:T(8,128)} %param.25) | copy-start | bytes 884740
  0.7 111.3 %copy-start.1 = (f32[1,3072,24]{1,2,0:T(8,128)S(1)}, f32[1,3072,24]{1,2,0:T(8,128)}, u32[]{:S(2)}) copy-start(f32[1,3072,24]{1,2,0:T(8,128)} %param.26) | copy-start | bytes 884740
  0.7 111.3 %copy-start.2 = (f32[1,24,3072]{2,1,0:T(8,128)S(1)}, f32[1,24,3072]{2,1,0:T(8,128)}, u32[]{:S(2)}) copy-start(f32[1,24,3072]{2,1,0:T(8,128)} %param.29) | copy-start | bytes 884740
  0.7 111.3 %copy-start.3 = (f32[1,24,3072]{2,1,0:T(8,128)S(1)}, f32[1,24,3072]{2,1,0:T(8,128)}, u32[]{:S(2)}) copy-start(f32[1,24,3072]{2,1,0:T(8,128)} %param.30) | copy-start | bytes 884740
  0.7 111.3 %copy-start.4 = (f32[1,3072,24]{1,2,0:T(8,128)S(1)}, f32[1,3072,24]{1,2,0:T(8,128)}, u32[]{:S(2)}) copy-start(f32[1,3072,24]{1,2,0:T(8,128)} %param.31) | copy-start | bytes 884740
  0.7 111.3 %copy-start.5 = (f32[1,3072,24]{1,2,0:T(8,128)S(1)}, f32[1,3072,24]{1,2,0:T(8,128)}, u32[]{:S(2)}) copy-start(f32[1,3072,24]{1,2,0:T(8,128)} %param.32) | copy-start | bytes 884740
  0.7 111.3 %copy-start.6 = (f32[1,5,24]{2,0,1:T(1,128)S(1)}, f32[1,5,24]{2,0,1:T(1,128)}, u32[]{:S(2)}) copy-start(f32[1,5,24]{2,0,1:T(1,128)} %param.28) | copy-start | bytes 1444
  0.7 111.3 %copy-start.7 = (f32[1,5,24]{2,0,1:T(1,128)S(1)}, f32[1,5,24]{2,0,1:T(1,128)}, u32[]{:S(2)}) copy-start(f32[1,5,24]{2,0,1:T(1,128)} %param.35) | copy-start | bytes 1444
  0.7 111.3 %copy-start.8 = (f32[1,5,24]{2,0,1:T(1,128)S(1)}, f32[1,5,24]{2,0,1:T(1,128)}, u32[]{:S(2)}) copy-start(f32[1,5,24]{2,0,1:T(1,128)} %param.36) | copy-start | bytes 1444
  0.7 111.3 %copy-start.9 = (f32[1,96]{1,0:T(1,128)S(1)}, f32[1,96]{1,0:T(1,128)}, u32[]{:S(2)}) copy-start(f32[1,96]{1,0:T(1,128)} %refs_10_.2) | copy-start | bytes 1156
  0.8 111.3 %copy-start.10 = (f32[1,96]{1,0:T(1,128)S(1)}, f32[1,96]{1,0:T(1,128)}, u32[]{:S(2)}) copy-start(f32[1,96]{1,0:T(1,128)} %refs_11_.2) | copy-start | bytes 1156
  0.8 111.3 %copy-start.11 = (f32[1,96]{1,0:T(1,128)S(1)}, f32[1,96]{1,0:T(1,128)}, u32[]{:S(2)}) copy-start(f32[1,96]{1,0:T(1,128)} %refs_12_.2) | copy-start | bytes 1156

commit v6 on v5

--- a/solution.py
+++ b/solution.py
@@ -349,9 +349,10 @@
     tt_b="tt_v",
     un_b="un_v",
 )
+FIRST = ("w1", "w2", "x", "tt_f")
 LATER = ("tt_b", "un_b")
 FORWARD_KINDS = (1, 1, 1, 1, 0, 2)
-BACK_KINDS = (4, 6, 1, 1, 0, 0, 5, 5, 5, 1, 5, 0)
+BACK_KINDS = (0, 7, 7, 0, 1, 1, 1, 1, 5, 0, 5, 5)
 
 
 def layer_kernel(n, names, *refs):
@@ -402,8 +403,8 @@
             getattr(r, name), getattr(r, held), r.load_sem.at[sorted(set(LOADS.values())).index(held)]
         )
         setattr(loads, name, load)
-        if name not in LATER:
-            load.start()
+    for name in FIRST:
+        getattr(loads, name).start()
 
     everyone = [
         ((batch_at + i // n.seq) % n.batch, (seq_at + i % n.seq) % n.seq)
@@ -430,6 +431,10 @@
             other_core,
             seq_at,
         ).start()
+
+    for name in LOADS:
+        if name not in FIRST and name not in LATER:
+            getattr(loads, name).start()
 
     def swapped(m):
         return bytes_of(r.stage.at[m, pl.ds(0, n.rows)], r.swap_send.at[m], r.swap_recv.at[m])
@@ -711,8 +716,8 @@
     tall = 64
     mine, theirs = pl.ds(0, tokens), pl.ds(tokens, tokens)
 
-    def row_loop(body):
-        @pl.loop(0, tokens // tall, unroll=True)
+    def row_loop(body, first=0, last=tokens):
+        @pl.loop(first // tall, last // tall, unroll=True)
         def _(i):
             body(pl.ds(pl.multiple_of(i * tall, tall), tall))
 
@@ -769,8 +774,10 @@
 
     gathered_parts = []
 
-    def swap_ff():
-        return swap(1, r.part_low, r.part_in)
+    halves = [pl.ds(j * tokens // 2, tokens // 2) for j in range(2)]
+
+    def swap_ff(j):
+        return swap(1 + j, r.part_low.at[halves[j]], r.part_in.at[halves[j]])
 
     def drop(q):
         weights_here(n.chunks + q)
@@ -780,7 +787,8 @@
             part = r.total[half, :] + part if len(gathered_parts) > 1 else part
             if len(gathered_parts) == n.chunks and half is theirs:
                 r.part_low[...] = part.astype(BF16)
-                swap_ff().start()
+                for j in range(2):
+                    swap_ff(j).start()
             else:
                 r.total[half, :] = part
 
@@ -802,8 +810,6 @@
     )
     for task, *which in forward_steps:
         task(*which)
-    swap_ff().wait_recv()
-
     def second_norm(at):
         v = (
             r.h[at, :]
@@ -822,14 +828,20 @@
         r.dr2[at, :] = dv
         r.dz[at, :] = dv.astype(BF16)
 
-    row_loop(second_norm)
-    swap_dz = swap(2, r.dz.at[mine], r.dz.at[theirs])
-    swap_dz.start()
-    swap_dz.wait_recv()
-
-    acc, out_low = r.acc, r.give
+    def swap_dz(j):
+        return swap(
+            3 + j,
+            r.dz.at[halves[j]],
+            r.dz.at[pl.ds(tokens + j * tokens // 2, tokens // 2)],
+        )
+
+    for j in range(2):
+        swap_ff(j).wait_recv()
+        row_loop(second_norm, j * tokens // 2, (j + 1) * tokens // 2)
+        swap_dz(j).start()
 
     pieces = grad_pieces(n)
+    acc = r.acc
 
     def wide(c):
         slot, start, width_of = pieces[c]
@@ -839,6 +851,19 @@
     def held(c, at=slice(None), lead=()):
         slot, start, width_of = pieces[c]
         return (slot, *lead, at, pl.ds(start, width_of))
+
+    def product(c, tokens_at):
+        m, q, at = wide(c)
+        left, right = (r.dz, r.act) if m else (r.h_low, r.dpre)
+        return dot(left[tokens_at, :], right[q, tokens_at, at], TN)
+
+    begun = (1, 4, 3)
+    for c in begun:
+        acc[held(c)] = product(c, mine)
+    for j in range(2):
+        swap_dz(j).wait_recv()
+
+    out_low = r.give
 
     def grad_copy(c, at, into, recv, to):
         return remote(out_low.at[held(c, at)], into, r.grad_send, recv, *to)
@@ -997,11 +1022,10 @@
         return value + sum(r.in_sides[held(c, own, lead=(i,))].astype(F32) for i in range(2))
 
     def grad_product(c):
-        m, q, at = wide(c)
-        if m:
-            acc[held(c)] = dot(r.dz[...], r.act[q, :, at], TN)
+        if c in begun:
+            acc[held(c)] = acc[held(c)] + product(c, theirs)
         else:
-            acc[held(c)] = dot(r.h_low[...], r.dpre[q, :, at], TN)
+            acc[held(c)] = product(c, slice(None))
         if back_mode(c) == 3:
             first_start(c)
             return
@@ -1143,7 +1167,7 @@
                 r.total[half, :] = part
 
     def swap_dh():
-        return swap(3, r.part_low2, r.part_in2)
+        return swap(5, r.part_low2, r.part_in2)
 
     def first_norm_back(at):
         dh = r.total[at, :] + r.part_in2[at, :].astype(F32) + r.dr2[at, :]
@@ -1252,25 +1276,25 @@
         r.dx[...] = r.dx[...] + r.mixed[...]
 
     for task, *which in (
-        (grad_product, 4), (grad_product, 2), (grad_product, 1), (slope_back, 2),
-        (grad_product, 11), (grad_product, 3), (slope_back, 1), (slope_back, 0), (grad_side, 1),
-        (grad_side, 2), (grad_product, 6), (norm_back,), (grad_side, 3), (grad_product, 7),
-        (grad_line, 2), (grad_side, 4), (grad_side, 6), (outputs,), (grad_product, 10),
-        (grad_side, 7), (grad_product, 5), (grad_line, 3), (grad_line, 1), (grad_across, 2),
-        (grad_line, 6), (grad_product, 9), (grad_line, 4), (grad_across, 3), (grad_line, 7),
-        (grad_side, 11), (grad_side, 10), (grad_across, 6), (grad_across, 7), (grad_out, 6),
-        (turn_back,), (grad_out, 3), (grad_across, 4), (grad_side, 5), (grad_product, 8),
-        (grad_side, 9), (grad_out, 7), (grad_far, 7), (grad_product, 0), (grad_out, 2),
-        (grad_far, 2), (grad_line, 11), (grad_line, 5), (small_grads,), (grad_across, 11),
-        (grad_line, 9), (grad_far, 6), (grad_side, 8), (grad_line, 10), (grad_across, 5),
-        (grad_across, 10), (grad_side, 0), (grad_out, 11), (grad_out, 10), (grad_end, 2),
-        (grad_far, 10), (small_rows_back,), (grad_across, 9), (grad_across, 1), (grad_out, 4),
-        (grad_line, 8), (grad_across, 8), (grad_end, 10), (grad_out, 5), (small_end,),
-        (grad_end, 7), (grad_line, 0), (grad_out, 8), (grad_out, 1), (grad_out, 9),
-        (grad_far, 11), (grad_far, 4), (grad_far, 8), (grad_far, 3), (grad_far, 1),
-        (grad_far, 5), (grad_across, 0), (grad_end, 1), (grad_end, 4), (grad_far, 9),
-        (grad_end, 6), (grad_end, 8), (grad_out, 0), (grad_end, 5), (grad_far, 0),
-        (grad_end, 3), (mix_back,), (grad_end, 11), (grad_end, 9), (grad_end, 0),
+        (grad_product, 1), (grad_product, 4), (grad_product, 3), (slope_back, 2),
+        (slope_back, 1), (slope_back, 0), (grad_side, 3), (grad_side, 1), (grad_product, 2),
+        (grad_product, 5), (grad_side, 4), (grad_product, 9), (norm_back,), (grad_line, 3),
+        (grad_product, 6), (small_grads,), (grad_line, 4), (grad_side, 9), (grad_side, 5),
+        (grad_product, 0), (grad_side, 2), (grad_line, 1), (grad_product, 11), (outputs,),
+        (grad_product, 7), (grad_side, 6), (grad_line, 9), (small_rows_back,), (grad_across, 3),
+        (grad_line, 5), (grad_across, 4), (turn_back,), (grad_side, 0), (grad_product, 8),
+        (grad_line, 2), (grad_product, 10), (grad_across, 9), (grad_side, 7), (grad_out, 4),
+        (grad_line, 6), (grad_out, 3), (grad_far, 3), (grad_across, 5), (grad_side, 11),
+        (grad_across, 6), (grad_line, 0), (grad_across, 2), (grad_across, 1), (grad_side, 8),
+        (grad_far, 4), (grad_line, 7), (grad_end, 3), (grad_across, 0), (grad_line, 11),
+        (grad_out, 9), (grad_side, 10), (grad_across, 7), (grad_across, 11), (grad_out, 11),
+        (grad_out, 6), (grad_line, 8), (grad_across, 8), (grad_out, 5), (grad_far, 6),
+        (grad_far, 9), (grad_far, 5), (grad_out, 8), (grad_far, 8), (grad_end, 4),
+        (grad_end, 9), (grad_out, 0), (small_end,), (grad_out, 2), (grad_out, 1), (mix_back,),
+        (grad_line, 10), (grad_far, 11), (grad_far, 0), (grad_across, 10), (grad_out, 7),
+        (grad_end, 11), (grad_end, 5), (grad_end, 8), (grad_far, 1), (grad_out, 10),
+        (grad_end, 1), (grad_end, 6), (grad_far, 7), (grad_far, 2), (grad_far, 10),
+        (grad_end, 2), (grad_end, 7), (grad_end, 0), (grad_end, 10),
     ):
         task(*which)
 
@@ -1381,7 +1405,7 @@
         h=vmem((tokens, width), F32),
         h_low=vmem((2 * tokens, width), BF16),
         core_send=dma,
-        core_recv=dma((4,)),
+        core_recv=dma((6,)),
         total=vmem((2 * tokens, width), F32),
         act=vmem((q, 2 * tokens, cols), BF16),
         lift=vmem((2 * tokens, cols), F32),

time: 115 us -> 114 us (level)
  no operation moved by 1% of the time
where the time goes in v6:
time: 114 us
  Pallas kernels  113 us (99%)
    pallas_call x1, Pallas kernels, run_layer(): pl.pallas_call(functools.partial(layer_kernel, n, names), out_shape=[vmem...  111 us
    pallas_call x1, Pallas kernels, run_adam(): pl.pallas_call(functools.partial(adam_kernel, n, names), out_shape=list(o...  2.3 us

profile of v6, /device:TPU:0, one launch (start us, length us, event | category | flops | bytes accessed | tf_op | source)
XLA Modules:
  0.0 113.9 jit_solution(1224349424979969741)
XLA Ops:
  0.7 0.0 copy-start
  0.7 0.0 copy-start.1
  0.7 0.0 copy-start.2
  0.7 0.0 copy-start.3
  0.7 0.0 copy-start.4
  0.7 0.0 copy-start.5
  0.7 0.0 copy-start.6
  0.7 0.0 copy-start.7
  0.7 0.0 copy-start.8
  0.7 0.0 copy-start.9
  0.8 110.5 %fused_layer.1 = (bf16[256,768]{1,0:T(8,128)(2,1)S(1)}, f32[256,768]{1,0:T(8,128)S(1)}, f32[24,3072]{1,0:T(8,128)S(1)}, f32[24,3072]{1,0:T(8,128)S(1)}, f32[8,128]{1,0:T(8,128)S(1)}, /*index=5*/f32[8,128]{1,0:T(8,128)S(1)}) custom-call(f32[1,96]{1,0:T(1,128)} %refs_10_.2, f32[5,1,24]{2,1,0:T(1,128)} %bitcast.43, bf16[256,768]{1,0:T(8,128)(2,1)} %bitcast.47, ...), custom_call_target="tpu_custom_call" | custom-call | tf_op jit(solution)/shard_map/fused_layer/pallas_call | solution.py:1466
  111.3 0.0 copy-done
  111.3 0.0 copy-done.1
  111.3 0.0 copy-done.2
  111.3 0.0 copy-done.3
  111.3 0.0 copy-done.4
  111.4 0.0 copy-done.5
  111.4 0.0 copy-done.6
  111.4 0.0 copy-done.7
  111.4 0.0 copy-done.8
  111.4 0.0 copy-done.9
  111.4 0.0 copy-done.10
  111.4 0.0 copy-done.11
  111.4 2.3 %adam.1 = (f32[1,1]{1,0:T(1,128)}, f32[24,3072]{1,0:T(8,128)}, f32[24,3072]{1,0:T(8,128)}, f32[24,3072]{1,0:T(8,128)}, f32[24,3072]{1,0:T(8,128)}, /*index=5*/f3...) custom-call(f32[24,3072]{1,0:T(8,128)S(1)} %get-tuple-element.36.ref, ...), custom_call_target="tpu_custom_call" | custom-call | tf_op jit(solution)/shard_map/adam/pallas_call | solution.py:1532
  (2 shorter events, 0.0 us)
Async XLA Ops:
  0.7 110.7 %copy-start = (f32[1,24,3072]{2,1,0:T(8,128)S(1)}, f32[1,24,3072]{2,1,0:T(8,128)}, u32[]{:S(2)}) copy-start(f32[1,24,3072]{2,1,0:T(8,128)} %param.25) | copy-start | bytes 884740
  0.7 110.7 %copy-start.1 = (f32[1,3072,24]{1,2,0:T(8,128)S(1)}, f32[1,3072,24]{1,2,0:T(8,128)}, u32[]{:S(2)}) copy-start(f32[1,3072,24]{1,2,0:T(8,128)} %param.26) | copy-start | bytes 884740
  0.7 110.7 %copy-start.2 = (f32[1,24,3072]{2,1,0:T(8,128)S(1)}, f32[1,24,3072]{2,1,0:T(8,128)}, u32[]{:S(2)}) copy-start(f32[1,24,3072]{2,1,0:T(8,128)} %param.29) | copy-start | bytes 884740
  0.7 110.7 %copy-start.3 = (f32[1,24,3072]{2,1,0:T(8,128)S(1)}, f32[1,24,3072]{2,1,0:T(8,128)}, u32[]{:S(2)}) copy-start(f32[1,24,3072]{2,1,0:T(8,128)} %param.30) | copy-start | bytes 884740
  0.7 110.7 %copy-start.4 = (f32[1,3072,24]{1,2,0:T(8,128)S(1)}, f32[1,3072,24]{1,2,0:T(8,128)}, u32[]{:S(2)}) copy-start(f32[1,3072,24]{1,2,0:T(8,128)} %param.31) | copy-start | bytes 884740
  0.7 110.7 %copy-start.5 = (f32[1,3072,24]{1,2,0:T(8,128)S(1)}, f32[1,3072,24]{1,2,0:T(8,128)}, u32[]{:S(2)}) copy-start(f32[1,3072,24]{1,2,0:T(8,128)} %param.32) | copy-start | bytes 884740
  0.7 110.7 %copy-start.6 = (f32[1,5,24]{2,0,1:T(1,128)S(1)}, f32[1,5,24]{2,0,1:T(1,128)}, u32[]{:S(2)}) copy-start(f32[1,5,24]{2,0,1:T(1,128)} %param.28) | copy-start | bytes 1444
  0.7 110.7 %copy-start.7 = (f32[1,5,24]{2,0,1:T(1,128)S(1)}, f32[1,5,24]{2,0,1:T(1,128)}, u32[]{:S(2)}) copy-start(f32[1,5,24]{2,0,1:T(1,128)} %param.35) | copy-start | bytes 1444
  0.7 110.7 %copy-start.8 = (f32[1,5,24]{2,0,1:T(1,128)S(1)}, f32[1,5,24]{2,0,1:T(1,128)}, u32[]{:S(2)}) copy-start(f32[1,5,24]{2,0,1:T(1,128)} %param.36) | copy-start | bytes 1444
  0.7 110.7 %copy-start.9 = (f32[1,96]{1,0:T(1,128)S(1)}, f32[1,96]{1,0:T(1,128)}, u32[]{:S(2)}) copy-start(f32[1,96]{1,0:T(1,128)} %refs_10_.2) | copy-start | bytes 1156
  0.8 110.7 %copy-start.10 = (f32[1,96]{1,0:T(1,128)S(1)}, f32[1,96]{1,0:T(1,128)}, u32[]{:S(2)}) copy-start(f32[1,96]{1,0:T(1,128)} %refs_11_.2) | copy-start | bytes 1156
  0.8 110.7 %copy-start.11 = (f32[1,96]{1,0:T(1,128)S(1)}, f32[1,96]{1,0:T(1,128)}, u32[]{:S(2)}) copy-start(f32[1,96]{1,0:T(1,128)} %refs_12_.2) | copy-start | bytes 1156

commit v7 on v6

--- a/solution.py
+++ b/solution.py
@@ -349,10 +349,10 @@
     tt_b="tt_v",
     un_b="un_v",
 )
-FIRST = ("w1", "w2", "x", "tt_f")
+FIRST = ("w1", "w2")
 LATER = ("tt_b", "un_b")
 FORWARD_KINDS = (1, 1, 1, 1, 0, 2)
-BACK_KINDS = (0, 7, 7, 0, 1, 1, 1, 1, 5, 0, 5, 5)
+BACK_KINDS = (3, 6, 5, 0, 0, 4, 5, 1, 0, 1, 1, 5)
 
 
 def layer_kernel(n, names, *refs):
@@ -411,9 +411,13 @@
         for i in range(1, n.devices)
     ]
     barrier = pltpu.get_barrier_semaphore()
-    for device in everyone:
+    partners = [(across(k), seq_at) for k in range(1, n.batch)]
+    partners += [(batch_at, plane(k)) for k in range(n.seq - 1, 0, -1)]
+    for device in partners:
         pl.semaphore_signal(barrier, inc=1, device_id=device, device_id_type=MESH)
-    pl.semaphore_wait(barrier, n.devices - 1)
+    loads.x.start()
+    loads.tt_f.start()
+    pl.semaphore_wait(barrier, len(partners))
 
     loads.w1.wait()
     loads.w2.wait()
@@ -433,7 +437,7 @@
         ).start()
 
     for name in LOADS:
-        if name not in FIRST and name not in LATER:
+        if name not in FIRST + LATER + ("x", "tt_f"):
             getattr(loads, name).start()
 
     def swapped(m):
@@ -857,7 +861,7 @@
         left, right = (r.dz, r.act) if m else (r.h_low, r.dpre)
         return dot(left[tokens_at, :], right[q, tokens_at, at], TN)
 
-    begun = (1, 4, 3)
+    begun = (0, 1, 3)
     for c in begun:
         acc[held(c)] = product(c, mine)
     for j in range(2):
@@ -1276,25 +1280,25 @@
         r.dx[...] = r.dx[...] + r.mixed[...]
 
     for task, *which in (
-        (grad_product, 1), (grad_product, 4), (grad_product, 3), (slope_back, 2),
-        (slope_back, 1), (slope_back, 0), (grad_side, 3), (grad_side, 1), (grad_product, 2),
-        (grad_product, 5), (grad_side, 4), (grad_product, 9), (norm_back,), (grad_line, 3),
-        (grad_product, 6), (small_grads,), (grad_line, 4), (grad_side, 9), (grad_side, 5),
-        (grad_product, 0), (grad_side, 2), (grad_line, 1), (grad_product, 11), (outputs,),
-        (grad_product, 7), (grad_side, 6), (grad_line, 9), (small_rows_back,), (grad_across, 3),
-        (grad_line, 5), (grad_across, 4), (turn_back,), (grad_side, 0), (grad_product, 8),
-        (grad_line, 2), (grad_product, 10), (grad_across, 9), (grad_side, 7), (grad_out, 4),
-        (grad_line, 6), (grad_out, 3), (grad_far, 3), (grad_across, 5), (grad_side, 11),
-        (grad_across, 6), (grad_line, 0), (grad_across, 2), (grad_across, 1), (grad_side, 8),
-        (grad_far, 4), (grad_line, 7), (grad_end, 3), (grad_across, 0), (grad_line, 11),
-        (grad_out, 9), (grad_side, 10), (grad_across, 7), (grad_across, 11), (grad_out, 11),
-        (grad_out, 6), (grad_line, 8), (grad_across, 8), (grad_out, 5), (grad_far, 6),
-        (grad_far, 9), (grad_far, 5), (grad_out, 8), (grad_far, 8), (grad_end, 4),
-        (grad_end, 9), (grad_out, 0), (small_end,), (grad_out, 2), (grad_out, 1), (mix_back,),
-        (grad_line, 10), (grad_far, 11), (grad_far, 0), (grad_across, 10), (grad_out, 7),
-        (grad_end, 11), (grad_end, 5), (grad_end, 8), (grad_far, 1), (grad_out, 10),
-        (grad_end, 1), (grad_end, 6), (grad_far, 7), (grad_far, 2), (grad_far, 10),
-        (grad_end, 2), (grad_end, 7), (grad_end, 0), (grad_end, 10),
+        (grad_product, 0), (grad_product, 1), (grad_product, 3), (grad_product, 2),
+        (slope_back, 1), (grad_product, 4), (slope_back, 0), (slope_back, 2), (grad_side, 1),
+        (grad_product, 10), (grad_side, 0), (grad_line, 0), (grad_side, 2), (norm_back,),
+        (grad_side, 3), (grad_across, 0), (grad_side, 10), (grad_product, 8), (grad_side, 4),
+        (grad_product, 9), (grad_product, 5), (grad_line, 3), (outputs,), (small_grads,),
+        (grad_line, 1), (grad_line, 4), (grad_across, 3), (grad_product, 7), (grad_side, 9),
+        (grad_across, 4), (grad_line, 2), (grad_line, 10), (turn_back,), (grad_across, 2),
+        (grad_side, 8), (grad_out, 2), (grad_across, 10), (grad_product, 11), (grad_side, 7),
+        (grad_out, 3), (grad_side, 5), (grad_far, 3), (grad_product, 6), (grad_far, 2),
+        (grad_line, 8), (small_rows_back,), (grad_line, 9), (grad_across, 1), (grad_out, 4),
+        (grad_side, 11), (grad_across, 8), (grad_out, 0), (grad_across, 9), (grad_line, 7),
+        (grad_line, 5), (mix_back,), (grad_end, 3), (small_end,), (grad_out, 10),
+        (grad_side, 6), (grad_far, 10), (grad_out, 1), (grad_across, 7), (grad_across, 5),
+        (grad_end, 10), (grad_out, 8), (grad_out, 9), (grad_line, 11), (grad_far, 1),
+        (grad_out, 5), (grad_across, 11), (grad_out, 11), (grad_far, 5), (grad_far, 9),
+        (grad_far, 0), (grad_far, 8), (grad_line, 6), (grad_across, 6), (grad_end, 2),
+        (grad_end, 8), (grad_far, 4), (grad_end, 5), (grad_out, 6), (grad_out, 7),
+        (grad_far, 11), (grad_far, 7), (grad_far, 6), (grad_end, 0), (grad_end, 9),
+        (grad_end, 11), (grad_end, 1), (grad_end, 7), (grad_end, 4), (grad_end, 6),
     ):
         task(*which)
 

time: 114 us -> 113 us (level)
  no operation moved by 1% of the time
where the time goes in v7:
time: 113 us
  Pallas kernels  112 us (99%)
    pallas_call x1, Pallas kernels, run_layer(): pl.pallas_call(functools.partial(layer_kernel, n, names), out_shape=[vmem...  109 us
    pallas_call x1, Pallas kernels, run_adam(): pl.pallas_call(functools.partial(adam_kernel, n, names), out_shape=list(o...  2.3 us

profile of v7, /device:TPU:0, one launch (start us, length us, event | category | flops | bytes accessed | tf_op | source)
XLA Modules:
  0.0 112.8 jit_solution(13148190941737474098)
XLA Ops:
  0.7 0.0 copy-start
  0.7 0.0 copy-start.1
  0.7 0.0 copy-start.2
  0.7 0.0 copy-start.3
  0.7 0.0 copy-start.4
  0.7 0.0 copy-start.5
  0.7 0.0 copy-start.6
  0.7 0.0 copy-start.7
  0.7 0.0 copy-start.8
  0.7 0.0 copy-start.9
  0.8 0.0 copy-start.10
  0.8 0.0 copy-start.11
  0.8 109.5 %fused_layer.1 = (bf16[256,768]{1,0:T(8,128)(2,1)S(1)}, f32[256,768]{1,0:T(8,128)S(1)}, f32[24,3072]{1,0:T(8,128)S(1)}, f32[24,3072]{1,0:T(8,128)S(1)}, f32[8,128]{1,0:T(8,128)S(1)}, /*index=5*/f32[8,128]{1,0:T(8,128)S(1)}) custom-call(f32[1,96]{1,0:T(1,128)} %refs_10_.2, f32[5,1,24]{2,1,0:T(1,128)} %bitcast.43, bf16[256,768]{1,0:T(8,128)(2,1)} %bitcast.47, ...), custom_call_target="tpu_custom_call" | custom-call | tf_op jit(solution)/shard_map/fused_layer/pallas_call | solution.py:1470
  110.2 0.0 copy-done
  110.3 0.0 copy-done.1
  110.3 0.0 copy-done.2
  110.3 0.0 copy-done.3
  110.3 0.0 copy-done.4
  110.3 0.0 copy-done.5
  110.3 0.0 copy-done.6
  110.3 0.0 copy-done.7
  110.3 0.0 copy-done.8
  110.3 0.0 copy-done.9
  110.4 2.3 %adam.1 = (f32[1,1]{1,0:T(1,128)}, f32[24,3072]{1,0:T(8,128)}, f32[24,3072]{1,0:T(8,128)}, f32[24,3072]{1,0:T(8,128)}, f32[24,3072]{1,0:T(8,128)}, /*index=5*/f3...) custom-call(f32[24,3072]{1,0:T(8,128)S(1)} %get-tuple-element.36.ref, ...), custom_call_target="tpu_custom_call" | custom-call | tf_op jit(solution)/shard_map/adam/pallas_call | solution.py:1536
  (2 shorter events, 0.0 us)
Async XLA Ops:
  0.7 109.6 %copy-start = (f32[1,24,3072]{2,1,0:T(8,128)S(1)}, f32[1,24,3072]{2,1,0:T(8,128)}, u32[]{:S(2)}) copy-start(f32[1,24,3072]{2,1,0:T(8,128)} %param.25) | copy-start | bytes 884740
  0.7 109.6 %copy-start.1 = (f32[1,3072,24]{1,2,0:T(8,128)S(1)}, f32[1,3072,24]{1,2,0:T(8,128)}, u32[]{:S(2)}) copy-start(f32[1,3072,24]{1,2,0:T(8,128)} %param.26) | copy-start | bytes 884740
  0.7 109.6 %copy-start.2 = (f32[1,24,3072]{2,1,0:T(8,128)S(1)}, f32[1,24,3072]{2,1,0:T(8,128)}, u32[]{:S(2)}) copy-start(f32[1,24,3072]{2,1,0:T(8,128)} %param.29) | copy-start | bytes 884740
  0.7 109.6 %copy-start.3 = (f32[1,24,3072]{2,1,0:T(8,128)S(1)}, f32[1,24,3072]{2,1,0:T(8,128)}, u32[]{:S(2)}) copy-start(f32[1,24,3072]{2,1,0:T(8,128)} %param.30) | copy-start | bytes 884740
  0.7 109.6 %copy-start.4 = (f32[1,3072,24]{1,2,0:T(8,128)S(1)}, f32[1,3072,24]{1,2,0:T(8,128)}, u32[]{:S(2)}) copy-start(f32[1,3072,24]{1,2,0:T(8,128)} %param.31) | copy-start | bytes 884740
  0.7 109.6 %copy-start.5 = (f32[1,3072,24]{1,2,0:T(8,128)S(1)}, f32[1,3072,24]{1,2,0:T(8,128)}, u32[]{:S(2)}) copy-start(f32[1,3072,24]{1,2,0:T(8,128)} %param.32) | copy-start | bytes 884740
  0.7 109.6 %copy-start.6 = (f32[1,5,24]{2,0,1:T(1,128)S(1)}, f32[1,5,24]{2,0,1:T(1,128)}, u32[]{:S(2)}) copy-start(f32[1,5,24]{2,0,1:T(1,128)} %param.28) | copy-start | bytes 1444
  0.7 109.6 %copy-start.7 = (f32[1,5,24]{2,0,1:T(1,128)S(1)}, f32[1,5,24]{2,0,1:T(1,128)}, u32[]{:S(2)}) copy-start(f32[1,5,24]{2,0,1:T(1,128)} %param.35) | copy-start | bytes 1444
  0.7 109.6 %copy-start.8 = (f32[1,5,24]{2,0,1:T(1,128)S(1)}, f32[1,5,24]{2,0,1:T(1,128)}, u32[]{:S(2)}) copy-start(f32[1,5,24]{2,0,1:T(1,128)} %param.36) | copy-start | bytes 1444
  0.7 109.6 %copy-start.9 = (f32[1,96]{1,0:T(1,128)S(1)}, f32[1,96]{1,0:T(1,128)}, u32[]{:S(2)}) copy-start(f32[1,96]{1,0:T(1,128)} %refs_10_.2) | copy-start | bytes 1156
  0.8 109.6 %copy-start.10 = (f32[1,96]{1,0:T(1,128)S(1)}, f32[1,96]{1,0:T(1,128)}, u32[]{:S(2)}) copy-start(f32[1,96]{1,0:T(1,128)} %refs_11_.2) | copy-start | bytes 1156
  0.8 109.6 %copy-start.11 = (f32[1,96]{1,0:T(1,128)S(1)}, f32[1,96]{1,0:T(1,128)}, u32[]{:S(2)}) copy-start(f32[1,96]{1,0:T(1,128)} %refs_12_.2) | copy-start | bytes 1156

commit v8 on v7

--- a/solution.py
+++ b/solution.py
@@ -448,9 +448,12 @@
         y_ref[...] = dot(table[...], source, NT).astype(BF16)
         l_ref[seq_at] = y_ref[rows_of(seq_at, n.packed), :]
 
+    half_way = n.seq // 2
+    mix_order = [*range(half_way, n.seq), *range(2, half_way), 1]
+
     def mix_send(t):
         y_ref, l_ref = r.y_buf.at[t], r.l_buf.at[t]
-        for k in range(1, n.seq):
+        for k in mix_order:
             remote(
                 y_ref.at[rows_of(plane(k), n.packed)],
                 l_ref.at[seq_at],
@@ -487,7 +490,7 @@
             value = (jnp.where(first, by_cos, by_sin) * scale).astype(BF16)
             z_ref[e] = value[:, : n.block]
             z_ref[e + 1] = value[:, n.block :]
-        for k in range(1, n.seq):
+        for k in mix_order:
             remote(
                 z_ref.at[plane(k)],
                 r_ref.at[seq_at],
@@ -717,7 +720,7 @@
         mix_turn(0)
 
     step = 32
-    tall = 64
+    tall = 128
     mine, theirs = pl.ds(0, tokens), pl.ds(tokens, tokens)
 
     def row_loop(body, first=0, last=tokens):
@@ -1306,7 +1309,7 @@
     r.norm_own[...] = jnp.sum(squares, axis=0, keepdims=True)
     r.norm_all[batch_at * n.seq + seq_at] = r.norm_own[...]
 
-    for device in everyone:
+    for device in reversed(everyone):
         remote(
             r.norm_own,
             r.norm_all.at[batch_at * n.seq + seq_at],

time: 113 us -> 113 us (level)
  no operation moved by 1% of the time
where the time goes in v8:
time: 113 us
  Pallas kernels  112 us (99%)
    pallas_call x1, Pallas kernels, run_layer(): pl.pallas_call(functools.partial(layer_kernel, n, names), out_shape=[vmem...  109 us
    pallas_call x1, Pallas kernels, run_adam(): pl.pallas_call(functools.partial(adam_kernel, n, names), out_shape=list(o...  2.3 us

profile of v8, /device:TPU:0, one launch (start us, length us, event | category | flops | bytes accessed | tf_op | source)
XLA Modules:
  0.0 112.7 jit_solution(10614092601381807120)
XLA Ops:
  0.7 0.0 copy-start
  0.7 0.0 copy-start.1
  0.7 0.0 copy-start.2
  0.7 0.0 copy-start.3
  0.7 0.0 copy-start.4
  0.7 0.0 copy-start.5
  0.7 0.0 copy-start.6
  0.7 0.0 copy-start.7
  0.7 0.0 copy-start.8
  0.7 0.0 copy-start.9
  0.8 0.0 copy-start.10
  0.8 0.0 copy-start.11
  0.8 109.4 %fused_layer.1 = (bf16[256,768]{1,0:T(8,128)(2,1)S(1)}, f32[256,768]{1,0:T(8,128)S(1)}, f32[24,3072]{1,0:T(8,128)S(1)}, f32[24,3072]{1,0:T(8,128)S(1)}, f32[8,128]{1,0:T(8,128)S(1)}, /*index=5*/f32[8,128]{1,0:T(8,128)S(1)}) custom-call(f32[1,96]{1,0:T(1,128)} %refs_10_.2, f32[5,1,24]{2,1,0:T(1,128)} %bitcast.43, bf16[256,768]{1,0:T(8,128)(2,1)} %bitcast.47, ...), custom_call_target="tpu_custom_call" | custom-call | tf_op jit(solution)/shard_map/fused_layer/pallas_call | solution.py:1473
  110.1 0.0 copy-done
  110.2 0.0 copy-done.1
  110.2 0.0 copy-done.2
  110.2 0.0 copy-done.3
  110.2 0.0 copy-done.4
  110.2 0.0 copy-done.5
  110.2 0.0 copy-done.6
  110.2 0.0 copy-done.7
  110.2 0.0 copy-done.8
  110.2 0.0 copy-done.9
  110.3 2.3 %adam.1 = (f32[1,1]{1,0:T(1,128)}, f32[24,3072]{1,0:T(8,128)}, f32[24,3072]{1,0:T(8,128)}, f32[24,3072]{1,0:T(8,128)}, f32[24,3072]{1,0:T(8,128)}, /*index=5*/f3...) custom-call(f32[24,3072]{1,0:T(8,128)S(1)} %get-tuple-element.36.ref, ...), custom_call_target="tpu_custom_call" | custom-call | tf_op jit(solution)/shard_map/adam/pallas_call | solution.py:1539
  (2 shorter events, 0.0 us)
Async XLA Ops:
  0.7 109.5 %copy-start = (f32[1,24,3072]{2,1,0:T(8,128)S(1)}, f32[1,24,3072]{2,1,0:T(8,128)}, u32[]{:S(2)}) copy-start(f32[1,24,3072]{2,1,0:T(8,128)} %param.25) | copy-start | bytes 884740
  0.7 109.5 %copy-start.1 = (f32[1,3072,24]{1,2,0:T(8,128)S(1)}, f32[1,3072,24]{1,2,0:T(8,128)}, u32[]{:S(2)}) copy-start(f32[1,3072,24]{1,2,0:T(8,128)} %param.26) | copy-start | bytes 884740
  0.7 109.5 %copy-start.2 = (f32[1,24,3072]{2,1,0:T(8,128)S(1)}, f32[1,24,3072]{2,1,0:T(8,128)}, u32[]{:S(2)}) copy-start(f32[1,24,3072]{2,1,0:T(8,128)} %param.29) | copy-start | bytes 884740
  0.7 109.5 %copy-start.3 = (f32[1,24,3072]{2,1,0:T(8,128)S(1)}, f32[1,24,3072]{2,1,0:T(8,128)}, u32[]{:S(2)}) copy-start(f32[1,24,3072]{2,1,0:T(8,128)} %param.30) | copy-start | bytes 884740
  0.7 109.5 %copy-start.4 = (f32[1,3072,24]{1,2,0:T(8,128)S(1)}, f32[1,3072,24]{1,2,0:T(8,128)}, u32[]{:S(2)}) copy-start(f32[1,3072,24]{1,2,0:T(8,128)} %param.31) | copy-start | bytes 884740
  0.7 109.5 %copy-start.5 = (f32[1,3072,24]{1,2,0:T(8,128)S(1)}, f32[1,3072,24]{1,2,0:T(8,128)}, u32[]{:S(2)}) copy-start(f32[1,3072,24]{1,2,0:T(8,128)} %param.32) | copy-start | bytes 884740
  0.7 109.5 %copy-start.6 = (f32[1,5,24]{2,0,1:T(1,128)S(1)}, f32[1,5,24]{2,0,1:T(1,128)}, u32[]{:S(2)}) copy-start(f32[1,5,24]{2,0,1:T(1,128)} %param.28) | copy-start | bytes 1444
  0.7 109.5 %copy-start.7 = (f32[1,5,24]{2,0,1:T(1,128)S(1)}, f32[1,5,24]{2,0,1:T(1,128)}, u32[]{:S(2)}) copy-start(f32[1,5,24]{2,0,1:T(1,128)} %param.35) | copy-start | bytes 1444
  0.7 109.5 %copy-start.8 = (f32[1,5,24]{2,0,1:T(1,128)S(1)}, f32[1,5,24]{2,0,1:T(1,128)}, u32[]{:S(2)}) copy-start(f32[1,5,24]{2,0,1:T(1,128)} %param.36) | copy-start | bytes 1444
  0.7 109.5 %copy-start.9 = (f32[1,96]{1,0:T(1,128)S(1)}, f32[1,96]{1,0:T(1,128)}, u32[]{:S(2)}) copy-start(f32[1,96]{1,0:T(1,128)} %refs_10_.2) | copy-start | bytes 1156
  0.8 109.5 %copy-start.10 = (f32[1,96]{1,0:T(1,128)S(1)}, f32[1,96]{1,0:T(1,128)}, u32[]{:S(2)}) copy-start(f32[1,96]{1,0:T(1,128)} %refs_11_.2) | copy-start | bytes 1156
  0.8 109.5 %copy-start.11 = (f32[1,96]{1,0:T(1,128)S(1)}, f32[1,96]{1,0:T(1,128)}, u32[]{:S(2)}) copy-start(f32[1,96]{1,0:T(1,128)} %refs_12_.2) | copy-start | bytes 1156
